TPU v7x, 32 devices: a whole 2x2x4 slice. The times are simulated.
32 devices in a mesh: grp: 2 (over y), row: 4 (over x, core), col: 4 (over z).
Axes of the slice: x: 2, y: 2, z: 4, core: 2. Of those that a mesh axis runs over, the one named last changes fastest.
Arguments:
- video: bfloat16 [514, 32, 512], P('grp', 'row', 'col'), parts along dimension 0, may hold values from -6 to 6, as said below
- filters: float32 [4, 2, 7, 7], replicated, may hold values from -0.875 to 0.875
- start_basis: float32 [256, 64], replicated, may hold values from -6 to 6
Outputs:
- basis: float32 [512, 64], P('grp'), parts along dimension 0
- modes: float32 [16, 128, 256], P(('grp', 'row'), 'col'), parts along dimension 0
There are 2 independent parts, one for each index of `grp`. A program takes and returns all parts, laid end to end along the dimension named above; an argument that names none is the same for every part. Nothing has to cross between parts.
Inputs may be any that keep to these rules, and one draw needn't show every extreme that they name: `video`: grey levels: a fixed texture plus a per-pixel oscillation in time.
All inputs are finite; a program needn't handle non-finite values.
Results may differ from a plain program's by a relative error of at most 0.0034.
Values may be sent and summed in bfloat16 or wider, within the bound.
No kernel may reach another device: no remote copies, remote signals or barrier semaphores. Data moves between devices by JAX's collectives and lax.ppermute only.
A program may use at most 64 MiB of HBM per device.

v0:
```python
import jax
import jax.numpy as jnp
from jax import lax
from jax.sharding import PartitionSpec as P

FRAMES = 256
MODES = 64
ORIENT = 4
TAPS = 7
SWEEPS = 2


def padded_2(array, sides, width):
    for axis, dim in sides:
        size, length = (lax.axis_size(axis), array.shape[dim])
        up = [(i, (i + 1) % size) for i in range(size - 1)]
        down = [(j, i) for i, j in up]
        last = lax.slice_in_dim(array, length - width, length, axis=dim)
        first = lax.slice_in_dim(array, 0, width, axis=dim)
        before = lax.ppermute(last, axis, up)
        after = lax.ppermute(first, axis, down)
        array = jnp.concatenate([before, array, after], axis=dim)
    return array


def orthonormal(stacked):
    inner = jnp.dot(stacked.T, stacked, precision=lax.Precision.HIGHEST)
    factor = jnp.linalg.cholesky(inner)
    return lax.linalg.triangular_solve(
        factor, stacked, left_side=False, lower=True, transpose_a=True
    )


def on_device(video, filters, start_basis):
    tile_rows = video.shape[1]
    tile_cols = video.shape[2]
    padded = padded_2(video, (("row", 1), ("col", 2)), 3)

    def orient(taps):
        kernels = taps.reshape(2, 1, TAPS, TAPS)
        lifted = padded.astype(jnp.float32)[:, None]
        response = lax.conv_general_dilated(
            lifted, kernels, (1, 1), "VALID", precision=lax.Precision.HIGHEST
        )
        real_part = response[:, 0]
        imag_part = response[:, 1]
        prod_real = real_part[1:] * real_part[:-1] + imag_part[1:] * imag_part[:-1]
        prod_imag = imag_part[1:] * real_part[:-1] - real_part[1:] * imag_part[:-1]
        motion = prod_imag / jnp.sqrt(prod_real * prod_real + prod_imag * prod_imag + 1.0)
        pooled = motion.reshape(FRAMES, tile_rows // 4, 4, tile_cols // 4, 4).mean(axis=(2, 4))
        return pooled.astype(jnp.bfloat16)

    stacked = lax.map(orient, filters)
    flat = jnp.transpose(stacked, (1, 0, 2, 3)).reshape(FRAMES, -1)
    devices_all = lax.axis_size("row") * lax.axis_size("col")
    npix_all = flat.shape[1] * devices_all
    basis_now = start_basis
    local_gram = jnp.dot(flat, flat.T, preferred_element_type=jnp.float32)
    gram = lax.psum(local_gram, ("row", "col")) / npix_all
    for sweep in range(SWEEPS):
        basis_now = orthonormal(jnp.dot(gram, basis_now, precision=lax.Precision.HIGHEST))
    projected = jnp.dot(basis_now.astype(jnp.bfloat16).T, flat, preferred_element_type=jnp.float32)
    fields = projected.reshape(MODES, ORIENT, tile_rows // 4, tile_cols // 4)
    modes = jnp.transpose(fields, (2, 3, 1, 0)).reshape(
        tile_rows // 4, tile_cols // 4, ORIENT * MODES
    )
    return (basis_now, modes)


def solution(mesh):
    return jax.shard_map(
        on_device,
        mesh=mesh,
        in_specs=(P("grp", "row", "col"), P(), P()),
        out_specs=(P("grp", None), P(("grp", "row"), "col", None)),
        check_vma=False,
    )
```

profile of v0, /device:TPU:0, one launch (start us, length us, event | category | flops | bytes accessed | tf_op | source)
XLA Modules:
  0.0 571.3 jit_solution(12141925055525839283)
XLA Ops:
  7.2 1.5 copy.25
  8.8 2.4 collective-permute-start
  11.1 1.3 collective-permute-start.1
  12.4 4.3 collective-permute-done.1
  16.8 3.5 collective-permute-start.2
  20.2 1.3 collective-permute-start.3
  21.6 0.4 collective-permute-done.2
  21.9 4.2 collective-permute-done.3
  26.2 1.8 pad_maximum_fusion
  27.9 414.1 %while.10 = (s32[]{:T(128)}, bf16[4,256,2,32]{1,3,2,0:T(8,128)(2,1)S(1)}, bf16[257,14,134]{0,2,1:T(8,128)(2,1)}, f32[4,2,7,7]{3,1,2,0:T(2,128)}, s32[]{:T(128)}) while((s32[]{:T(128)}, bf16[4,256,2,32]{1,3,2,0:T(8,128)(2,1)S(1)}, bf16[257,14,134]{0,2,1:T(8,128)(2,1)}, f32[4,2,7,7]{3,1,2,0:T(2,128)}, s32[]{:T(128)}) %tuple.29), condition=%wide.region_2.3_spmd, body=%wide.region_0.2_spmd.sunk | while | flops 312647680 | bytes 15818389 | solution.py:53
  27.9 0.7 dynamic-slice_bitcast_fusion.2
  28.8 87.6 %fusion.42 = f32[257,2,8,128]{0,1,3,2:T(2,128)S(1)} fusion(f32[2,1,7,7]{1,0,3,2:T(2,128)S(1)} %copy.40, bf16[257,1,14,134]{0,3,2,1:T(8,128)(2,1)} %bitcast.71), kind=kOutput, calls=%fused_computation.clone.1 | convolution fusion | flops 309485568 | bytes 3070000 | tf_op jit(solution)/shard_map/while/body/eval_jaxpr/conv_general_dilated | solution.py:42
  116.4 13.7 %multiply_reduce_fusion.4 = (f32[256,8,128]{0,2,1:T(8,128)S(1)}, f32[256,8,128]{0,2,1:T(8,128)S(1)}) fusion(f32[257,2,8,128]{0,1,3,2:T(2,128)S(1)} %fusion.42), kind=kLoop, calls=%fused_computation.3.clone.1 | loop fusion | flops 1835008 | bytes 6291456 | tf_op jit(solution)/shard_map/while/body/eval_jaxpr/mul | solution.py:49
  130.1 0.3 mul.70
  130.5 0.3 sub.13
  130.8 0.6 multiply_reduce_fusion.5
  131.4 0.7 dynamic-slice_bitcast_fusion.2
  132.3 87.6 %fusion.42 = f32[257,2,8,128]{0,1,3,2:T(2,128)S(1)} fusion(f32[2,1,7,7]{1,0,3,2:T(2,128)S(1)} %copy.40, bf16[257,1,14,134]{0,3,2,1:T(8,128)(2,1)} %bitcast.71), kind=kOutput, calls=%fused_computation.clone.1 | convolution fusion | flops 309485568 | bytes 3070000 | tf_op jit(solution)/shard_map/while/body/eval_jaxpr/conv_general_dilated | solution.py:42
  219.9 13.7 %multiply_reduce_fusion.4 = (f32[256,8,128]{0,2,1:T(8,128)S(1)}, f32[256,8,128]{0,2,1:T(8,128)S(1)}) fusion(f32[257,2,8,128]{0,1,3,2:T(2,128)S(1)} %fusion.42), kind=kLoop, calls=%fused_computation.3.clone.1 | loop fusion | flops 1835008 | bytes 6291456 | tf_op jit(solution)/shard_map/while/body/eval_jaxpr/mul | solution.py:49
  233.6 0.3 mul.70
  233.9 0.3 sub.13
  234.3 0.6 multiply_reduce_fusion.5
  234.9 0.7 dynamic-slice_bitcast_fusion.2
  235.8 87.6 %fusion.42 = f32[257,2,8,128]{0,1,3,2:T(2,128)S(1)} fusion(f32[2,1,7,7]{1,0,3,2:T(2,128)S(1)} %copy.40, bf16[257,1,14,134]{0,3,2,1:T(8,128)(2,1)} %bitcast.71), kind=kOutput, calls=%fused_computation.clone.1 | convolution fusion | flops 309485568 | bytes 3070000 | tf_op jit(solution)/shard_map/while/body/eval_jaxpr/conv_general_dilated | solution.py:42
  323.4 13.7 %multiply_reduce_fusion.4 = (f32[256,8,128]{0,2,1:T(8,128)S(1)}, f32[256,8,128]{0,2,1:T(8,128)S(1)}) fusion(f32[257,2,8,128]{0,1,3,2:T(2,128)S(1)} %fusion.42), kind=kLoop, calls=%fused_computation.3.clone.1 | loop fusion | flops 1835008 | bytes 6291456 | tf_op jit(solution)/shard_map/while/body/eval_jaxpr/mul | solution.py:49
  337.1 0.3 mul.70
  337.4 0.3 sub.13
  337.8 0.6 multiply_reduce_fusion.5
  338.4 0.7 dynamic-slice_bitcast_fusion.2
  339.3 87.6 %fusion.42 = f32[257,2,8,128]{0,1,3,2:T(2,128)S(1)} fusion(f32[2,1,7,7]{1,0,3,2:T(2,128)S(1)} %copy.40, bf16[257,1,14,134]{0,3,2,1:T(8,128)(2,1)} %bitcast.71), kind=kOutput, calls=%fused_computation.clone.1 | convolution fusion | flops 309485568 | bytes 3070000 | tf_op jit(solution)/shard_map/while/body/eval_jaxpr/conv_general_dilated | solution.py:42
  426.9 13.7 %multiply_reduce_fusion.4 = (f32[256,8,128]{0,2,1:T(8,128)S(1)}, f32[256,8,128]{0,2,1:T(8,128)S(1)}) fusion(f32[257,2,8,128]{0,1,3,2:T(2,128)S(1)} %fusion.42), kind=kLoop, calls=%fused_computation.3.clone.1 | loop fusion | flops 1835008 | bytes 6291456 | tf_op jit(solution)/shard_map/while/body/eval_jaxpr/mul | solution.py:49
  440.6 0.3 mul.70
  440.9 0.3 sub.13
  441.2 0.6 multiply_reduce_fusion.5
  442.1 0.9 convolution_bitcast_fusion
  443.0 92.4 %all-reduce.2.cloned.1.call-done = f32[256,256]{1,0:T(8,128)} async-done(((f32[256,256]{1,0:T(8,128)}), f32[256,256]{1,0:T(8,128)}) %all-reduce.2.cloned.1.call-update) | async-done | bytes 262160 | tf_op jit(solution)/shard_map/psum | solution.py:59
  535.4 1.3 fusion.6
  537.1 5.8 %cholesky.44 = f32[64,64]{1,0:T(8,128)S(1)} custom-call(f32[64,64]{1,0:T(8,128)S(1)} %fusion.18), custom_call_target="Cholesky" | custom-call | tf_op jit(solution)/shard_map/jit(cholesky)/cholesky | solution.py:28
  543.0 0.6 compare_reduce_fusion.1
  543.6 0.7 fusion.12
  544.3 4.9 custom-call.6
  549.2 0.3 convolution_bitcast_fusion.3
  549.4 1.3 fusion.4
  551.1 5.8 %cholesky.55 = f32[64,64]{1,0:T(8,128)S(1)} custom-call(f32[64,64]{1,0:T(8,128)S(1)} %fusion.16), custom_call_target="Cholesky" | custom-call | tf_op jit(solution)/shard_map/jit(cholesky)/cholesky | solution.py:28
  556.9 0.6 compare_reduce_fusion
  557.6 0.7 fusion.13
  558.2 4.9 custom-call.7
  563.7 0.8 reshape.57
  (29 shorter events, 2.1 us)
Async XLA Ops:
  7.2 528.3 %copy-start = (f32[256,64]{0,1:T(8,128)S(1)}, f32[256,64]{0,1:T(8,128)}, u32[]{:S(2)}) copy-start(f32[256,64]{0,1:T(8,128)} %param.10) | copy-start | bytes 196612
  7.2 528.3 %all-reduce.2.cloned.1.call-start = ((), (), s32[]{:S(2)}) async-start(), calls=%async_computation | async-start | bytes 524288 | tf_op jit(solution)/shard_map/psum | solution.py:59
  8.8 3.7 collective-permute-start
  11.1 5.6 collective-permute-start.1
  16.8 5.2 collective-permute-start.2
  20.2 5.9 %collective-permute-start.3 = (bf16[257,14,3]{0,2,1:T(4,128)(2,1)S(1)}, bf16[257,14,3]{0,2,1:T(4,128)(2,1)S(1)}, u32[]{:S(2)}, u32[]{:S(2)}) collective-permute-start(bf16[257,14,3]{0,2,1:T(4,128)(2,1)S(1)} %get-tuple-element.38), channel_id=1, source_target_pairs={{1,0},{2,1},{3,2},{5,4},{6,5},{7,6},{9,8},{10,9},{11,10},{13,12},{... | collective-permute-start | bytes 64772 | tf_op jit(solution)/shard_map/ppermute | solution.py:21
  563.4 1.0 copy-start.1
Sparse Core Ops, SparseCore 0:
  443.1 92.2 all-reduce.1
where the time goes:
time: 572 us; the launch traced here: 571 us
  matrix products  355 us (62%)
  waiting for transfers between devices  101 us (18%)
  other arithmetic  83.2 us (15%)
  between operations  14.2 us (2%)
  local copies, waits for them, and re-layouts  8.54 us (1%)
  starting transfers between devices  8.48 us (1%)
    conv_general_dilated x4, matrix products, orient(): lax.conv_general_dilated(lifted, kernels, (1, 1), 'VALID', precision=lax....  350 us
    psum x1, waiting for transfers between devices, on_device(): gram = lax.psum(local_gram, ('row', 'col')) / npix_all  92.4 us
    mul x4, other arithmetic, orient(): prod_real * prod_real + prod_imag * prod_imag + 1.0  54.8 us
    another operation x6, other arithmetic, orthonormal(): factor = jnp.linalg.cholesky(inner)  13 us
  transfers between devices with their start and end apart: 5, of which 4 were waited for; matrix products, arithmetic and copies ran while one was open for 0% of the time, Pallas kernels for 0%

commit v1 on v0

v1 whole, which is shorter than its diff:
```python
import functools

import jax
import jax.numpy as jnp
from jax import lax
from jax.experimental import pallas as pl
from jax.experimental.pallas import tpu as pltpu
from jax.sharding import PartitionSpec as P

FRAMES = 256
HALF = FRAMES // 2
MODES = 64
ORIENT = 4
TAPS = 7
REACH = 3
SWEEPS = 2
ROWS = 8
COLS = 128
BLOCKS = 16
F32 = jnp.float32
BF16 = jnp.bfloat16
HIGHEST = lax.Precision.HIGHEST
PARAMS = pltpu.CompilerParams(vmem_limit_bytes=48 * 1024 * 1024)
VMEM = pl.BlockSpec(memory_space=pltpu.VMEM)
SMEM = pl.BlockSpec(memory_space=pltpu.SMEM)


def spread(rows_ref, out_ref):
    for pair in range(ROWS // 2):
        for group in range(3):
            parts = []
            for row in (2 * pair, 2 * pair + 1):
                tile = rows_ref[pl.ds(group * ROWS + row, HALF, stride=2 * ROWS), :]
                parts.append(tile.T.reshape(BLOCKS, 8, HALF))
            both = jnp.concatenate(parts, axis=1).astype(BF16)
            out_ref[:, 16 * pair : 16 * pair + 16, HALF * group : HALF * (group + 1)] = both


def own_kernel(video_ref, taps_ref, own_ref, band_ref, rows_ref):
    rows_ref[...] = video_ref[...].astype(F32).reshape(rows_ref.shape)
    spread(rows_ref, own_ref)
    taps = taps_ref[...]
    high = taps.astype(BF16)
    low = (taps - high.astype(F32)).astype(BF16)
    parts = jnp.concatenate([high, low], axis=0)
    tap = lax.broadcasted_iota(jnp.int32, (128, 256), 0)
    lane = lax.broadcasted_iota(jnp.int32, (128, 256), 1)
    slot = (lane >> 3) & 15
    column = ((lane >> 7) << 3) | (lane & 7)
    slot_hit = slot == ((((tap >> 3) & 7) - REACH) & 15)
    ahead = column - (tap & 7) - 1 - 4 * (tap >> 6)
    for j in range(4):
        select = jnp.where(slot_hit & (ahead == j), 1.0, 0.0).astype(BF16)
        base = jnp.dot(parts, select, preferred_element_type=F32)
        for i in range(ROWS):
            start = (4 * i + j) * 16
            for side in range(2):
                rolled = base[:, 128 * side : 128 * side + 128]
                if i:
                    rolled = pltpu.roll(rolled, 8 * i, 1)
                rolled = rolled.astype(BF16)
                for part in range(2):
                    at = 256 * part + 128 * side
                    band_ref[start : start + 16, at : at + 128] = rolled[16 * part : 16 * part + 16]


def halo_kernel(parity_ref, a_ref, b_ref, own_ref, halo_ref, edge_a_ref, edge_b_ref, rows_ref):
    even = parity_ref[0] == 0
    got_a = a_ref[...].astype(F32)
    got_b = b_ref[...].astype(F32)
    below = jnp.where(even, got_a, got_b)
    above = jnp.where(even, got_b, got_a)
    none = jnp.zeros((FRAMES + 1, 2, COLS), F32)
    rows_ref[...] = jnp.concatenate([below, none, above], axis=1).reshape(rows_ref.shape)
    spread(rows_ref, halo_ref)
    block_a = (BLOCKS - 1) * (1 - parity_ref[1])
    block_b = (BLOCKS - 1) * parity_ref[1]
    edge_a_ref[0:64] = own_ref[block_a]
    edge_a_ref[64:128] = halo_ref[block_a]
    edge_b_ref[0:64] = own_ref[block_b]
    edge_b_ref[64:128] = halo_ref[block_b]


def block_feats(band_ref, window):
    pooled = []
    for cell in range(2):
        rows = slice(256 * cell, 256 * cell + 256)
        resp = jnp.dot(band_ref[rows, 0:256], window, preferred_element_type=F32)
        resp = resp + jnp.dot(band_ref[rows, 256:512], window, preferred_element_type=F32)
        total = jnp.zeros((8, FRAMES), F32)
        for pixel in range(16):
            real = resp[16 * pixel : 16 * pixel + 8]
            imag = resp[16 * pixel + 8 : 16 * pixel + 16]
            real_old, real_now = real[:, :FRAMES], real[:, HALF:]
            imag_old, imag_now = imag[:, :FRAMES], imag[:, HALF:]
            prod_real = real_now * real_old + imag_now * imag_old
            prod_imag = imag_now * real_old - real_now * imag_old
            total += prod_imag * lax.rsqrt(prod_real * prod_real + prod_imag * prod_imag + 1.0)
        pooled.append(total * (1.0 / 16.0))
    return jnp.concatenate(pooled, axis=0)


def inner_kernel(band_ref, own_ref, halo_ref, feats_ref):
    def body(block, carry):
        window = jnp.concatenate(
            [own_ref[block], halo_ref[block], own_ref[block + 1], halo_ref[block + 1]], axis=0
        )
        feats_ref[block] = block_feats(band_ref, window).astype(BF16)
        return carry

    lax.fori_loop(0, BLOCKS - 1, body, 0)


def edge_kernel(parity_ref, band_ref, own_ref, halo_ref, a_ref, b_ref, inner_ref, feats_ref, mine_ref, other_ref):
    even = parity_ref[1] == 0
    got_a = a_ref[...]
    got_b = b_ref[...]
    right = jnp.where(even, got_a, got_b)
    left = jnp.where(even, got_b, got_a)
    window_left = jnp.concatenate([left, own_ref[0], halo_ref[0]], axis=0)
    window_right = jnp.concatenate([own_ref[BLOCKS - 1], halo_ref[BLOCKS - 1], right], axis=0)
    feats_left = block_feats(band_ref, window_left)
    feats_right = block_feats(band_ref, window_right)
    second = (lax.broadcasted_iota(jnp.int32, (16, FRAMES), 0) & 4) == 4
    feats_ref[0 : BLOCKS - 1] = inner_ref[0 : BLOCKS - 1]
    feats_ref[BLOCKS - 1] = jnp.where(second, feats_left, feats_right).astype(BF16)
    flat = feats_ref[...].reshape(16 * BLOCKS, FRAMES)
    gram = lax.dot_general(flat, flat, (((0,), (0,)), ((), ())), preferred_element_type=F32)
    top, cross, low = gram[:HALF, :HALF], gram[:HALF, HALF:], gram[HALF:, HALF:]
    i = lax.broadcasted_iota(jnp.int32, (HALF, HALF), 0)
    j = lax.broadcasted_iota(jnp.int32, (HALF, HALF), 1)
    folded = jnp.where(i <= j, top, low)
    diagonal = jnp.sum(jnp.where(i == j, low, 0.0), axis=0, keepdims=True)
    first = parity_ref[0] == 0
    spare = jnp.broadcast_to(diagonal, (8, HALF))
    mine_ref[0:HALF] = jnp.where(first, cross, folded)
    mine_ref[HALF : HALF + 8] = spare
    other_ref[0:HALF] = jnp.where(first, folded, cross)
    other_ref[HALF : HALF + 8] = spare


def inverse_factor(inner):
    count = MODES // 8
    i = lax.broadcasted_iota(jnp.int32, (MODES, MODES), 0)
    j = lax.broadcasted_iota(jnp.int32, (MODES, MODES), 1)
    work = jnp.concatenate([jnp.where(i == j, 1.0, 0.0), inner], axis=1)
    work = [work[8 * v : 8 * v + 8] for v in range(count)]
    sub = lax.broadcasted_iota(jnp.int32, (8, 2 * MODES), 0)
    scale = [jnp.zeros((8, 2 * MODES), F32) for v in range(count)]
    for k in range(MODES):
        v0, s = divmod(k, 8)
        pivot_row = work[v0][s : s + 1, :]
        pivot = pivot_row[:, MODES + k : MODES + k + 1]
        scaled = pivot_row * (1.0 / pivot)
        scale[v0] = jnp.where(sub == s, lax.rsqrt(pivot), scale[v0])
        for v in range(v0, count):
            factor = work[v][:, MODES + k : MODES + k + 1]
            change = factor * scaled
            if v == v0:
                change = jnp.where(sub > s, change, 0.0)
            work[v] = work[v] - change
    return jnp.concatenate([work[v] * scale[v] for v in range(count)], axis=0)[:, :MODES]


def basis_kernel(scale, parity_ref, mine_ref, other_ref, start_ref, feats_ref, basis_ref, modes_ref, rows_ref, out_ref):
    first = parity_ref[0] == 0
    mine, other = mine_ref[...], other_ref[...]
    cross = jnp.where(first, mine, other)[:HALF]
    second = jnp.where(first, other, mine)
    folded = second[:HALF]
    i = lax.broadcasted_iota(jnp.int32, (HALF, HALF), 0)
    j = lax.broadcasted_iota(jnp.int32, (HALF, HALF), 1)
    turned = folded.T
    top = jnp.where(i <= j, folded, turned)
    low = jnp.where(i > j, folded, jnp.where(i < j, turned, second[HALF : HALF + 1]))
    gram = jnp.concatenate(
        [jnp.concatenate([top, cross], axis=1), jnp.concatenate([cross.T, low], axis=1)], axis=0
    )
    gram = gram * scale
    start = start_ref[...]
    rows_ref[...] = jnp.concatenate([start, start], axis=1)
    basis = jnp.concatenate([rows_ref[pl.ds(g, HALF, stride=2), :].T for g in range(2)], axis=1)[:MODES]
    for sweep in range(SWEEPS):
        stacked = jnp.dot(basis, gram, precision=HIGHEST, preferred_element_type=F32)
        inner = lax.dot_general(
            stacked, stacked, (((1,), (1,)), ((), ())), precision=HIGHEST, preferred_element_type=F32
        )
        basis = jnp.dot(inverse_factor(inner), stacked, precision=HIGHEST, preferred_element_type=F32)
    twice = jnp.concatenate([basis, basis], axis=0)
    for g in range(2):
        rows_ref[pl.ds(g, HALF, stride=2), :] = twice[:, HALF * g : HALF * g + HALF].T
    basis_ref[...] = rows_ref[:, :MODES]
    flat = feats_ref[...].reshape(16 * BLOCKS, FRAMES)
    rows_ref[...] = lax.dot_general(
        flat, twice.astype(BF16), (((1,), (1,)), ((), ())), preferred_element_type=F32
    )
    left = lax.broadcasted_iota(jnp.int32, (BLOCKS, 2 * MODES), 1) < MODES
    for row in range(2):
        for half in range(2):
            for cell in range(2):
                at = 8 * row + 4 * cell + 2 * half
                field = jnp.where(
                    left, rows_ref[pl.ds(at, BLOCKS, stride=16), :], rows_ref[pl.ds(at + 1, BLOCKS, stride=16), :]
                )
                if cell:
                    field = pltpu.roll(field, 1, 0)
                out_ref[pl.ds(64 * row + 32 * half + 1 - cell, BLOCKS, stride=2), :] = field
            modes_ref[row, :, 128 * half : 128 * half + 128] = out_ref[64 * row + 32 * half : 64 * row + 32 * half + 32]


def call(kernel, outs, n_smem, n_in, scratch=()):
    return pl.pallas_call(
        kernel,
        out_shape=[jax.ShapeDtypeStruct(shape, dtype) for shape, dtype in outs],
        in_specs=[SMEM] * n_smem + [VMEM] * (n_in - n_smem),
        out_specs=[VMEM] * len(outs),
        scratch_shapes=list(scratch),
        compiler_params=PARAMS,
    )


def pairs(size, start):
    swaps = []
    for i in range(start, size - 1, 2):
        swaps += [(i, i + 1), (i + 1, i)]
    return swaps


def on_device(video, filters, start_basis):
    size_row, size_col = lax.axis_size("row"), lax.axis_size("col")
    parity = jnp.stack([lax.axis_index("row") % 2, lax.axis_index("col") % 2]).astype(jnp.int32)
    even_row = parity[0] == 0

    first, last = video[:, :REACH, :], video[:, ROWS - REACH :, :]
    got_a = lax.ppermute(jnp.where(even_row, last, first), "row", pairs(size_row, 0))
    got_b = lax.ppermute(jnp.where(even_row, first, last), "row", pairs(size_row, 1))

    taps = jnp.pad(filters, ((0, 0), (0, 0), (0, 1), (0, 1))).reshape(ORIENT, 2, 64)
    taps = jnp.transpose(taps, (1, 0, 2))[:, None, :, None, :] * jnp.eye(2, dtype=F32)[None, :, None, :, None]
    taps = taps.reshape(16, 128)
    rows = pltpu.VMEM(((FRAMES + 1) * ROWS, COLS), F32)
    tile = ((BLOCKS, 64, 3 * HALF), BF16)
    edge = ((128, 3 * HALF), BF16)
    own, band = call(own_kernel, [tile, ((512, 512), BF16)], 0, 2, [rows])(video, taps)
    halo, edge_a, edge_b = call(halo_kernel, [tile, edge, edge], 1, 4, [rows])(parity, got_a, got_b, own)
    got_a = lax.ppermute(edge_a, "col", pairs(size_col, 0))
    got_b = lax.ppermute(edge_b, "col", pairs(size_col, 1))
    feats_shape = ((BLOCKS, 16, FRAMES), BF16)
    (inner,) = call(inner_kernel, [feats_shape], 0, 3)(band, own, halo)
    part = ((HALF + 8, HALF), F32)
    feats, mine, other = call(edge_kernel, [feats_shape, part, part], 1, 7)(
        parity, band, own, halo, got_a, got_b, inner
    )

    mine = mine + lax.ppermute(other, "row", pairs(size_row, 0))
    for axis, size, step in (("row", size_row, 2), ("col", size_col, 1)):
        while step < size:
            mine = mine + lax.ppermute(mine, axis, [(i, i ^ step) for i in range(size)])
            step *= 2
    other = lax.ppermute(mine, "row", pairs(size_row, 0))

    features = ORIENT * (size_row * ROWS // 4) * (size_col * COLS // 4)
    kernel = functools.partial(basis_kernel, 1.0 / features)
    return tuple(
        call(
            kernel,
            [((FRAMES, MODES), F32), ((ROWS // 4, COLS // 4, ORIENT * MODES), F32)],
            1,
            5,
            [pltpu.VMEM((FRAMES, 2 * MODES), F32), pltpu.VMEM((128, 128), F32)],
        )(parity, mine, other, start_basis, feats)
    )


def solution(mesh):
    return jax.shard_map(
        on_device,
        mesh=mesh,
        in_specs=(P("grp", "row", "col"), P(), P()),
        out_specs=(P("grp", None), P(("grp", "row"), "col", None)),
        check_vma=False,
    )
```

time: 572 us -> 57.1 us (0.10)
  matrix products: 355 us -> 0 us
  waiting for transfers between devices: 101 us -> 10.6 us
  other arithmetic: 83.2 us -> 1.73 us
  Pallas kernels: 0 us -> 24.4 us
  between operations: 14.2 us -> 0.8 us
  starting transfers between devices: 8.48 us -> 18.4 us
  local copies, waits for them, and re-layouts: 8.54 us -> 1 us
    conv_general_dilated x4 -> x0, matrix products: 350 us -> none  [orient(): lax.conv_general_dilated(lifted, kernels, (1, 1), 'VALID', precision=lax....]
    psum x1 -> x0, waiting for transfers between devices: 92.4 us -> none  [on_device(): gram = lax.psum(local_gram, ('row', 'col')) / npix_all]
    mul x4 -> x1, other arithmetic: 54.8 us -> 0.07 us  [on_device(): jnp.transpose(taps, (1, 0, 2))[:, None, :, None, :]]
    pallas_call x0 -> x5, Pallas kernels: none -> 24.4 us  [the longest x1 13.9 us: on_device(): call(kernel, [((FRAMES, MODES), F32), ((ROWS // 4, COLS // 4, ORIENT * MO...]
    another operation x10 -> x1, other arithmetic: 24.1 us -> 0.08 us  [on_device(): jnp.stack([lax.axis_index('row') % 2, lax.axis_index('col') % 2])]
    ppermute x4 -> x9, starting transfers between devices: 8.44 us -> 18.4 us  [the longest x3 7.69 us: on_device(): mine = mine + lax.ppermute(mine, axis, [(i, i ^ step) for i in range(size)])]
  transfers between devices with their start and end apart: 5 -> 9, of which waited for: 4 -> 5; matrix products, arithmetic and copies ran while one was open for 0% -> 1% of each run, Pallas kernels for 0% -> 13%
where the time goes in v1:
time: 57.1 us; the launch traced here: 56.9 us
  Pallas kernels  24.4 us (43%)
  starting transfers between devices  18.4 us (32%)
  waiting for transfers between devices  10.6 us (19%)
  other arithmetic  1.73 us (3%)
  local copies, waits for them, and re-layouts  1 us (2%)
  between operations  0.8 us (1%)
    pallas_call x1, Pallas kernels, on_device(): call(kernel, [((FRAMES, MODES), F32), ((ROWS // 4, COLS // 4, ORIENT * MO...  13.9 us
    ppermute x3, waiting for transfers between devices, on_device(): mine = mine + lax.ppermute(mine, axis, [(i, i ^ step) for i in range(size)])  8.55 us
    ppermute x3, starting transfers between devices, on_device(): mine = mine + lax.ppermute(mine, axis, [(i, i ^ step) for i in range(size)])  7.69 us
    pallas_call x1, Pallas kernels, on_device(): inner, = call(inner_kernel, [feats_shape], 0, 3)(band, own, halo)  6.74 us
    ppermute x1, starting transfers between devices, on_device(): mine = mine + lax.ppermute(other, 'row', pairs(size_row, 0))  6.09 us
    ppermute x1, starting transfers between devices, on_device(): got_a = lax.ppermute(edge_a, 'col', pairs(size_col, 0))  2.66 us
    pallas_call x1, Pallas kernels, on_device(): call(edge_kernel, [feats_shape, part, part], 1, 7)  1.55 us
    select_n x1, other arithmetic, on_device(): jnp.where(even_row, first, last)  1.53 us
  transfers between devices with their start and end apart: 9, of which 5 were waited for; matrix products, arithmetic and copies ran while one was open for 1% of the time, Pallas kernels for 13%

profile of v1, /device:TPU:0, one launch (start us, length us, event | category | flops | bytes accessed | tf_op | source)
XLA Modules:
  0.0 56.9 jit_solution(17213971718901288917)
XLA Ops:
  0.6 0.0 copy-start.2
  0.7 0.0 copy-start
  0.7 1.5 %broadcast_select_fusion = (bf16[257,3,128]{2,1,0:T(4,128)(2,1)S(1)}, bf16[257,3,128]{2,1,0:T(4,128)(2,1)S(1)}) fusion(pred[]{:T(512)S(6)} %eq.14, bf16[257,8,128]{2,1,0:T(8,128)(2,1)} %video_ref.1), kind=kLoop, calls=%fused_computation | loop fusion | flops 197376 | bytes 789505 | tf_op jit(solution)/shard_map/jit(_where)/select_n | solution.py:236
  2.2 0.5 collective-permute-start
  2.7 0.7 %collective-permute-start.1 = (bf16[257,3,128]{2,1,0:T(4,128)(2,1)S(1)}, bf16[257,3,128]{2,1,0:T(4,128)(2,1)S(1)}, u32[]{:S(2)}, u32[]{:S(2)}) collective-permute-start(bf16[257,3,128]{2,1,0:T(4,128)(2,1)S(1)} %get-tuple-element.22), channel_id=1, source_target_pairs={{4,8},{8,4},{5,9},{9,5},{6,10},{10,6},{7,11},{11,7},{20,24},{24,20... | collective-permute-start | bytes 592136 | tf_op jit(solution)/shard_map/ppermute | solution.py:236
  3.4 0.0 copy-done.2
  3.4 0.1 reshape.20
  3.5 0.1 broadcast_multiply_fusion
  3.6 0.1 mul.20.taps_ref
  3.7 0.0 copy-done
  3.7 0.8 %shard_map.50 = (bf16[16,64,384]{2,1,0:T(8,128)(2,1)S(1)}, bf16[512,512]{1,0:T(8,128)(2,1)S(1)}) custom-call(bf16[257,8,128]{2,1,0:T(8,128)(2,1)S(1)} %copy-done, f32[16,128]{1,0:T(8,128)S(1)} %mul.20.taps_ref), custom_call_target="tpu_custom_call" | custom-call | tf_op jit(solution)/shard_map/pallas_call | solution.py:244
  4.5 0.1 pad_add_fusion.parity_ref
  4.6 0.0 collective-permute-done.a_ref
  4.6 0.0 collective-permute-done.1.b_ref
  4.6 1.4 %shard_map.51 = (bf16[16,64,384]{2,1,0:T(8,128)(2,1)S(1)}, bf16[128,384]{1,0:T(8,128)(2,1)S(1)}, bf16[128,384]{1,0:T(8,128)(2,1)S(1)}) custom-call(s32[2]{0:T(128)S(1)} %pad_add_fusion.parity_ref, bf16[257,3,128]{2,1,0:T(4,128)(2,1)S(1)} %collective-permute-done.a_ref, bf16[257,3,128]{2,1,0:T(4,128)(2,1)S(1)} %collective-permute-done.1.b_ref, ...), custom_call_target="tpu_custom_call" | custom-call | tf_op jit(solution)/shard_map/pallas_call | solution.py:245
  6.0 2.7 %collective-permute-start.2 = (bf16[128,384]{1,0:T(8,128)(2,1)S(1)}, bf16[128,384]{1,0:T(8,128)(2,1)S(1)}, u32[]{:S(2)}, u32[]{:S(2)}) collective-permute-start(bf16[128,384]{1,0:T(8,128)(2,1)S(1)} %get-tuple-element.13), channel_id=1, source_target_pairs={{0,1},{1,0},{2,3},{3,2},{4,5},{5,4},{6,7},{7,6},{8,9},{9,8},{10,11... | collective-permute-start | bytes 294920 | tf_op jit(solution)/shard_map/ppermute | solution.py:246
  8.6 0.7 %collective-permute-start.3 = (bf16[128,384]{1,0:T(8,128)(2,1)S(1)}, bf16[128,384]{1,0:T(8,128)(2,1)S(1)}, u32[]{:S(2)}, u32[]{:S(2)}) collective-permute-start(bf16[128,384]{1,0:T(8,128)(2,1)S(1)} %get-tuple-element.14), channel_id=1, source_target_pairs={{1,2},{2,1},{5,6},{6,5},{9,10},{10,9},{13,14},{14,13},{17,18},{18,... | collective-permute-start | bytes 294920 | tf_op jit(solution)/shard_map/ppermute | solution.py:247
  9.3 6.7 %shard_map.52.inner_ref = bf16[16,16,256]{2,1,0:T(8,128)(2,1)S(1)} custom-call(bf16[512,512]{1,0:T(8,128)(2,1)S(1)} %get-tuple-element.10.band_ref, bf16[16,64,384]{2,1,0:T(8,128)(2,1)S(1)} %get-tuple-element.11.own_ref, bf16[16,64,384]{2,1,0:T(8,128)(2,1)S(1)} %get-tuple-element.12.halo_ref), custom_call_target="tpu_custom_call" | custom-call | tf_op jit(solution)/shard_map/pallas_call | solution.py:249
  16.0 0.0 collective-permute-done.2.a_ref
  16.1 0.0 collective-permute-done.3.b_ref
  16.1 1.6 %shard_map.53 = (bf16[16,16,256]{2,1,0:T(8,128)(2,1)S(1)}, f32[136,128]{1,0:T(8,128)S(1)}, f32[136,128]{1,0:T(8,128)S(1)}) custom-call(s32[2]{0:T(128)S(1)} %pad_add_fusion.parity_ref, bf16[512,512]{1,0:T(8,128)(2,1)S(1)} %get-tuple-element.10.band_ref, bf16[16,64,384]{2,1,0:T(8,128)(2,1)S(1)} %get-tuple-element.11.own_ref, ...), custom_call_target="tpu_custom_call" | custom-call | tf_op jit(solution)/shard_map/pallas_call | solution.py:251
  17.6 6.1 %collective-permute-start.4 = (f32[136,128]{1,0:T(8,128)S(1)}, f32[136,128]{1,0:T(8,128)S(1)}, u32[]{:S(2)}, u32[]{:S(2)}) collective-permute-start(f32[136,128]{1,0:T(8,128)S(1)} %get-tuple-element.16), channel_id=1, source_target_pairs={{0,4},{4,0},{8,12},{12,8},{1,5},{5,1},{9,13},{13,9},{2,6},{6,2},{1... | collective-permute-start | bytes 208904 | tf_op jit(solution)/shard_map/ppermute | solution.py:255
  23.7 0.9 %collective-permute-done.4 = f32[136,128]{1,0:T(8,128)S(1)} collective-permute-done((f32[136,128]{1,0:T(8,128)S(1)}, f32[136,128]{1,0:T(8,128)S(1)}, u32[]{:S(2)}, u32[]{:S(2)}) %collective-permute-start.4) | collective-permute-done | bytes 69664 | tf_op jit(solution)/shard_map/ppermute | solution.py:255
  24.6 1.7 %collective-permute-start.5 = (f32[136,128]{1,0:T(8,128)S(1)}, f32[136,128]{1,0:T(8,128)S(1)}, u32[]{:S(2)}, u32[]{:S(2)}) collective-permute-start(f32[136,128]{1,0:T(8,128)S(1)} %add.23), channel_id=1, source_target_pairs={{0,8},{4,12},{8,0},{12,4},{1,9},{5,13},{9,1},{13,5},{2,10},{6,14},... | collective-permute-start | bytes 208904 | tf_op jit(solution)/shard_map/ppermute | solution.py:258
  26.3 2.8 %collective-permute-done.5 = f32[136,128]{1,0:T(8,128)S(1)} collective-permute-done((f32[136,128]{1,0:T(8,128)S(1)}, f32[136,128]{1,0:T(8,128)S(1)}, u32[]{:S(2)}, u32[]{:S(2)}) %collective-permute-start.5) | collective-permute-done | bytes 69664 | tf_op jit(solution)/shard_map/ppermute | solution.py:258
  29.2 4.2 %collective-permute-start.6 = (f32[136,128]{1,0:T(8,128)S(1)}, f32[136,128]{1,0:T(8,128)S(1)}, u32[]{:S(2)}, u32[]{:S(2)}) collective-permute-start(f32[136,128]{1,0:T(8,128)S(1)} %add.24), channel_id=1, source_target_pairs={{0,1},{1,0},{2,3},{3,2},{4,5},{5,4},{6,7},{7,6},{8,9},{9,8},{10,11... | collective-permute-start | bytes 208904 | tf_op jit(solution)/shard_map/ppermute | solution.py:258
  33.3 2.3 %collective-permute-done.6 = f32[136,128]{1,0:T(8,128)S(1)} collective-permute-done((f32[136,128]{1,0:T(8,128)S(1)}, f32[136,128]{1,0:T(8,128)S(1)}, u32[]{:S(2)}, u32[]{:S(2)}) %collective-permute-start.6) | collective-permute-done | bytes 69664 | tf_op jit(solution)/shard_map/ppermute | solution.py:258
  35.6 0.0 copy-start.1
  35.6 1.8 %collective-permute-start.7 = (f32[136,128]{1,0:T(8,128)S(1)}, f32[136,128]{1,0:T(8,128)S(1)}, u32[]{:S(2)}, u32[]{:S(2)}) collective-permute-start(f32[136,128]{1,0:T(8,128)S(1)} %add.25), channel_id=1, source_target_pairs={{0,2},{1,3},{2,0},{3,1},{4,6},{5,7},{6,4},{7,5},{8,10},{9,11},{10,... | collective-permute-start | bytes 208904 | tf_op jit(solution)/shard_map/ppermute | solution.py:258
  37.5 3.5 %collective-permute-done.7 = f32[136,128]{1,0:T(8,128)S(1)} collective-permute-done((f32[136,128]{1,0:T(8,128)S(1)}, f32[136,128]{1,0:T(8,128)S(1)}, u32[]{:S(2)}, u32[]{:S(2)}) %collective-permute-start.7) | collective-permute-done | bytes 69664 | tf_op jit(solution)/shard_map/ppermute | solution.py:258
  40.9 0.1 collective-permute-start.8
  41.0 0.0 copy-done.1
  41.0 0.1 copy.9.start_ref
  41.1 1.1 %collective-permute-done.8.other_ref = f32[136,128]{1,0:T(8,128)S(1)} collective-permute-done((f32[136,128]{1,0:T(8,128)S(1)}, f32[136,128]{1,0:T(8,128)S(1)}, u32[]{:S(2)}, u32[]{:S(2)}) %collective-permute-start.8) | collective-permute-done | bytes 69664 | tf_op jit(solution)/shard_map/ppermute | solution.py:260
  42.3 13.9 %shard_map.54 = (f32[256,64]{1,0:T(8,128)S(1)}, f32[2,32,256]{2,1,0:T(8,128)}) custom-call(s32[2]{0:T(128)S(1)} %pad_add_fusion.parity_ref, f32[136,128]{1,0:T(8,128)S(1)} %add.26.mine_ref, f32[136,128]{1,0:T(8,128)S(1)} %collective-permute-done.8.other_ref, f32[256,64]{1,0:T(8,128)S(1)} %copy.9.start_ref, bf16[16,16,256]{2,1,0:T(8,128)(2,1)S(1)} %get-tuple-element.17.feats_ref), custom_call_target="tpu_custom_call" | custom-call | tf_op jit(solution)/shard_map/pallas_call | solution.py:265
  56.2 0.7 %copy.10 = f32[256,64]{0,1:T(8,128)} copy(f32[256,64]{1,0:T(8,128)S(1)} %get-tuple-element.20) | data formatting | bytes 131072 | tf_op jit(solution)/shard_map/pallas_call | solution.py:265
  (8 shorter events, 0.1 us)
Async XLA Ops:
  0.6 2.8 %copy-start.2 = (f32[4,2,7,7]{3,1,2,0:T(2,128)S(1)}, f32[4,2,7,7]{3,1,2,0:T(2,128)}, u32[]{:S(2)}) copy-start(f32[4,2,7,7]{3,1,2,0:T(2,128)} %param.4) | copy-start | bytes 4708
  0.7 3.0 %copy-start = (bf16[257,8,128]{2,1,0:T(8,128)(2,1)S(1)}, bf16[257,8,128]{2,1,0:T(8,128)(2,1)}, u32[]{:S(2)}) copy-start(bf16[257,8,128]{2,1,0:T(8,128)(2,1)} %video_ref.1) | copy-start | bytes 1579012
  2.2 2.4 %collective-permute-start = (bf16[257,3,128]{2,1,0:T(4,128)(2,1)S(1)}, bf16[257,3,128]{2,1,0:T(4,128)(2,1)S(1)}, u32[]{:S(2)}, u32[]{:S(2)}) collective-permute-start(bf16[257,3,128]{2,1,0:T(4,128)(2,1)S(1)} %get-tuple-element.23), channel_id=1, source_target_pairs={{0,4},{4,0},{8,12},{12,8},{1,5},{5,1},{9,13},{13,9},{2,6},{6,2},{1... | collective-permute-start | bytes 592136 | tf_op jit(solution)/shard_map/ppermute | solution.py:235
  2.7 1.9 %collective-permute-start.1 = (bf16[257,3,128]{2,1,0:T(4,128)(2,1)S(1)}, bf16[257,3,128]{2,1,0:T(4,128)(2,1)S(1)}, u32[]{:S(2)}, u32[]{:S(2)}) collective-permute-start(bf16[257,3,128]{2,1,0:T(4,128)(2,1)S(1)} %get-tuple-element.22), channel_id=1, source_target_pairs={{4,8},{8,4},{5,9},{9,5},{6,10},{10,6},{7,11},{11,7},{20,24},{24,20... | collective-permute-start | bytes 592136 | tf_op jit(solution)/shard_map/ppermute | solution.py:236
  6.0 10.1 %collective-permute-start.2 = (bf16[128,384]{1,0:T(8,128)(2,1)S(1)}, bf16[128,384]{1,0:T(8,128)(2,1)S(1)}, u32[]{:S(2)}, u32[]{:S(2)}) collective-permute-start(bf16[128,384]{1,0:T(8,128)(2,1)S(1)} %get-tuple-element.13), channel_id=1, source_target_pairs={{0,1},{1,0},{2,3},{3,2},{4,5},{5,4},{6,7},{7,6},{8,9},{9,8},{10,11... | collective-permute-start | bytes 294920 | tf_op jit(solution)/shard_map/ppermute | solution.py:246
  8.6 7.4 %collective-permute-start.3 = (bf16[128,384]{1,0:T(8,128)(2,1)S(1)}, bf16[128,384]{1,0:T(8,128)(2,1)S(1)}, u32[]{:S(2)}, u32[]{:S(2)}) collective-permute-start(bf16[128,384]{1,0:T(8,128)(2,1)S(1)} %get-tuple-element.14), channel_id=1, source_target_pairs={{1,2},{2,1},{5,6},{6,5},{9,10},{10,9},{13,14},{14,13},{17,18},{18,... | collective-permute-start | bytes 294920 | tf_op jit(solution)/shard_map/ppermute | solution.py:247
  17.6 7.0 %collective-permute-start.4 = (f32[136,128]{1,0:T(8,128)S(1)}, f32[136,128]{1,0:T(8,128)S(1)}, u32[]{:S(2)}, u32[]{:S(2)}) collective-permute-start(f32[136,128]{1,0:T(8,128)S(1)} %get-tuple-element.16), channel_id=1, source_target_pairs={{0,4},{4,0},{8,12},{12,8},{1,5},{5,1},{9,13},{13,9},{2,6},{6,2},{1... | collective-permute-start | bytes 208904 | tf_op jit(solution)/shard_map/ppermute | solution.py:255
  24.6 4.5 %collective-permute-start.5 = (f32[136,128]{1,0:T(8,128)S(1)}, f32[136,128]{1,0:T(8,128)S(1)}, u32[]{:S(2)}, u32[]{:S(2)}) collective-permute-start(f32[136,128]{1,0:T(8,128)S(1)} %add.23), channel_id=1, source_target_pairs={{0,8},{4,12},{8,0},{12,4},{1,9},{5,13},{9,1},{13,5},{2,10},{6,14},... | collective-permute-start | bytes 208904 | tf_op jit(solution)/shard_map/ppermute | solution.py:258
  29.2 6.5 %collective-permute-start.6 = (f32[136,128]{1,0:T(8,128)S(1)}, f32[136,128]{1,0:T(8,128)S(1)}, u32[]{:S(2)}, u32[]{:S(2)}) collective-permute-start(f32[136,128]{1,0:T(8,128)S(1)} %add.24), channel_id=1, source_target_pairs={{0,1},{1,0},{2,3},{3,2},{4,5},{5,4},{6,7},{7,6},{8,9},{9,8},{10,11... | collective-permute-start | bytes 208904 | tf_op jit(solution)/shard_map/ppermute | solution.py:258
  35.6 5.4 %copy-start.1 = (f32[256,64]{0,1:T(8,128)S(1)}, f32[256,64]{0,1:T(8,128)}, u32[]{:S(2)}) copy-start(f32[256,64]{0,1:T(8,128)} %param.5) | copy-start | bytes 196612
  35.6 5.3 %collective-permute-start.7 = (f32[136,128]{1,0:T(8,128)S(1)}, f32[136,128]{1,0:T(8,128)S(1)}, u32[]{:S(2)}, u32[]{:S(2)}) collective-permute-start(f32[136,128]{1,0:T(8,128)S(1)} %add.25), channel_id=1, source_target_pairs={{0,2},{1,3},{2,0},{3,1},{4,6},{5,7},{6,4},{7,5},{8,10},{9,11},{10,... | collective-permute-start | bytes 208904 | tf_op jit(solution)/shard_map/ppermute | solution.py:258
  40.9 1.3 %collective-permute-start.8 = (f32[136,128]{1,0:T(8,128)S(1)}, f32[136,128]{1,0:T(8,128)S(1)}, u32[]{:S(2)}, u32[]{:S(2)}) collective-permute-start(f32[136,128]{1,0:T(8,128)S(1)} %add.26.mine_ref), channel_id=1, source_target_pairs={{0,4},{4,0},{8,12},{12,8},{1,5},{5,1},{9,13},{13,9},{2,6},{6,2},{1... | collective-permute-start | bytes 208904 | tf_op jit(solution)/shard_map/ppermute | solution.py:260

commit v2 on v1

v2 whole, which is shorter than its diff:
```python
import functools

import jax
import jax.numpy as jnp
from jax import lax
from jax.experimental import pallas as pl
from jax.experimental.pallas import tpu as pltpu
from jax.sharding import PartitionSpec as P

FRAMES = 256
HALF = FRAMES // 2
MODES = 64
ORIENT = 4
TAPS = 7
REACH = 3
SWEEPS = 2
ROWS = 8
COLS = 128
BLOCKS = 16
F32 = jnp.float32
BF16 = jnp.bfloat16
HIGHEST = lax.Precision.HIGHEST
PARAMS = pltpu.CompilerParams(vmem_limit_bytes=48 * 1024 * 1024)
VMEM = pl.BlockSpec(memory_space=pltpu.VMEM)
SMEM = pl.BlockSpec(memory_space=pltpu.SMEM)


def turned(rows_ref, row, group):
    return rows_ref[pl.ds(group * ROWS + row, HALF, stride=2 * ROWS), :].T


def blocked(upper, lower):
    both = [part.reshape(BLOCKS, 8, HALF) for part in (upper, lower)]
    return jnp.concatenate(both, axis=1).astype(BF16)


def own_kernel(parity_ref, video_ref, send_a_ref, send_b_ref, x_ref, rim_ref, rows_ref):
    even = parity_ref[0] == 0
    rows_ref[...] = video_ref[...].astype(F32).reshape(rows_ref.shape)
    for group in range(3):
        lanes = slice(HALF * group, HALF * group + HALF)
        tiles = [turned(rows_ref, row, group) for row in range(ROWS)]
        if group < 2:
            for i in range(REACH):
                first, last = tiles[i], tiles[ROWS - REACH + i]
                at = slice(COLS * i, COLS * i + COLS)
                send_a_ref[at, lanes] = jnp.where(even, last, first).astype(BF16)
                send_b_ref[at, lanes] = jnp.where(even, first, last).astype(BF16)
        for pair in range(3):
            x_ref[:, 32 + 16 * pair : 48 + 16 * pair, lanes] = blocked(tiles[2 * pair + 1], tiles[2 * pair + 2])
        rim_ref[0, :, lanes] = tiles[0]
        rim_ref[1, :, lanes] = tiles[ROWS - 1]
    final = rows_ref[FRAMES * ROWS : FRAMES * ROWS + ROWS, :]
    shifted = pltpu.roll(final, REACH, 0)
    fill = jnp.zeros((8, COLS), F32)
    for ref, chosen in ((send_a_ref, jnp.where(even, shifted, final)), (send_b_ref, jnp.where(even, final, shifted))):
        tail = jnp.concatenate([chosen, fill], axis=0).astype(BF16)
        ref[REACH * COLS : REACH * COLS + 16, 0:COLS] = tail
        ref[REACH * COLS : REACH * COLS + 16, COLS : 2 * COLS] = tail


def band_kernel(taps_ref, start_ref, band_ref, basis_ref):
    taps = taps_ref[...]
    high = taps.astype(BF16)
    low = (taps - high.astype(F32)).astype(BF16)
    parts = jnp.concatenate([high, low], axis=0)
    tap = lax.broadcasted_iota(jnp.int32, (128, 128), 0)
    lane = lax.broadcasted_iota(jnp.int32, (128, 128), 1)
    column = ((lane >> 6) << 3) | (lane & 7)
    row_hit = ((lane >> 3) & 7) == ((tap >> 3) & 7)
    ahead = column - (tap & 7) - 1 - 4 * (tap >> 6)
    for j in range(4):
        select = jnp.where(row_hit & (ahead == j), 1.0, 0.0).astype(BF16)
        base = jnp.dot(parts, select, preferred_element_type=F32)
        for i in range(2):
            start = (4 * i + j) * 16
            rolled = (pltpu.roll(base, 8, 1) if i else base).astype(BF16)
            band_ref[start : start + 16, 0:128] = rolled[:16]
            band_ref[start : start + 16, 128:256] = rolled[16:]
    basis_ref[...] = jnp.dot(start_ref[...], frame_order(0), precision=HIGHEST, preferred_element_type=F32)


def frame_order(axis):
    frame = lax.broadcasted_iota(jnp.int32, (FRAMES, FRAMES), axis)
    lane = lax.broadcasted_iota(jnp.int32, (FRAMES, FRAMES), 1 - axis)
    return jnp.where(frame == 2 * (lane & (HALF - 1)) + (lane >> 7), 1.0, 0.0).astype(F32)


def halo_kernel(parity_ref, a_ref, b_ref, x_in_ref, rim_ref, x_ref, edge_a_ref, edge_b_ref):
    even = parity_ref[0] == 0
    got_a, got_b = a_ref[...], b_ref[...]
    final = lax.broadcasted_iota(jnp.int32, (COLS, HALF), 1) == HALF - 1
    sides = []
    for got in (jnp.where(even, got_b, got_a), jnp.where(even, got_a, got_b)):
        got = got.astype(F32)
        ends = got[REACH * COLS : REACH * COLS + 8, :COLS].T
        rows = []
        for i in range(REACH):
            tile = got[COLS * i : COLS * i + COLS]
            late = jnp.where(final, ends[:, i : i + 1], pltpu.roll(tile[:, :HALF], HALF - 1, 1))
            rows.append([tile[:, :HALF], tile[:, HALF:], late])
        sides.append(rows)
    above, below = sides
    for group in range(3):
        lanes = slice(HALF * group, HALF * group + HALF)
        x_ref[:, 0:16, lanes] = blocked(above[0][group], above[1][group])
        x_ref[:, 16:32, lanes] = blocked(above[2][group], rim_ref[0, :, lanes])
        x_ref[:, 80:96, lanes] = blocked(rim_ref[1, :, lanes], below[0][group])
        x_ref[:, 96:112, lanes] = blocked(below[1][group], below[2][group])
    x_ref[:, 32:80, :] = x_in_ref[:, 32:80, :]
    edge_a_ref[...] = x_ref[(BLOCKS - 1) * (1 - parity_ref[1])]
    edge_b_ref[...] = x_ref[(BLOCKS - 1) * parity_ref[1]]


def block_feats(band_ref, left, right):
    pooled = []
    for cell in range(2):
        windows = []
        for half in range(2):
            at = 16 * (2 * cell + half)
            windows.append(jnp.concatenate([left[at : at + 64], right[at : at + 64]], axis=0))
        window = jnp.concatenate(
            [windows[0][:, :FRAMES], windows[1][:, :FRAMES], windows[0][:, FRAMES:], windows[1][:, FRAMES:]], axis=1
        )
        window = jnp.concatenate([window, window], axis=0)
        resp = jnp.dot(band_ref[...], window, preferred_element_type=F32)
        total = [None, None]
        for half in range(2):
            starts = (FRAMES * half, FRAMES * half + HALF, 2 * FRAMES + HALF * half)
            for pixel in range(8):
                at = 16 * pixel
                real = [resp[at : at + 8, s : s + HALF] for s in starts]
                imag = [resp[at + 8 : at + 16, s : s + HALF] for s in starts]
                for g in range(2):
                    prod_real = real[g + 1] * real[g] + imag[g + 1] * imag[g]
                    prod_imag = imag[g + 1] * real[g] - real[g + 1] * imag[g]
                    motion = prod_imag * lax.rsqrt(prod_real * prod_real + prod_imag * prod_imag + 1.0)
                    total[g] = motion if total[g] is None else total[g] + motion
        pooled.append(jnp.concatenate(total, axis=1) * (1.0 / 16.0))
    return jnp.concatenate(pooled, axis=0)


def inner_kernel(band_ref, x_ref, feats_ref):
    def body(step, carry):
        for i in range(3):
            block = 3 * step + i
            feats_ref[block] = block_feats(band_ref, x_ref[block], x_ref[block + 1]).astype(BF16)
        return carry

    lax.fori_loop(0, (BLOCKS - 1) // 3, body, 0)


def edge_kernel(parity_ref, band_ref, x_ref, a_ref, b_ref, inner_ref, feats_ref, mine_ref, other_ref):
    even = parity_ref[1] == 0
    got_a = a_ref[...]
    got_b = b_ref[...]
    right = jnp.where(even, got_a, got_b)
    left = jnp.where(even, got_b, got_a)
    feats_left = block_feats(band_ref, left, x_ref[0])
    feats_right = block_feats(band_ref, x_ref[BLOCKS - 1], right)
    second = (lax.broadcasted_iota(jnp.int32, (16, FRAMES), 0) & 4) == 4
    feats_ref[0 : BLOCKS - 1] = inner_ref[0 : BLOCKS - 1]
    feats_ref[BLOCKS - 1] = jnp.where(second, feats_left, feats_right).astype(BF16)
    flat = feats_ref[...].reshape(16 * BLOCKS, FRAMES)
    gram = lax.dot_general(flat, flat, (((0,), (0,)), ((), ())), preferred_element_type=F32)
    top, cross, low = gram[:HALF, :HALF], gram[:HALF, HALF:], gram[HALF:, HALF:]
    i = lax.broadcasted_iota(jnp.int32, (HALF, HALF), 0)
    j = lax.broadcasted_iota(jnp.int32, (HALF, HALF), 1)
    folded = jnp.where(i <= j, top, low)
    diagonal = jnp.sum(jnp.where(i == j, low, 0.0), axis=0, keepdims=True)
    first = parity_ref[0] == 0
    spare = jnp.broadcast_to(diagonal, (8, HALF))
    mine_ref[0:HALF] = jnp.where(first, cross, folded)
    mine_ref[HALF : HALF + 8] = spare
    other_ref[0:HALF] = jnp.where(first, folded, cross)
    other_ref[HALF : HALF + 8] = spare


def inverse_factor(inner):
    count = MODES // 8
    shape = (8, 2 * MODES)
    i = lax.broadcasted_iota(jnp.int32, (MODES, MODES), 0)
    j = lax.broadcasted_iota(jnp.int32, (MODES, MODES), 1)
    work = jnp.concatenate([jnp.where(i == j, 1.0, 0.0), inner], axis=1)
    work = [work[8 * v : 8 * v + 8] for v in range(count)]
    sub = lax.broadcasted_iota(jnp.int32, shape, 0)
    done = []
    for b in range(count):
        lane = MODES + 8 * b
        cols = [[jnp.broadcast_to(work[v][:, lane + m : lane + m + 1], shape) for v in range(b, count)] for m in range(8)]
        scale = jnp.zeros(shape, F32)
        for m in range(8):
            lead = cols[m][0]
            pivot = jnp.broadcast_to(lead[m : m + 1], shape)
            inverse = 1.0 / pivot
            scale = jnp.where(sub == m, lax.rsqrt(pivot), scale)
            row = jnp.broadcast_to(work[b][m : m + 1], shape) * inverse
            for q in range(m + 1, 8):
                times = jnp.broadcast_to(lead[q : q + 1], shape) * inverse
                cols[q] = [c - d * times for c, d in zip(cols[q], cols[m])]
            work[b] = work[b] - jnp.where(sub > m, lead, 0.0) * row
            for v in range(b + 1, count):
                work[v] = work[v] - cols[m][v - b] * row
        done.append(work[b] * scale)
    return jnp.concatenate(done, axis=0)[:, :MODES]


def basis_kernel(scale, parity_ref, mine_ref, other_ref, start_ref, feats_ref, basis_ref, modes_ref, rows_ref, out_ref):
    first = parity_ref[0] == 0
    mine, other = mine_ref[...], other_ref[...]
    cross = jnp.where(first, mine, other)[:HALF]
    second = jnp.where(first, other, mine)
    folded = second[:HALF]
    i = lax.broadcasted_iota(jnp.int32, (HALF, HALF), 0)
    j = lax.broadcasted_iota(jnp.int32, (HALF, HALF), 1)
    flipped = folded.T
    top = jnp.where(i <= j, folded, flipped)
    low = jnp.where(i > j, folded, jnp.where(i < j, flipped, second[HALF : HALF + 1]))
    gram = jnp.concatenate(
        [jnp.concatenate([top, cross], axis=1), jnp.concatenate([cross.T, low], axis=1)], axis=0
    )
    gram = gram * scale
    basis = start_ref[...]
    for sweep in range(SWEEPS):
        stacked = jnp.dot(basis, gram, precision=HIGHEST, preferred_element_type=F32)
        inner = lax.dot_general(
            stacked, stacked, (((1,), (1,)), ((), ())), precision=HIGHEST, preferred_element_type=F32
        )
        basis = jnp.dot(inverse_factor(inner), stacked, precision=HIGHEST, preferred_element_type=F32)
    basis_ref[...] = jnp.dot(basis, frame_order(1), precision=HIGHEST, preferred_element_type=F32)
    twice = jnp.concatenate([basis, basis], axis=0)
    flat = feats_ref[...].reshape(16 * BLOCKS, FRAMES)
    rows_ref[...] = lax.dot_general(
        flat, twice.astype(BF16), (((1,), (1,)), ((), ())), preferred_element_type=F32
    )
    left = lax.broadcasted_iota(jnp.int32, (BLOCKS, 2 * MODES), 1) < MODES
    for row in range(2):
        for half in range(2):
            for cell in range(2):
                at = 8 * row + 4 * cell + 2 * half
                field = jnp.where(
                    left, rows_ref[pl.ds(at, BLOCKS, stride=16), :], rows_ref[pl.ds(at + 1, BLOCKS, stride=16), :]
                )
                if cell:
                    field = pltpu.roll(field, 1, 0)
                out_ref[pl.ds(64 * row + 32 * half + 1 - cell, BLOCKS, stride=2), :] = field
            modes_ref[row, :, 128 * half : 128 * half + 128] = out_ref[64 * row + 32 * half : 64 * row + 32 * half + 32]


def call(kernel, outs, n_smem, n_in, scratch=(), aliases={}):
    return pl.pallas_call(
        kernel,
        out_shape=[jax.ShapeDtypeStruct(shape, dtype) for shape, dtype in outs],
        in_specs=[SMEM] * n_smem + [VMEM] * (n_in - n_smem),
        out_specs=[VMEM] * len(outs),
        scratch_shapes=list(scratch),
        input_output_aliases=aliases,
        compiler_params=PARAMS,
    )


def pairs(size, start):
    swaps = []
    for i in range(start, size - 1, 2):
        swaps += [(i, i + 1), (i + 1, i)]
    return swaps


def on_device(video, filters, start_basis):
    size_row, size_col = lax.axis_size("row"), lax.axis_size("col")
    parity = jnp.stack([lax.axis_index("row") & 1, lax.axis_index("col") & 1]).astype(jnp.int32)

    rows = pltpu.VMEM(((FRAMES + 1) * ROWS, COLS), F32)
    send = ((REACH * COLS + 16, FRAMES), BF16)
    tile = ((BLOCKS, 112, 3 * HALF), BF16)
    rim = ((2, COLS, 3 * HALF), F32)
    send_a, send_b, x, rim = call(own_kernel, [send, send, tile, rim], 1, 2, [rows])(parity, video)
    got_a = lax.ppermute(send_a, "row", pairs(size_row, 0))
    got_b = lax.ppermute(send_b, "row", pairs(size_row, 1))

    taps = jnp.pad(filters, ((0, 0), (0, 0), (0, 1), (0, 1))).reshape(ORIENT, 2, 64)
    taps = jnp.transpose(taps, (1, 0, 2))[:, None, :, None, :] * jnp.eye(2, dtype=F32)[None, :, None, :, None]
    band, start = call(band_kernel, [((128, 256), BF16), ((MODES, FRAMES), F32)], 0, 2)(
        taps.reshape(16, 128), start_basis.T
    )
    edge = ((112, 3 * HALF), BF16)
    x, edge_a, edge_b = call(halo_kernel, [tile, edge, edge], 1, 5)(parity, got_a, got_b, x, rim)
    got_a = lax.ppermute(edge_a, "col", pairs(size_col, 0))
    got_b = lax.ppermute(edge_b, "col", pairs(size_col, 1))
    feats_shape = ((BLOCKS, 16, FRAMES), BF16)
    (inner,) = call(inner_kernel, [feats_shape], 0, 2)(band, x)
    part = ((HALF + 8, HALF), F32)
    feats, mine, other = call(edge_kernel, [feats_shape, part, part], 1, 6)(parity, band, x, got_a, got_b, inner)

    mine = mine + lax.ppermute(other, "row", pairs(size_row, 0))
    for axis, size, step in (("row", size_row, 2), ("col", size_col, 1)):
        while step < size:
            mine = mine + lax.ppermute(mine, axis, [(i, i ^ step) for i in range(size)])
            step *= 2
    other = lax.ppermute(mine, "row", pairs(size_row, 0))

    features = ORIENT * (size_row * ROWS // 4) * (size_col * COLS // 4)
    kernel = functools.partial(basis_kernel, 1.0 / features)
    basis, modes = call(
        kernel,
        [((MODES, FRAMES), F32), ((ROWS // 4, COLS // 4, ORIENT * MODES), F32)],
        1,
        5,
        [pltpu.VMEM((FRAMES, 2 * MODES), F32), pltpu.VMEM((128, 128), F32)],
    )(parity, mine, other, start, feats)
    return basis.T, modes


def solution(mesh):
    return jax.shard_map(
        on_device,
        mesh=mesh,
        in_specs=(P("grp", "row", "col"), P(), P()),
        out_specs=(P("grp", None), P(("grp", "row"), "col", None)),
        check_vma=False,
    )
```

time: 57.1 us -> 47.6 us (0.83)
  Pallas kernels: 24.4 us -> 13.9 us
  local copies, waits for them, and re-layouts: 1 us -> 3.48 us
  other arithmetic: 1.73 us -> 0.19 us
    pallas_call x5 -> x6, Pallas kernels: 24.4 us -> 13.9 us  [the longest x1 6.85 us: on_device(): call(kernel, [((MODES, FRAMES), F32), ((ROWS // 4, COLS // 4, ORIENT * MO...]
    unnamed x8 -> x11, local copies, waits for them, and re-layouts: 0.11 us -> 3.3 us
    select_n x1 -> x0, other arithmetic: 1.53 us -> none  [on_device(): jnp.where(even_row, first, last)]
    pallas_call x1 -> x0, local copies, waits for them, and re-layouts: 0.71 us -> none  [on_device(): call(kernel, [((FRAMES, MODES), F32), ((ROWS // 4, COLS // 4, ORIENT * MO...]
  transfers between devices with their start and end apart: 9 -> 9, of which waited for: 5 -> 5; matrix products, arithmetic and copies ran while one was open for 1% -> 2% of each run, Pallas kernels for 13% -> 6%
where the time goes in v2:
time: 47.6 us; the launch traced here: 47.3 us
  starting transfers between devices  18 us (38%)
  Pallas kernels  13.9 us (29%)
  waiting for transfers between devices  11 us (23%)
  local copies, waits for them, and re-layouts  3.48 us (7%)
  between operations  0.77 us (2%)
    ppermute x3, waiting for transfers between devices, on_device(): mine = mine + lax.ppermute(mine, axis, [(i, i ^ step) for i in range(size)])  8.85 us
    ppermute x3, starting transfers between devices, on_device(): mine = mine + lax.ppermute(mine, axis, [(i, i ^ step) for i in range(size)])  7.39 us
    pallas_call x1, Pallas kernels, on_device(): call(kernel, [((MODES, FRAMES), F32), ((ROWS // 4, COLS // 4, ORIENT * MO...  6.85 us
    ppermute x1, starting transfers between devices, on_device(): mine = mine + lax.ppermute(other, 'row', pairs(size_row, 0))  6.06 us
    unnamed x11, local copies, waits for them, and re-layouts  3.3 us
    pallas_call x1, Pallas kernels, on_device(): inner, = call(inner_kernel, [feats_shape], 0, 2)(band, x)  2.76 us
    ppermute x1, starting transfers between devices, on_device(): got_a = lax.ppermute(edge_a, 'col', pairs(size_col, 0))  2.6 us
    pallas_call x1, Pallas kernels, on_device(): call(halo_kernel, [tile, edge, edge], 1, 5)(parity, got_a, got_b, x, rim)  1.53 us
  transfers between devices with their start and end apart: 9, of which 5 were waited for; matrix products, arithmetic and copies ran while one was open for 2% of the time, Pallas kernels for 6%

profile of v2, /device:TPU:0, one launch (start us, length us, event | category | flops | bytes accessed | tf_op | source)
XLA Modules:
  0.0 47.3 jit_solution(3167362412465161546)
XLA Ops:
  0.6 0.1 pad_add_fusion.parity_ref
  0.7 0.0 copy-start
  0.7 1.0 %copy-done = bf16[257,8,128]{2,1,0:T(8,128)(2,1)S(1)} copy-done((bf16[257,8,128]{2,1,0:T(8,128)(2,1)S(1)}, bf16[257,8,128]{2,1,0:T(8,128)(2,1)}, u32[]{:S(2)}) %copy-start) | copy-done | bytes 526360
  1.8 0.0 copy-start.2
  1.8 1.2 %shard_map.51 = (bf16[400,256]{1,0:T(8,128)(2,1)S(1)}, bf16[400,256]{1,0:T(8,128)(2,1)S(1)}, bf16[16,112,384]{2,1,0:T(8,128)(2,1)S(1)}, f32[2,128,384]{2,1,0:T(8,128)S(1)}) custom-call(s32[2]{0:T(128)S(1)} %pad_add_fusion.parity_ref, bf16[257,8,128]{2,1,0:T(8,128)(2,1)S(1)} %copy-done), custom_call_target="tpu_custom_call" | custom-call | tf_op jit(solution)/shard_map/pallas_call | solution.py:277
  2.9 0.5 %collective-permute-start = (bf16[400,256]{1,0:T(8,128)(2,1)S(1)}, bf16[400,256]{1,0:T(8,128)(2,1)S(1)}, u32[]{:S(2)}, u32[]{:S(2)}) collective-permute-start(bf16[400,256]{1,0:T(8,128)(2,1)S(1)} %get-tuple-element.17), channel_id=1, source_target_pairs={{0,4},{4,0},{8,12},{12,8},{1,5},{5,1},{9,13},{13,9},{2,6},{6,2},{1... | collective-permute-start | bytes 614408 | tf_op jit(solution)/shard_map/ppermute | solution.py:278
  3.5 0.0 copy-done.2
  3.5 0.7 %collective-permute-start.1 = (bf16[400,256]{1,0:T(8,128)(2,1)S(1)}, bf16[400,256]{1,0:T(8,128)(2,1)S(1)}, u32[]{:S(2)}, u32[]{:S(2)}) collective-permute-start(bf16[400,256]{1,0:T(8,128)(2,1)S(1)} %get-tuple-element.18), channel_id=1, source_target_pairs={{4,8},{8,4},{5,9},{9,5},{6,10},{10,6},{7,11},{11,7},{20,24},{24,20... | collective-permute-start | bytes 614408 | tf_op jit(solution)/shard_map/ppermute | solution.py:279
  4.1 0.8 %copy.7 = f32[4,2,7,7]{3,2,1,0:T(8,128)S(1)} copy(f32[4,2,7,7]{3,1,2,0:T(2,128)} %param.4) | data formatting | bytes 3136
  4.9 0.1 reshape.20
  5.0 0.0 collective-permute-done.a_ref
  5.0 0.0 collective-permute-done.1.b_ref
  5.0 0.0 copy-start.3
  5.0 0.6 %copy-done.3 = s32[2]{0:T(128)S(1)} copy-done((s32[2]{0:T(128)S(1)}, s32[2]{0:T(128)}, u32[]{:S(2)}) %copy-start.3) | copy-done | bytes 32
  5.7 1.5 %shard_map.52 = (bf16[16,112,384]{2,1,0:T(8,128)(2,1)S(1)}, bf16[112,384]{1,0:T(8,128)(2,1)}, bf16[112,384]{1,0:T(8,128)(2,1)}) custom-call(s32[2]{0:T(128)S(1)} %copy-done.3, bf16[400,256]{1,0:T(8,128)(2,1)S(1)} %collective-permute-done.a_ref, bf16[400,256]{1,0:T(8,128)(2,1)S(1)} %collective-permute-done.1.b_ref, ...), custom_call_target="tpu_custom_call" | custom-call | tf_op jit(solution)/shard_map/pallas_call | solution.py:287
  7.2 0.0 copy-start.4
  7.2 2.6 %collective-permute-start.2 = (bf16[112,384]{1,0:T(8,128)(2,1)}, bf16[112,384]{1,0:T(8,128)(2,1)S(1)}, u32[]{:S(2)}, u32[]{:S(2)}) collective-permute-start(bf16[112,384]{1,0:T(8,128)(2,1)} %get-tuple-element.22), channel_id=1, source_target_pairs={{0,1},{1,0},{2,3},{3,2},{4,5},{5,4},{6,7},{7,6},{8,9},{9,8},{10,11... | collective-permute-start | bytes 258056 | tf_op jit(solution)/shard_map/ppermute | solution.py:288
  9.8 0.7 %collective-permute-start.3 = (bf16[112,384]{1,0:T(8,128)(2,1)}, bf16[112,384]{1,0:T(8,128)(2,1)S(1)}, u32[]{:S(2)}, u32[]{:S(2)}) collective-permute-start(bf16[112,384]{1,0:T(8,128)(2,1)} %get-tuple-element.23), channel_id=1, source_target_pairs={{1,2},{2,1},{5,6},{6,5},{9,10},{10,9},{13,14},{14,13},{17,18},{18,... | collective-permute-start | bytes 258056 | tf_op jit(solution)/shard_map/ppermute | solution.py:289
  10.5 0.1 broadcast_multiply_fusion
  10.6 0.1 mul.20.taps_ref
  10.7 0.0 copy-start.1
  10.7 0.8 %copy-done.1 = f32[256,64]{0,1:T(8,128)S(1)} copy-done((f32[256,64]{0,1:T(8,128)S(1)}, f32[256,64]{0,1:T(8,128)}, u32[]{:S(2)}) %copy-start.1) | copy-done | bytes 65560
  11.5 0.3 shard_map.50
  11.8 2.8 %shard_map.53.inner_ref = bf16[16,16,256]{2,1,0:T(8,128)(2,1)S(1)} custom-call(bf16[128,256]{1,0:T(8,128)(2,1)S(1)} %get-tuple-element.16.band_ref, bf16[16,112,384]{2,1,0:T(8,128)(2,1)S(1)} %get-tuple-element.21.x_ref), custom_call_target="tpu_custom_call" | custom-call | tf_op jit(solution)/shard_map/pallas_call | solution.py:291
  14.6 0.0 collective-permute-done.2.a_ref
  14.6 0.0 collective-permute-done.3.b_ref
  14.6 0.0 copy-done.4
  14.6 1.2 %shard_map.54 = (bf16[16,16,256]{2,1,0:T(8,128)(2,1)S(1)}, f32[136,128]{1,0:T(8,128)S(1)}, f32[136,128]{1,0:T(8,128)S(1)}) custom-call(s32[2]{0:T(128)S(1)} %copy-done.4, bf16[128,256]{1,0:T(8,128)(2,1)S(1)} %get-tuple-element.16.band_ref, bf16[16,112,384]{2,1,0:T(8,128)(2,1)S(1)} %get-tuple-element.21.x_ref, ...), custom_call_target="tpu_custom_call" | custom-call | tf_op jit(solution)/shard_map/pallas_call | solution.py:293
  15.8 6.1 %collective-permute-start.4 = (f32[136,128]{1,0:T(8,128)S(1)}, f32[136,128]{1,0:T(8,128)S(1)}, u32[]{:S(2)}, u32[]{:S(2)}) collective-permute-start(f32[136,128]{1,0:T(8,128)S(1)} %get-tuple-element.25), channel_id=1, source_target_pairs={{0,4},{4,0},{8,12},{12,8},{1,5},{5,1},{9,13},{13,9},{2,6},{6,2},{1... | collective-permute-start | bytes 208904 | tf_op jit(solution)/shard_map/ppermute | solution.py:295
  21.9 0.9 %collective-permute-done.4 = f32[136,128]{1,0:T(8,128)S(1)} collective-permute-done((f32[136,128]{1,0:T(8,128)S(1)}, f32[136,128]{1,0:T(8,128)S(1)}, u32[]{:S(2)}, u32[]{:S(2)}) %collective-permute-start.4) | collective-permute-done | bytes 69664 | tf_op jit(solution)/shard_map/ppermute | solution.py:295
  22.8 1.4 %collective-permute-start.5 = (f32[136,128]{1,0:T(8,128)S(1)}, f32[136,128]{1,0:T(8,128)S(1)}, u32[]{:S(2)}, u32[]{:S(2)}) collective-permute-start(f32[136,128]{1,0:T(8,128)S(1)} %add.14), channel_id=1, source_target_pairs={{0,8},{4,12},{8,0},{12,4},{1,9},{5,13},{9,1},{13,5},{2,10},{6,14},... | collective-permute-start | bytes 208904 | tf_op jit(solution)/shard_map/ppermute | solution.py:298
  24.2 3.1 %collective-permute-done.5 = f32[136,128]{1,0:T(8,128)S(1)} collective-permute-done((f32[136,128]{1,0:T(8,128)S(1)}, f32[136,128]{1,0:T(8,128)S(1)}, u32[]{:S(2)}, u32[]{:S(2)}) %collective-permute-start.5) | collective-permute-done | bytes 69664 | tf_op jit(solution)/shard_map/ppermute | solution.py:298
  27.3 4.2 %collective-permute-start.6 = (f32[136,128]{1,0:T(8,128)S(1)}, f32[136,128]{1,0:T(8,128)S(1)}, u32[]{:S(2)}, u32[]{:S(2)}) collective-permute-start(f32[136,128]{1,0:T(8,128)S(1)} %add.15), channel_id=1, source_target_pairs={{0,1},{1,0},{2,3},{3,2},{4,5},{5,4},{6,7},{7,6},{8,9},{9,8},{10,11... | collective-permute-start | bytes 208904 | tf_op jit(solution)/shard_map/ppermute | solution.py:298
  31.5 2.3 %collective-permute-done.6 = f32[136,128]{1,0:T(8,128)S(1)} collective-permute-done((f32[136,128]{1,0:T(8,128)S(1)}, f32[136,128]{1,0:T(8,128)S(1)}, u32[]{:S(2)}, u32[]{:S(2)}) %collective-permute-start.6) | collective-permute-done | bytes 69664 | tf_op jit(solution)/shard_map/ppermute | solution.py:298
  33.8 1.8 %collective-permute-start.7 = (f32[136,128]{1,0:T(8,128)S(1)}, f32[136,128]{1,0:T(8,128)S(1)}, u32[]{:S(2)}, u32[]{:S(2)}) collective-permute-start(f32[136,128]{1,0:T(8,128)S(1)} %add.16), channel_id=1, source_target_pairs={{0,2},{1,3},{2,0},{3,1},{4,6},{5,7},{6,4},{7,5},{8,10},{9,11},{10,... | collective-permute-start | bytes 208904 | tf_op jit(solution)/shard_map/ppermute | solution.py:298
  35.6 3.5 %collective-permute-done.7 = f32[136,128]{1,0:T(8,128)S(1)} collective-permute-done((f32[136,128]{1,0:T(8,128)S(1)}, f32[136,128]{1,0:T(8,128)S(1)}, u32[]{:S(2)}, u32[]{:S(2)}) %collective-permute-start.7) | collective-permute-done | bytes 69664 | tf_op jit(solution)/shard_map/ppermute | solution.py:298
  39.1 0.1 collective-permute-start.8
  39.2 1.2 %collective-permute-done.8.other_ref = f32[136,128]{1,0:T(8,128)S(1)} collective-permute-done((f32[136,128]{1,0:T(8,128)S(1)}, f32[136,128]{1,0:T(8,128)S(1)}, u32[]{:S(2)}, u32[]{:S(2)}) %collective-permute-start.8) | collective-permute-done | bytes 69664 | tf_op jit(solution)/shard_map/ppermute | solution.py:300
  40.4 6.9 %shard_map.55 = (f32[64,256]{1,0:T(8,128)}, f32[2,32,256]{2,1,0:T(8,128)}) custom-call(s32[2]{0:T(128)S(1)} %copy-done.4, f32[136,128]{1,0:T(8,128)S(1)} %add.17.mine_ref, f32[136,128]{1,0:T(8,128)S(1)} %collective-permute-done.8.other_ref, f32[64,256]{1,0:T(8,128)S(1)} %get-tuple-element.26.start_ref, bf16[16,16,256]{2,1,0:T(8,128)(2,1)S(1)} %get-tuple-element.27.feats_ref), custom_call_target="tpu_custom_call" | custom-call | tf_op jit(solution)/shard_map/pallas_call | solution.py:304
  (7 shorter events, 0.1 us)
Async XLA Ops:
  0.7 1.0 %copy-start = (bf16[257,8,128]{2,1,0:T(8,128)(2,1)S(1)}, bf16[257,8,128]{2,1,0:T(8,128)(2,1)}, u32[]{:S(2)}) copy-start(bf16[257,8,128]{2,1,0:T(8,128)(2,1)} %video_ref.1) | copy-start | bytes 1579012
  1.8 1.7 %copy-start.2 = (s32[2]{0:T(128)}, s32[2]{0:T(128)S(1)}, u32[]{:S(2)}) copy-start(s32[2]{0:T(128)S(1)} %pad_add_fusion.parity_ref) | copy-start | bytes 28
  2.9 2.1 %collective-permute-start = (bf16[400,256]{1,0:T(8,128)(2,1)S(1)}, bf16[400,256]{1,0:T(8,128)(2,1)S(1)}, u32[]{:S(2)}, u32[]{:S(2)}) collective-permute-start(bf16[400,256]{1,0:T(8,128)(2,1)S(1)} %get-tuple-element.17), channel_id=1, source_target_pairs={{0,4},{4,0},{8,12},{12,8},{1,5},{5,1},{9,13},{13,9},{2,6},{6,2},{1... | collective-permute-start | bytes 614408 | tf_op jit(solution)/shard_map/ppermute | solution.py:278
  3.5 1.6 %collective-permute-start.1 = (bf16[400,256]{1,0:T(8,128)(2,1)S(1)}, bf16[400,256]{1,0:T(8,128)(2,1)S(1)}, u32[]{:S(2)}, u32[]{:S(2)}) collective-permute-start(bf16[400,256]{1,0:T(8,128)(2,1)S(1)} %get-tuple-element.18), channel_id=1, source_target_pairs={{4,8},{8,4},{5,9},{9,5},{6,10},{10,6},{7,11},{11,7},{20,24},{24,20... | collective-permute-start | bytes 614408 | tf_op jit(solution)/shard_map/ppermute | solution.py:279
  5.0 0.7 %copy-start.3 = (s32[2]{0:T(128)S(1)}, s32[2]{0:T(128)}, u32[]{:S(2)}) copy-start(s32[2]{0:T(128)} %copy-done.2) | copy-start | bytes 28
  7.2 7.4 %copy-start.4 = (s32[2]{0:T(128)S(1)}, s32[2]{0:T(128)}, u32[]{:S(2)}) copy-start(s32[2]{0:T(128)} %copy-done.2) | copy-start | bytes 28
  7.2 7.3 %collective-permute-start.2 = (bf16[112,384]{1,0:T(8,128)(2,1)}, bf16[112,384]{1,0:T(8,128)(2,1)S(1)}, u32[]{:S(2)}, u32[]{:S(2)}) collective-permute-start(bf16[112,384]{1,0:T(8,128)(2,1)} %get-tuple-element.22), channel_id=1, source_target_pairs={{0,1},{1,0},{2,3},{3,2},{4,5},{5,4},{6,7},{7,6},{8,9},{9,8},{10,11... | collective-permute-start | bytes 258056 | tf_op jit(solution)/shard_map/ppermute | solution.py:288
  9.8 4.7 %collective-permute-start.3 = (bf16[112,384]{1,0:T(8,128)(2,1)}, bf16[112,384]{1,0:T(8,128)(2,1)S(1)}, u32[]{:S(2)}, u32[]{:S(2)}) collective-permute-start(bf16[112,384]{1,0:T(8,128)(2,1)} %get-tuple-element.23), channel_id=1, source_target_pairs={{1,2},{2,1},{5,6},{6,5},{9,10},{10,9},{13,14},{14,13},{17,18},{18,... | collective-permute-start | bytes 258056 | tf_op jit(solution)/shard_map/ppermute | solution.py:289
  10.7 0.8 %copy-start.1 = (f32[256,64]{0,1:T(8,128)S(1)}, f32[256,64]{0,1:T(8,128)}, u32[]{:S(2)}) copy-start(f32[256,64]{0,1:T(8,128)} %param.5) | copy-start | bytes 196612
  15.8 7.0 %collective-permute-start.4 = (f32[136,128]{1,0:T(8,128)S(1)}, f32[136,128]{1,0:T(8,128)S(1)}, u32[]{:S(2)}, u32[]{:S(2)}) collective-permute-start(f32[136,128]{1,0:T(8,128)S(1)} %get-tuple-element.25), channel_id=1, source_target_pairs={{0,4},{4,0},{8,12},{12,8},{1,5},{5,1},{9,13},{13,9},{2,6},{6,2},{1... | collective-permute-start | bytes 208904 | tf_op jit(solution)/shard_map/ppermute | solution.py:295
  22.8 4.5 %collective-permute-start.5 = (f32[136,128]{1,0:T(8,128)S(1)}, f32[136,128]{1,0:T(8,128)S(1)}, u32[]{:S(2)}, u32[]{:S(2)}) collective-permute-start(f32[136,128]{1,0:T(8,128)S(1)} %add.14), channel_id=1, source_target_pairs={{0,8},{4,12},{8,0},{12,4},{1,9},{5,13},{9,1},{13,5},{2,10},{6,14},... | collective-permute-start | bytes 208904 | tf_op jit(solution)/shard_map/ppermute | solution.py:298
  27.3 6.5 %collective-permute-start.6 = (f32[136,128]{1,0:T(8,128)S(1)}, f32[136,128]{1,0:T(8,128)S(1)}, u32[]{:S(2)}, u32[]{:S(2)}) collective-permute-start(f32[136,128]{1,0:T(8,128)S(1)} %add.15), channel_id=1, source_target_pairs={{0,1},{1,0},{2,3},{3,2},{4,5},{5,4},{6,7},{7,6},{8,9},{9,8},{10,11... | collective-permute-start | bytes 208904 | tf_op jit(solution)/shard_map/ppermute | solution.py:298
  33.8 5.3 %collective-permute-start.7 = (f32[136,128]{1,0:T(8,128)S(1)}, f32[136,128]{1,0:T(8,128)S(1)}, u32[]{:S(2)}, u32[]{:S(2)}) collective-permute-start(f32[136,128]{1,0:T(8,128)S(1)} %add.16), channel_id=1, source_target_pairs={{0,2},{1,3},{2,0},{3,1},{4,6},{5,7},{6,4},{7,5},{8,10},{9,11},{10,... | collective-permute-start | bytes 208904 | tf_op jit(solution)/shard_map/ppermute | solution.py:298
  39.1 1.3 %collective-permute-start.8 = (f32[136,128]{1,0:T(8,128)S(1)}, f32[136,128]{1,0:T(8,128)S(1)}, u32[]{:S(2)}, u32[]{:S(2)}) collective-permute-start(f32[136,128]{1,0:T(8,128)S(1)} %add.17.mine_ref), channel_id=1, source_target_pairs={{0,4},{4,0},{8,12},{12,8},{1,5},{5,1},{9,13},{13,9},{2,6},{6,2},{1... | collective-permute-start | bytes 208904 | tf_op jit(solution)/shard_map/ppermute | solution.py:300

commit v3 on v2

--- a/solution.py
+++ b/solution.py
@@ -20,9 +20,8 @@
 F32 = jnp.float32
 BF16 = jnp.bfloat16
 HIGHEST = lax.Precision.HIGHEST
-PARAMS = pltpu.CompilerParams(vmem_limit_bytes=48 * 1024 * 1024)
+PARAMS = pltpu.CompilerParams(vmem_limit_bytes=24 * 1024 * 1024)
 VMEM = pl.BlockSpec(memory_space=pltpu.VMEM)
-SMEM = pl.BlockSpec(memory_space=pltpu.SMEM)
 
 
 def turned(rows_ref, row, group):
@@ -34,18 +33,29 @@
     return jnp.concatenate(both, axis=1).astype(BF16)
 
 
-def own_kernel(parity_ref, video_ref, send_a_ref, send_b_ref, x_ref, rim_ref, rows_ref):
-    even = parity_ref[0] == 0
+def is_even(axis):
+    return (lax.axis_index(axis) & 1) == 0
+
+
+def own_kernel(video_ref, side_a_ref, side_b_ref, send_a_ref, send_b_ref, x_ref, rim_ref, rows_ref):
+    even_row, even_col = is_even("row"), is_even("col")
     rows_ref[...] = video_ref[...].astype(F32).reshape(rows_ref.shape)
     for group in range(3):
         lanes = slice(HALF * group, HALF * group + HALF)
         tiles = [turned(rows_ref, row, group) for row in range(ROWS)]
+        for pair in range(ROWS // 2):
+            both = tiles[2 * pair : 2 * pair + 2]
+            left = jnp.concatenate([tile[:8] for tile in both], axis=0)
+            right = jnp.concatenate([tile[COLS - 8 :] for tile in both], axis=0)
+            at = slice(16 * pair, 16 * pair + 16)
+            side_a_ref[at, lanes] = jnp.where(even_col, right, left).astype(BF16)
+            side_b_ref[at, lanes] = jnp.where(even_col, left, right).astype(BF16)
         if group < 2:
             for i in range(REACH):
                 first, last = tiles[i], tiles[ROWS - REACH + i]
                 at = slice(COLS * i, COLS * i + COLS)
-                send_a_ref[at, lanes] = jnp.where(even, last, first).astype(BF16)
-                send_b_ref[at, lanes] = jnp.where(even, first, last).astype(BF16)
+                send_a_ref[at, lanes] = jnp.where(even_row, last, first).astype(BF16)
+                send_b_ref[at, lanes] = jnp.where(even_row, first, last).astype(BF16)
         for pair in range(3):
             x_ref[:, 32 + 16 * pair : 48 + 16 * pair, lanes] = blocked(tiles[2 * pair + 1], tiles[2 * pair + 2])
         rim_ref[0, :, lanes] = tiles[0]
@@ -53,10 +63,20 @@
     final = rows_ref[FRAMES * ROWS : FRAMES * ROWS + ROWS, :]
     shifted = pltpu.roll(final, REACH, 0)
     fill = jnp.zeros((8, COLS), F32)
-    for ref, chosen in ((send_a_ref, jnp.where(even, shifted, final)), (send_b_ref, jnp.where(even, final, shifted))):
-        tail = jnp.concatenate([chosen, fill], axis=0).astype(BF16)
-        ref[REACH * COLS : REACH * COLS + 16, 0:COLS] = tail
-        ref[REACH * COLS : REACH * COLS + 16, COLS : 2 * COLS] = tail
+    first, last = (jnp.concatenate([part, fill], axis=0).astype(BF16) for part in (final, shifted))
+    for ref, chosen in ((send_a_ref, jnp.where(even_row, last, first)), (send_b_ref, jnp.where(even_row, first, last))):
+        ref[REACH * COLS : REACH * COLS + 16, 0:COLS] = chosen
+        ref[REACH * COLS : REACH * COLS + 16, COLS : 2 * COLS] = chosen
+
+
+def corner_kernel(a_ref, b_ref, band_ref, send_a_ref, send_b_ref):
+    even_row, even_col = is_even("row"), is_even("col")
+    got_a, got_b = a_ref[...], b_ref[...]
+    for side, got in enumerate((jnp.where(even_col, got_b, got_a), jnp.where(even_col, got_a, got_b))):
+        got = got.astype(F32)
+        first, last = got[: 8 * REACH], got[8 * (ROWS - REACH) :]
+        send_a_ref[side] = jnp.where(even_row, last, first)
+        send_b_ref[side] = jnp.where(even_row, first, last)
 
 
 def band_kernel(taps_ref, start_ref, band_ref, basis_ref):
@@ -86,8 +106,8 @@
     return jnp.where(frame == 2 * (lane & (HALF - 1)) + (lane >> 7), 1.0, 0.0).astype(F32)
 
 
-def halo_kernel(parity_ref, a_ref, b_ref, x_in_ref, rim_ref, x_ref, edge_a_ref, edge_b_ref):
-    even = parity_ref[0] == 0
+def halo_kernel(a_ref, b_ref, x_in_ref, rim_ref, x_ref):
+    even = is_even("row")
     got_a, got_b = a_ref[...], b_ref[...]
     final = lax.broadcasted_iota(jnp.int32, (COLS, HALF), 1) == HALF - 1
     sides = []
@@ -108,8 +128,6 @@
         x_ref[:, 80:96, lanes] = blocked(rim_ref[1, :, lanes], below[0][group])
         x_ref[:, 96:112, lanes] = blocked(below[1][group], below[2][group])
     x_ref[:, 32:80, :] = x_in_ref[:, 32:80, :]
-    edge_a_ref[...] = x_ref[(BLOCKS - 1) * (1 - parity_ref[1])]
-    edge_b_ref[...] = x_ref[(BLOCKS - 1) * parity_ref[1]]
 
 
 def block_feats(band_ref, left, right):
@@ -150,12 +168,16 @@
     lax.fori_loop(0, (BLOCKS - 1) // 3, body, 0)
 
 
-def edge_kernel(parity_ref, band_ref, x_ref, a_ref, b_ref, inner_ref, feats_ref, mine_ref, other_ref):
-    even = parity_ref[1] == 0
-    got_a = a_ref[...]
-    got_b = b_ref[...]
-    right = jnp.where(even, got_a, got_b)
-    left = jnp.where(even, got_b, got_a)
+def edge_kernel(band_ref, x_ref, side_a_ref, side_b_ref, a_ref, b_ref, inner_ref, feats_ref, mine_ref, other_ref):
+    even_row, even_col = is_even("row"), is_even("col")
+    side_a, side_b = side_a_ref[...], side_b_ref[...]
+    blocks = []
+    for side, got in enumerate((jnp.where(even_col, side_b, side_a), jnp.where(even_col, side_a, side_b))):
+        got_a, got_b = a_ref[side], b_ref[side]
+        above = jnp.where(even_row, got_b, got_a)
+        below = jnp.where(even_row, got_a, got_b)
+        blocks.append(jnp.concatenate([above, got.astype(F32), below], axis=0).astype(BF16))
+    left, right = blocks
     feats_left = block_feats(band_ref, left, x_ref[0])
     feats_right = block_feats(band_ref, x_ref[BLOCKS - 1], right)
     second = (lax.broadcasted_iota(jnp.int32, (16, FRAMES), 0) & 4) == 4
@@ -168,7 +190,7 @@
     j = lax.broadcasted_iota(jnp.int32, (HALF, HALF), 1)
     folded = jnp.where(i <= j, top, low)
     diagonal = jnp.sum(jnp.where(i == j, low, 0.0), axis=0, keepdims=True)
-    first = parity_ref[0] == 0
+    first = is_even("row")
     spare = jnp.broadcast_to(diagonal, (8, HALF))
     mine_ref[0:HALF] = jnp.where(first, cross, folded)
     mine_ref[HALF : HALF + 8] = spare
@@ -205,8 +227,8 @@
     return jnp.concatenate(done, axis=0)[:, :MODES]
 
 
-def basis_kernel(scale, parity_ref, mine_ref, other_ref, start_ref, feats_ref, basis_ref, modes_ref, rows_ref, out_ref):
-    first = parity_ref[0] == 0
+def basis_kernel(scale, mine_ref, other_ref, start_ref, feats_ref, basis_ref, modes_ref, rows_ref, out_ref):
+    first = is_even("row")
     mine, other = mine_ref[...], other_ref[...]
     cross = jnp.where(first, mine, other)[:HALF]
     second = jnp.where(first, other, mine)
@@ -247,14 +269,13 @@
             modes_ref[row, :, 128 * half : 128 * half + 128] = out_ref[64 * row + 32 * half : 64 * row + 32 * half + 32]
 
 
-def call(kernel, outs, n_smem, n_in, scratch=(), aliases={}):
+def call(kernel, outs, n_in, scratch=()):
     return pl.pallas_call(
         kernel,
         out_shape=[jax.ShapeDtypeStruct(shape, dtype) for shape, dtype in outs],
-        in_specs=[SMEM] * n_smem + [VMEM] * (n_in - n_smem),
+        in_specs=[VMEM] * n_in,
         out_specs=[VMEM] * len(outs),
         scratch_shapes=list(scratch),
-        input_output_aliases=aliases,
         compiler_params=PARAMS,
     )
 
@@ -266,31 +287,38 @@
     return swaps
 
 
+def swap(axis, a, b):
+    size = lax.axis_size(axis)
+    return lax.ppermute(a, axis, pairs(size, 0)), lax.ppermute(b, axis, pairs(size, 1))
+
+
 def on_device(video, filters, start_basis):
     size_row, size_col = lax.axis_size("row"), lax.axis_size("col")
-    parity = jnp.stack([lax.axis_index("row") & 1, lax.axis_index("col") & 1]).astype(jnp.int32)
-
-    rows = pltpu.VMEM(((FRAMES + 1) * ROWS, COLS), F32)
+    swap_row, swap_col = (functools.partial(swap, axis) for axis in ("row", "col"))
+
+    side = ((8 * ROWS, 3 * HALF), BF16)
     send = ((REACH * COLS + 16, FRAMES), BF16)
     tile = ((BLOCKS, 112, 3 * HALF), BF16)
     rim = ((2, COLS, 3 * HALF), F32)
-    send_a, send_b, x, rim = call(own_kernel, [send, send, tile, rim], 1, 2, [rows])(parity, video)
-    got_a = lax.ppermute(send_a, "row", pairs(size_row, 0))
-    got_b = lax.ppermute(send_b, "row", pairs(size_row, 1))
+    rows = pltpu.VMEM(((FRAMES + 1) * ROWS, COLS), F32)
+    side_a, side_b, send_a, send_b, x, rim = call(own_kernel, [side, side, send, send, tile, rim], 1, [rows])(video)
+    side_a, side_b = swap_col(side_a, side_b)
+    got_a, got_b = swap_row(send_a, send_b)
 
     taps = jnp.pad(filters, ((0, 0), (0, 0), (0, 1), (0, 1))).reshape(ORIENT, 2, 64)
     taps = jnp.transpose(taps, (1, 0, 2))[:, None, :, None, :] * jnp.eye(2, dtype=F32)[None, :, None, :, None]
-    band, start = call(band_kernel, [((128, 256), BF16), ((MODES, FRAMES), F32)], 0, 2)(
+    band, start = call(band_kernel, [((128, 256), BF16), ((MODES, FRAMES), F32)], 2)(
         taps.reshape(16, 128), start_basis.T
     )
-    edge = ((112, 3 * HALF), BF16)
-    x, edge_a, edge_b = call(halo_kernel, [tile, edge, edge], 1, 5)(parity, got_a, got_b, x, rim)
-    got_a = lax.ppermute(edge_a, "col", pairs(size_col, 0))
-    got_b = lax.ppermute(edge_b, "col", pairs(size_col, 1))
+    corner = ((2, 8 * REACH, 3 * HALF), F32)
+    corner_a, corner_b = swap_row(*call(corner_kernel, [corner, corner], 3)(side_a, side_b, band))
+    (x,) = call(halo_kernel, [tile], 4)(got_a, got_b, x, rim)
     feats_shape = ((BLOCKS, 16, FRAMES), BF16)
-    (inner,) = call(inner_kernel, [feats_shape], 0, 2)(band, x)
+    (inner,) = call(inner_kernel, [feats_shape], 2)(band, x)
     part = ((HALF + 8, HALF), F32)
-    feats, mine, other = call(edge_kernel, [feats_shape, part, part], 1, 6)(parity, band, x, got_a, got_b, inner)
+    feats, mine, other = call(edge_kernel, [feats_shape, part, part], 7)(
+        band, x, side_a, side_b, corner_a, corner_b, inner
+    )
 
     mine = mine + lax.ppermute(other, "row", pairs(size_row, 0))
     for axis, size, step in (("row", size_row, 2), ("col", size_col, 1)):
@@ -304,10 +332,9 @@
     basis, modes = call(
         kernel,
         [((MODES, FRAMES), F32), ((ROWS // 4, COLS // 4, ORIENT * MODES), F32)],
-        1,
-        5,
+        4,
         [pltpu.VMEM((FRAMES, 2 * MODES), F32), pltpu.VMEM((128, 128), F32)],
-    )(parity, mine, other, start, feats)
+    )(mine, other, start, feats)
     return basis.T, modes
 
 

time: 47.6 us -> 44.2 us (0.929)
  Pallas kernels: 13.9 us -> 11 us
  starting transfers between devices: 18 us -> 19 us
  waiting for transfers between devices: 11 us -> 10.1 us
  local copies, waits for them, and re-layouts: 3.48 us -> 2.81 us
    ppermute x1, starting transfers between devices: 6.06 us -> 2.23 us  [on_device(): mine = mine + lax.ppermute(other, 'row', pairs(size_row, 0))]
    ppermute x4 -> x6, starting transfers between devices: 4.44 us -> 7.77 us  [the longest x3 5.8 us: swap(): lax.ppermute(a, axis, pairs(size, 0))]
    pallas_call x5 -> x6, Pallas kernels: 7 us -> 4.71 us  [the longest x1 2.75 us: on_device(): inner, = call(inner_kernel, [feats_shape], 2)(band, x)]
    ppermute x3, starting transfers between devices: 7.39 us -> 8.97 us  [on_device(): mine = mine + lax.ppermute(mine, axis, [(i, i ^ step) for i in range(size)])]
    ppermute x3, waiting for transfers between devices: 8.85 us -> 7.94 us  [on_device(): mine = mine + lax.ppermute(mine, axis, [(i, i ^ step) for i in range(size)])]
    unnamed x11 -> x5, local copies, waits for them, and re-layouts: 3.3 us -> 2.63 us
    pallas_call x1, Pallas kernels: 6.85 us -> 6.32 us  [on_device(): call(kernel, [((MODES, FRAMES), F32), ((ROWS // 4, COLS // 4, ORIENT * MO...]
  transfers between devices with their start and end apart: 9 -> 11, of which waited for: 5 -> 5; matrix products, arithmetic and copies ran while one was open for 2% -> 2% of each run, Pallas kernels for 6% -> 8%
where the time goes in v3:
time: 44.2 us; the launch traced here: 43.9 us
  starting transfers between devices  19 us (43%)
  Pallas kernels  11 us (25%)
  waiting for transfers between devices  10.1 us (23%)
  local copies, waits for them, and re-layouts  2.81 us (6%)
  between operations  0.78 us (2%)
    ppermute x3, starting transfers between devices, on_device(): mine = mine + lax.ppermute(mine, axis, [(i, i ^ step) for i in range(size)])  8.97 us
    ppermute x3, waiting for transfers between devices, on_device(): mine = mine + lax.ppermute(mine, axis, [(i, i ^ step) for i in range(size)])  7.94 us
    pallas_call x1, Pallas kernels, on_device(): call(kernel, [((MODES, FRAMES), F32), ((ROWS // 4, COLS // 4, ORIENT * MO...  6.32 us
    ppermute x3, starting transfers between devices, swap(): lax.ppermute(a, axis, pairs(size, 0))  5.8 us
    pallas_call x1, Pallas kernels, on_device(): inner, = call(inner_kernel, [feats_shape], 2)(band, x)  2.75 us
    unnamed x5, local copies, waits for them, and re-layouts  2.63 us
    ppermute x1, starting transfers between devices, on_device(): mine = mine + lax.ppermute(other, 'row', pairs(size_row, 0))  2.23 us
    ppermute x3, starting transfers between devices, swap(): lax.ppermute(b, axis, pairs(size, 1))  1.97 us
  transfers between devices with their start and end apart: 11, of which 5 were waited for; matrix products, arithmetic and copies ran while one was open for 2% of the time, Pallas kernels for 8%

profile of v3, /device:TPU:0, one launch (start us, length us, event | category | flops | bytes accessed | tf_op | source)
XLA Modules:
  0.0 43.9 jit_solution(15683186324427234418)
XLA Ops:
  0.6 0.0 copy-start
  0.6 1.0 %copy-done = bf16[257,8,128]{2,1,0:T(8,128)(2,1)S(1)} copy-done((bf16[257,8,128]{2,1,0:T(8,128)(2,1)S(1)}, bf16[257,8,128]{2,1,0:T(8,128)(2,1)}, u32[]{:S(2)}) %copy-start) | copy-done | bytes 526360
  1.7 0.7 %shard_map.51 = (bf16[64,384]{1,0:T(8,128)(2,1)S(1)}, bf16[64,384]{1,0:T(8,128)(2,1)S(1)}, bf16[400,256]{1,0:T(8,128)(2,1)S(1)}, bf16[400,256]{1,0:T(8,128)(2,1)...) custom-call(bf16[257,8,128]{2,1,0:T(8,128)(2,1)S(1)} %copy-done), custom_call_target="tpu_custom_call" | custom-call | tf_op jit(solution)/shard_map/pallas_call | solution.py:304
  2.3 0.5 %collective-permute-start = (bf16[400,256]{1,0:T(8,128)(2,1)S(1)}, bf16[400,256]{1,0:T(8,128)(2,1)S(1)}, u32[]{:S(2)}, u32[]{:S(2)}) collective-permute-start(bf16[400,256]{1,0:T(8,128)(2,1)S(1)} %get-tuple-element.18), channel_id=1, source_target_pairs={{0,4},{4,0},{8,12},{12,8},{1,5},{5,1},{9,13},{13,9},{2,6},{6,2},{1... | collective-permute-start | bytes 614408 | tf_op jit(solution)/shard_map/ppermute | solution.py:292
  2.8 0.7 %collective-permute-start.1 = (bf16[400,256]{1,0:T(8,128)(2,1)S(1)}, bf16[400,256]{1,0:T(8,128)(2,1)S(1)}, u32[]{:S(2)}, u32[]{:S(2)}) collective-permute-start(bf16[400,256]{1,0:T(8,128)(2,1)S(1)} %get-tuple-element.19), channel_id=1, source_target_pairs={{4,8},{8,4},{5,9},{9,5},{6,10},{10,6},{7,11},{11,7},{20,24},{24,20... | collective-permute-start | bytes 614408 | tf_op jit(solution)/shard_map/ppermute | solution.py:292
  3.5 2.7 %collective-permute-start.2 = (bf16[64,384]{1,0:T(8,128)(2,1)S(1)}, bf16[64,384]{1,0:T(8,128)(2,1)S(1)}, u32[]{:S(2)}, u32[]{:S(2)}) collective-permute-start(bf16[64,384]{1,0:T(8,128)(2,1)S(1)} %get-tuple-element.22), channel_id=1, source_target_pairs={{0,1},{1,0},{2,3},{3,2},{4,5},{5,4},{6,7},{7,6},{8,9},{9,8},{10,11... | collective-permute-start | bytes 147464 | tf_op jit(solution)/shard_map/ppermute | solution.py:292
  6.2 0.7 %collective-permute-start.3 = (bf16[64,384]{1,0:T(8,128)(2,1)S(1)}, bf16[64,384]{1,0:T(8,128)(2,1)S(1)}, u32[]{:S(2)}, u32[]{:S(2)}) collective-permute-start(bf16[64,384]{1,0:T(8,128)(2,1)S(1)} %get-tuple-element.23), channel_id=1, source_target_pairs={{1,2},{2,1},{5,6},{6,5},{9,10},{10,9},{13,14},{14,13},{17,18},{18,... | collective-permute-start | bytes 147464 | tf_op jit(solution)/shard_map/ppermute | solution.py:292
  6.9 0.8 %copy.7 = f32[4,2,7,7]{3,2,1,0:T(8,128)S(1)} copy(f32[4,2,7,7]{3,1,2,0:T(2,128)} %param.4) | data formatting | bytes 3136
  7.6 0.1 reshape.20
  7.7 0.1 broadcast_multiply_fusion
  7.8 0.1 mul.20.taps_ref
  7.9 0.0 copy-start.1
  7.9 0.8 %copy-done.1 = f32[256,64]{0,1:T(8,128)S(1)} copy-done((f32[256,64]{0,1:T(8,128)S(1)}, f32[256,64]{0,1:T(8,128)}, u32[]{:S(2)}) %copy-start.1) | copy-done | bytes 65560
  8.7 0.3 shard_map.50
  9.0 0.0 collective-permute-done.2.a_ref.side_a_ref
  9.0 0.0 collective-permute-done.3.b_ref.side_b_ref
  9.1 2.6 %collective-permute-start.4 = (f32[2,24,384]{2,1,0:T(8,128)S(1)}, f32[2,24,384]{2,1,0:T(8,128)S(1)}, u32[]{:S(2)}, u32[]{:S(2)}) collective-permute-start(f32[2,24,384]{2,1,0:T(8,128)S(1)} %get-tuple-element.24), channel_id=1, source_target_pairs={{0,4},{4,0},{8,12},{12,8},{1,5},{5,1},{9,13},{13,9},{2,6},{6,2},{1... | collective-permute-start | bytes 221192 | tf_op jit(solution)/shard_map/ppermute | solution.py:292
  11.7 0.7 %collective-permute-start.5 = (f32[2,24,384]{2,1,0:T(8,128)S(1)}, f32[2,24,384]{2,1,0:T(8,128)S(1)}, u32[]{:S(2)}, u32[]{:S(2)}) collective-permute-start(f32[2,24,384]{2,1,0:T(8,128)S(1)} %get-tuple-element.25), channel_id=1, source_target_pairs={{4,8},{8,4},{5,9},{9,5},{6,10},{10,6},{7,11},{11,7},{20,24},{24,20... | collective-permute-start | bytes 221192 | tf_op jit(solution)/shard_map/ppermute | solution.py:292
  12.4 0.0 collective-permute-done.a_ref
  12.4 0.0 collective-permute-done.1.b_ref
  12.4 0.3 shard_map.52.x_ref
  12.7 2.7 %shard_map.54.inner_ref = bf16[16,16,256]{2,1,0:T(8,128)(2,1)S(1)} custom-call(bf16[128,256]{1,0:T(8,128)(2,1)S(1)} %get-tuple-element.17.band_ref, bf16[16,112,384]{2,1,0:T(8,128)(2,1)S(1)} %shard_map.52.x_ref), custom_call_target="tpu_custom_call" | custom-call | tf_op jit(solution)/shard_map/pallas_call | solution.py:317
  15.5 0.0 collective-permute-done.4.a_ref
  15.5 0.0 collective-permute-done.5.b_ref
  15.5 0.7 %shard_map.55 = (bf16[16,16,256]{2,1,0:T(8,128)(2,1)S(1)}, f32[136,128]{1,0:T(8,128)S(1)}, f32[136,128]{1,0:T(8,128)S(1)}) custom-call(bf16[128,256]{1,0:T(8,128)(2,1)S(1)} %get-tuple-element.17.band_ref, bf16[16,112,384]{2,1,0:T(8,128)(2,1)S(1)} %shard_map.52.x_ref, bf16[64,384]{1,0:T(8,128)(2,1)S(1)} %collective-permute-done.2.a_ref.side_a_ref, ...), custom_call_target="tpu_custom_call" | custom-call | tf_op jit(solution)/shard_map/pallas_call | solution.py:319
  16.1 2.2 %collective-permute-start.6 = (f32[136,128]{1,0:T(8,128)S(1)}, f32[136,128]{1,0:T(8,128)S(1)}, u32[]{:S(2)}, u32[]{:S(2)}) collective-permute-start(f32[136,128]{1,0:T(8,128)S(1)} %get-tuple-element.27), channel_id=1, source_target_pairs={{0,4},{4,0},{8,12},{12,8},{1,5},{5,1},{9,13},{13,9},{2,6},{6,2},{1... | collective-permute-start | bytes 208904 | tf_op jit(solution)/shard_map/ppermute | solution.py:323
  18.4 0.9 %collective-permute-done.6 = f32[136,128]{1,0:T(8,128)S(1)} collective-permute-done((f32[136,128]{1,0:T(8,128)S(1)}, f32[136,128]{1,0:T(8,128)S(1)}, u32[]{:S(2)}, u32[]{:S(2)}) %collective-permute-start.6) | collective-permute-done | bytes 69664 | tf_op jit(solution)/shard_map/ppermute | solution.py:323
  19.3 1.1 %collective-permute-start.7 = (f32[136,128]{1,0:T(8,128)S(1)}, f32[136,128]{1,0:T(8,128)S(1)}, u32[]{:S(2)}, u32[]{:S(2)}) collective-permute-start(f32[136,128]{1,0:T(8,128)S(1)} %add.14), channel_id=1, source_target_pairs={{0,8},{4,12},{8,0},{12,4},{1,9},{5,13},{9,1},{13,5},{2,10},{6,14},... | collective-permute-start | bytes 208904 | tf_op jit(solution)/shard_map/ppermute | solution.py:326
  20.4 3.4 %collective-permute-done.7 = f32[136,128]{1,0:T(8,128)S(1)} collective-permute-done((f32[136,128]{1,0:T(8,128)S(1)}, f32[136,128]{1,0:T(8,128)S(1)}, u32[]{:S(2)}, u32[]{:S(2)}) %collective-permute-start.7) | collective-permute-done | bytes 69664 | tf_op jit(solution)/shard_map/ppermute | solution.py:326
  23.8 4.5 %collective-permute-start.8 = (f32[136,128]{1,0:T(8,128)S(1)}, f32[136,128]{1,0:T(8,128)S(1)}, u32[]{:S(2)}, u32[]{:S(2)}) collective-permute-start(f32[136,128]{1,0:T(8,128)S(1)} %add.15), channel_id=1, source_target_pairs={{0,1},{1,0},{2,3},{3,2},{4,5},{5,4},{6,7},{7,6},{8,9},{9,8},{10,11... | collective-permute-start | bytes 208904 | tf_op jit(solution)/shard_map/ppermute | solution.py:326
  28.3 2.3 %collective-permute-done.8 = f32[136,128]{1,0:T(8,128)S(1)} collective-permute-done((f32[136,128]{1,0:T(8,128)S(1)}, f32[136,128]{1,0:T(8,128)S(1)}, u32[]{:S(2)}, u32[]{:S(2)}) %collective-permute-start.8) | collective-permute-done | bytes 69664 | tf_op jit(solution)/shard_map/ppermute | solution.py:326
  30.6 3.4 %collective-permute-start.9 = (f32[136,128]{1,0:T(8,128)S(1)}, f32[136,128]{1,0:T(8,128)S(1)}, u32[]{:S(2)}, u32[]{:S(2)}) collective-permute-start(f32[136,128]{1,0:T(8,128)S(1)} %add.16), channel_id=1, source_target_pairs={{0,2},{1,3},{2,0},{3,1},{4,6},{5,7},{6,4},{7,5},{8,10},{9,11},{10,... | collective-permute-start | bytes 208904 | tf_op jit(solution)/shard_map/ppermute | solution.py:326
  33.9 2.3 %collective-permute-done.9 = f32[136,128]{1,0:T(8,128)S(1)} collective-permute-done((f32[136,128]{1,0:T(8,128)S(1)}, f32[136,128]{1,0:T(8,128)S(1)}, u32[]{:S(2)}, u32[]{:S(2)}) %collective-permute-start.9) | collective-permute-done | bytes 69664 | tf_op jit(solution)/shard_map/ppermute | solution.py:326
  36.3 0.1 collective-permute-start.10
  36.3 1.2 %collective-permute-done.10.other_ref = f32[136,128]{1,0:T(8,128)S(1)} collective-permute-done((f32[136,128]{1,0:T(8,128)S(1)}, f32[136,128]{1,0:T(8,128)S(1)}, u32[]{:S(2)}, u32[]{:S(2)}) %collective-permute-start.10) | collective-permute-done | bytes 69664 | tf_op jit(solution)/shard_map/ppermute | solution.py:328
  37.6 6.3 %shard_map.56 = (f32[64,256]{1,0:T(8,128)}, f32[2,32,256]{2,1,0:T(8,128)}) custom-call(f32[136,128]{1,0:T(8,128)S(1)} %add.17.mine_ref, f32[136,128]{1,0:T(8,128)S(1)} %collective-permute-done.10.other_ref, f32[64,256]{1,0:T(8,128)S(1)} %get-tuple-element.28.start_ref, bf16[16,16,256]{2,1,0:T(8,128)(2,1)S(1)} %get-tuple-element.29.feats_ref), custom_call_target="tpu_custom_call" | custom-call | tf_op jit(solution)/shard_map/pallas_call | solution.py:332
  (8 shorter events, 0.1 us)
Async XLA Ops:
  0.6 1.0 %copy-start = (bf16[257,8,128]{2,1,0:T(8,128)(2,1)S(1)}, bf16[257,8,128]{2,1,0:T(8,128)(2,1)}, u32[]{:S(2)}) copy-start(bf16[257,8,128]{2,1,0:T(8,128)(2,1)} %video_ref.1) | copy-start | bytes 1579012
  2.3 10.0 %collective-permute-start = (bf16[400,256]{1,0:T(8,128)(2,1)S(1)}, bf16[400,256]{1,0:T(8,128)(2,1)S(1)}, u32[]{:S(2)}, u32[]{:S(2)}) collective-permute-start(bf16[400,256]{1,0:T(8,128)(2,1)S(1)} %get-tuple-element.18), channel_id=1, source_target_pairs={{0,4},{4,0},{8,12},{12,8},{1,5},{5,1},{9,13},{13,9},{2,6},{6,2},{1... | collective-permute-start | bytes 614408 | tf_op jit(solution)/shard_map/ppermute | solution.py:292
  2.8 9.5 %collective-permute-start.1 = (bf16[400,256]{1,0:T(8,128)(2,1)S(1)}, bf16[400,256]{1,0:T(8,128)(2,1)S(1)}, u32[]{:S(2)}, u32[]{:S(2)}) collective-permute-start(bf16[400,256]{1,0:T(8,128)(2,1)S(1)} %get-tuple-element.19), channel_id=1, source_target_pairs={{4,8},{8,4},{5,9},{9,5},{6,10},{10,6},{7,11},{11,7},{20,24},{24,20... | collective-permute-start | bytes 614408 | tf_op jit(solution)/shard_map/ppermute | solution.py:292
  3.5 5.5 %collective-permute-start.2 = (bf16[64,384]{1,0:T(8,128)(2,1)S(1)}, bf16[64,384]{1,0:T(8,128)(2,1)S(1)}, u32[]{:S(2)}, u32[]{:S(2)}) collective-permute-start(bf16[64,384]{1,0:T(8,128)(2,1)S(1)} %get-tuple-element.22), channel_id=1, source_target_pairs={{0,1},{1,0},{2,3},{3,2},{4,5},{5,4},{6,7},{7,6},{8,9},{9,8},{10,11... | collective-permute-start | bytes 147464 | tf_op jit(solution)/shard_map/ppermute | solution.py:292
  6.2 2.9 %collective-permute-start.3 = (bf16[64,384]{1,0:T(8,128)(2,1)S(1)}, bf16[64,384]{1,0:T(8,128)(2,1)S(1)}, u32[]{:S(2)}, u32[]{:S(2)}) collective-permute-start(bf16[64,384]{1,0:T(8,128)(2,1)S(1)} %get-tuple-element.23), channel_id=1, source_target_pairs={{1,2},{2,1},{5,6},{6,5},{9,10},{10,9},{13,14},{14,13},{17,18},{18,... | collective-permute-start | bytes 147464 | tf_op jit(solution)/shard_map/ppermute | solution.py:292
  7.9 0.8 %copy-start.1 = (f32[256,64]{0,1:T(8,128)S(1)}, f32[256,64]{0,1:T(8,128)}, u32[]{:S(2)}) copy-start(f32[256,64]{0,1:T(8,128)} %param.5) | copy-start | bytes 196612
  9.1 6.4 %collective-permute-start.4 = (f32[2,24,384]{2,1,0:T(8,128)S(1)}, f32[2,24,384]{2,1,0:T(8,128)S(1)}, u32[]{:S(2)}, u32[]{:S(2)}) collective-permute-start(f32[2,24,384]{2,1,0:T(8,128)S(1)} %get-tuple-element.24), channel_id=1, source_target_pairs={{0,4},{4,0},{8,12},{12,8},{1,5},{5,1},{9,13},{13,9},{2,6},{6,2},{1... | collective-permute-start | bytes 221192 | tf_op jit(solution)/shard_map/ppermute | solution.py:292
  11.7 3.8 %collective-permute-start.5 = (f32[2,24,384]{2,1,0:T(8,128)S(1)}, f32[2,24,384]{2,1,0:T(8,128)S(1)}, u32[]{:S(2)}, u32[]{:S(2)}) collective-permute-start(f32[2,24,384]{2,1,0:T(8,128)S(1)} %get-tuple-element.25), channel_id=1, source_target_pairs={{4,8},{8,4},{5,9},{9,5},{6,10},{10,6},{7,11},{11,7},{20,24},{24,20... | collective-permute-start | bytes 221192 | tf_op jit(solution)/shard_map/ppermute | solution.py:292
  16.1 3.1 %collective-permute-start.6 = (f32[136,128]{1,0:T(8,128)S(1)}, f32[136,128]{1,0:T(8,128)S(1)}, u32[]{:S(2)}, u32[]{:S(2)}) collective-permute-start(f32[136,128]{1,0:T(8,128)S(1)} %get-tuple-element.27), channel_id=1, source_target_pairs={{0,4},{4,0},{8,12},{12,8},{1,5},{5,1},{9,13},{13,9},{2,6},{6,2},{1... | collective-permute-start | bytes 208904 | tf_op jit(solution)/shard_map/ppermute | solution.py:323
  19.3 4.5 %collective-permute-start.7 = (f32[136,128]{1,0:T(8,128)S(1)}, f32[136,128]{1,0:T(8,128)S(1)}, u32[]{:S(2)}, u32[]{:S(2)}) collective-permute-start(f32[136,128]{1,0:T(8,128)S(1)} %add.14), channel_id=1, source_target_pairs={{0,8},{4,12},{8,0},{12,4},{1,9},{5,13},{9,1},{13,5},{2,10},{6,14},... | collective-permute-start | bytes 208904 | tf_op jit(solution)/shard_map/ppermute | solution.py:326
  23.8 6.8 %collective-permute-start.8 = (f32[136,128]{1,0:T(8,128)S(1)}, f32[136,128]{1,0:T(8,128)S(1)}, u32[]{:S(2)}, u32[]{:S(2)}) collective-permute-start(f32[136,128]{1,0:T(8,128)S(1)} %add.15), channel_id=1, source_target_pairs={{0,1},{1,0},{2,3},{3,2},{4,5},{5,4},{6,7},{7,6},{8,9},{9,8},{10,11... | collective-permute-start | bytes 208904 | tf_op jit(solution)/shard_map/ppermute | solution.py:326
  30.6 5.6 %collective-permute-start.9 = (f32[136,128]{1,0:T(8,128)S(1)}, f32[136,128]{1,0:T(8,128)S(1)}, u32[]{:S(2)}, u32[]{:S(2)}) collective-permute-start(f32[136,128]{1,0:T(8,128)S(1)} %add.16), channel_id=1, source_target_pairs={{0,2},{1,3},{2,0},{3,1},{4,6},{5,7},{6,4},{7,5},{8,10},{9,11},{10,... | collective-permute-start | bytes 208904 | tf_op jit(solution)/shard_map/ppermute | solution.py:326
  36.3 1.3 %collective-permute-start.10 = (f32[136,128]{1,0:T(8,128)S(1)}, f32[136,128]{1,0:T(8,128)S(1)}, u32[]{:S(2)}, u32[]{:S(2)}) collective-permute-start(f32[136,128]{1,0:T(8,128)S(1)} %add.17.mine_ref), channel_id=1, source_target_pairs={{0,4},{4,0},{8,12},{12,8},{1,5},{5,1},{9,13},{13,9},{2,6},{6,2},{1... | collective-permute-start | bytes 208904 | tf_op jit(solution)/shard_map/ppermute | solution.py:328

commit v4 on v2

--- a/solution.py
+++ b/solution.py
@@ -16,13 +16,13 @@
 SWEEPS = 2
 ROWS = 8
 COLS = 128
+SUMMED = HALF + 8
 BLOCKS = 16
 F32 = jnp.float32
 BF16 = jnp.bfloat16
 HIGHEST = lax.Precision.HIGHEST
-PARAMS = pltpu.CompilerParams(vmem_limit_bytes=48 * 1024 * 1024)
+PARAMS = pltpu.CompilerParams(vmem_limit_bytes=24 * 1024 * 1024)
 VMEM = pl.BlockSpec(memory_space=pltpu.VMEM)
-SMEM = pl.BlockSpec(memory_space=pltpu.SMEM)
 
 
 def turned(rows_ref, row, group):
@@ -34,9 +34,14 @@
     return jnp.concatenate(both, axis=1).astype(BF16)
 
 
-def own_kernel(parity_ref, video_ref, send_a_ref, send_b_ref, x_ref, rim_ref, rows_ref):
-    even = parity_ref[0] == 0
+def is_even(axis):
+    return (lax.axis_index(axis) & 1) == 0
+
+
+def own_kernel(video_ref, send_a_ref, send_b_ref, x_ref, rim_ref, rows_ref):
+    even = is_even("row")
     rows_ref[...] = video_ref[...].astype(F32).reshape(rows_ref.shape)
+    fill = jnp.zeros((8, COLS), F32)
     for group in range(3):
         lanes = slice(HALF * group, HALF * group + HALF)
         tiles = [turned(rows_ref, row, group) for row in range(ROWS)]
@@ -52,14 +57,21 @@
         rim_ref[1, :, lanes] = tiles[ROWS - 1]
     final = rows_ref[FRAMES * ROWS : FRAMES * ROWS + ROWS, :]
     shifted = pltpu.roll(final, REACH, 0)
-    fill = jnp.zeros((8, COLS), F32)
-    for ref, chosen in ((send_a_ref, jnp.where(even, shifted, final)), (send_b_ref, jnp.where(even, final, shifted))):
-        tail = jnp.concatenate([chosen, fill], axis=0).astype(BF16)
-        ref[REACH * COLS : REACH * COLS + 16, 0:COLS] = tail
-        ref[REACH * COLS : REACH * COLS + 16, COLS : 2 * COLS] = tail
-
-
-def band_kernel(taps_ref, start_ref, band_ref, basis_ref):
+    first, last = (jnp.concatenate([part, fill], axis=0).astype(BF16) for part in (final, shifted))
+    for ref, chosen in ((send_a_ref, jnp.where(even, last, first)), (send_b_ref, jnp.where(even, first, last))):
+        ref[REACH * COLS : REACH * COLS + 16, 0:COLS] = chosen
+        ref[REACH * COLS : REACH * COLS + 16, COLS : 2 * COLS] = chosen
+
+
+def band_kernel(filters_ref, band_ref, taps_ref):
+    taps_ref[...] = jnp.zeros((16, 128), F32)
+    for orient in range(ORIENT):
+        for part in range(2):
+            for i in range(TAPS):
+                line = filters_ref[orient, i, part : part + 1, :]
+                for cell in range(2):
+                    row, lane = 8 * part + 4 * cell + orient, 64 * cell + 8 * i
+                    taps_ref[row : row + 1, lane : lane + TAPS] = line
     taps = taps_ref[...]
     high = taps.astype(BF16)
     low = (taps - high.astype(F32)).astype(BF16)
@@ -77,6 +89,9 @@
             rolled = (pltpu.roll(base, 8, 1) if i else base).astype(BF16)
             band_ref[start : start + 16, 0:128] = rolled[:16]
             band_ref[start : start + 16, 128:256] = rolled[16:]
+
+
+def start_kernel(start_ref, basis_ref):
     basis_ref[...] = jnp.dot(start_ref[...], frame_order(0), precision=HIGHEST, preferred_element_type=F32)
 
 
@@ -86,8 +101,8 @@
     return jnp.where(frame == 2 * (lane & (HALF - 1)) + (lane >> 7), 1.0, 0.0).astype(F32)
 
 
-def halo_kernel(parity_ref, a_ref, b_ref, x_in_ref, rim_ref, x_ref, edge_a_ref, edge_b_ref):
-    even = parity_ref[0] == 0
+def halo_kernel(a_ref, b_ref, x_in_ref, rim_ref, band_ref, x_ref, side_ref):
+    even = is_even("row")
     got_a, got_b = a_ref[...], b_ref[...]
     final = lax.broadcasted_iota(jnp.int32, (COLS, HALF), 1) == HALF - 1
     sides = []
@@ -108,8 +123,7 @@
         x_ref[:, 80:96, lanes] = blocked(rim_ref[1, :, lanes], below[0][group])
         x_ref[:, 96:112, lanes] = blocked(below[1][group], below[2][group])
     x_ref[:, 32:80, :] = x_in_ref[:, 32:80, :]
-    edge_a_ref[...] = x_ref[(BLOCKS - 1) * (1 - parity_ref[1])]
-    edge_b_ref[...] = x_ref[(BLOCKS - 1) * parity_ref[1]]
+    side_ref[...] = x_ref[0]
 
 
 def block_feats(band_ref, left, right):
@@ -140,7 +154,11 @@
     return jnp.concatenate(pooled, axis=0)
 
 
-def inner_kernel(band_ref, x_ref, feats_ref):
+def second_cells():
+    return (lax.broadcasted_iota(jnp.int32, (16, FRAMES), 0) & 4) == 4
+
+
+def inner_kernel(band_ref, x_ref, feats_ref, start_ref):
     def body(step, carry):
         for i in range(3):
             block = 3 * step + i
@@ -148,32 +166,35 @@
         return carry
 
     lax.fori_loop(0, (BLOCKS - 1) // 3, body, 0)
-
-
-def edge_kernel(parity_ref, band_ref, x_ref, a_ref, b_ref, inner_ref, feats_ref, mine_ref, other_ref):
-    even = parity_ref[1] == 0
-    got_a = a_ref[...]
-    got_b = b_ref[...]
-    right = jnp.where(even, got_a, got_b)
-    left = jnp.where(even, got_b, got_a)
-    feats_left = block_feats(band_ref, left, x_ref[0])
-    feats_right = block_feats(band_ref, x_ref[BLOCKS - 1], right)
-    second = (lax.broadcasted_iota(jnp.int32, (16, FRAMES), 0) & 4) == 4
+    start = block_feats(band_ref, jnp.zeros((112, 3 * HALF), BF16), x_ref[0])
+    begins = lax.axis_index("col") == 0
+    start_ref[...] = jnp.where(second_cells() & begins, start, 0.0).astype(BF16)
+
+
+def edge_kernel(band_ref, x_ref, side_ref, inner_ref, start_ref, feats_ref, mine_ref, other_ref):
+    edge = block_feats(band_ref, x_ref[BLOCKS - 1], side_ref[...])
+    ends = lax.axis_index("col") == lax.axis_size("col") - 1
     feats_ref[0 : BLOCKS - 1] = inner_ref[0 : BLOCKS - 1]
-    feats_ref[BLOCKS - 1] = jnp.where(second, feats_left, feats_right).astype(BF16)
-    flat = feats_ref[...].reshape(16 * BLOCKS, FRAMES)
+    edge = jnp.where(second_cells() & ends, 0.0, edge).astype(BF16)
+    feats_ref[BLOCKS - 1] = edge
+    edge = edge.astype(F32)
+    flat = jnp.concatenate([feats_ref[...].reshape(16 * BLOCKS, FRAMES), start_ref[...]], axis=0)
     gram = lax.dot_general(flat, flat, (((0,), (0,)), ((), ())), preferred_element_type=F32)
     top, cross, low = gram[:HALF, :HALF], gram[:HALF, HALF:], gram[HALF:, HALF:]
     i = lax.broadcasted_iota(jnp.int32, (HALF, HALF), 0)
     j = lax.broadcasted_iota(jnp.int32, (HALF, HALF), 1)
     folded = jnp.where(i <= j, top, low)
     diagonal = jnp.sum(jnp.where(i == j, low, 0.0), axis=0, keepdims=True)
-    first = parity_ref[0] == 0
+    first = is_even("row")
     spare = jnp.broadcast_to(diagonal, (8, HALF))
     mine_ref[0:HALF] = jnp.where(first, cross, folded)
-    mine_ref[HALF : HALF + 8] = spare
+    mine_ref[HALF:SUMMED] = spare
+    passed = jnp.where(second_cells()[:8], edge[:8], pltpu.roll(edge[8:], 4, 0))
+    mine_ref[SUMMED : SUMMED + 8] = passed[:, :HALF]
+    mine_ref[SUMMED + 8 : SUMMED + 16] = passed[:, HALF:]
     other_ref[0:HALF] = jnp.where(first, folded, cross)
-    other_ref[HALF : HALF + 8] = spare
+    other_ref[HALF:SUMMED] = spare
+    other_ref[SUMMED : SUMMED + 16] = jnp.zeros((16, HALF), F32)
 
 
 def inverse_factor(inner):
@@ -205,8 +226,8 @@
     return jnp.concatenate(done, axis=0)[:, :MODES]
 
 
-def basis_kernel(scale, parity_ref, mine_ref, other_ref, start_ref, feats_ref, basis_ref, modes_ref, rows_ref, out_ref):
-    first = parity_ref[0] == 0
+def basis_kernel(scale, mine_ref, other_ref, start_ref, feats_ref, first_ref, before_ref, basis_ref, modes_ref, rows_ref, out_ref):
+    first = is_even("row")
     mine, other = mine_ref[...], other_ref[...]
     cross = jnp.where(first, mine, other)[:HALF]
     second = jnp.where(first, other, mine)
@@ -229,7 +250,11 @@
         basis = jnp.dot(inverse_factor(inner), stacked, precision=HIGHEST, preferred_element_type=F32)
     basis_ref[...] = jnp.dot(basis, frame_order(1), precision=HIGHEST, preferred_element_type=F32)
     twice = jnp.concatenate([basis, basis], axis=0)
-    flat = feats_ref[...].reshape(16 * BLOCKS, FRAMES)
+    before = jnp.concatenate([before_ref[:8], before_ref[8:]], axis=1)
+    before = jnp.concatenate([before, pltpu.roll(before, 4, 0)], axis=0)
+    before = jnp.where(lax.axis_index("col") == 0, first_ref[...].astype(F32), before)
+    cell = jnp.where(second_cells(), before, feats_ref[BLOCKS - 1].astype(F32)).astype(BF16)
+    flat = jnp.concatenate([feats_ref[0 : BLOCKS - 1].reshape(16 * BLOCKS - 16, FRAMES), cell], axis=0)
     rows_ref[...] = lax.dot_general(
         flat, twice.astype(BF16), (((1,), (1,)), ((), ())), preferred_element_type=F32
     )
@@ -247,14 +272,13 @@
             modes_ref[row, :, 128 * half : 128 * half + 128] = out_ref[64 * row + 32 * half : 64 * row + 32 * half + 32]
 
 
-def call(kernel, outs, n_smem, n_in, scratch=(), aliases={}):
+def call(kernel, outs, n_in, scratch=()):
     return pl.pallas_call(
         kernel,
         out_shape=[jax.ShapeDtypeStruct(shape, dtype) for shape, dtype in outs],
-        in_specs=[SMEM] * n_smem + [VMEM] * (n_in - n_smem),
+        in_specs=[VMEM] * n_in,
         out_specs=[VMEM] * len(outs),
         scratch_shapes=list(scratch),
-        input_output_aliases=aliases,
         compiler_params=PARAMS,
     )
 
@@ -268,46 +292,56 @@
 
 def on_device(video, filters, start_basis):
     size_row, size_col = lax.axis_size("row"), lax.axis_size("col")
-    parity = jnp.stack([lax.axis_index("row") & 1, lax.axis_index("col") & 1]).astype(jnp.int32)
-
-    rows = pltpu.VMEM(((FRAMES + 1) * ROWS, COLS), F32)
+    near, far = pairs(size_row, 0), pairs(size_row, 1)
+    to_left = [(i + 1, i) for i in range(size_col - 1)]
+
     send = ((REACH * COLS + 16, FRAMES), BF16)
     tile = ((BLOCKS, 112, 3 * HALF), BF16)
     rim = ((2, COLS, 3 * HALF), F32)
-    send_a, send_b, x, rim = call(own_kernel, [send, send, tile, rim], 1, 2, [rows])(parity, video)
-    got_a = lax.ppermute(send_a, "row", pairs(size_row, 0))
-    got_b = lax.ppermute(send_b, "row", pairs(size_row, 1))
-
-    taps = jnp.pad(filters, ((0, 0), (0, 0), (0, 1), (0, 1))).reshape(ORIENT, 2, 64)
-    taps = jnp.transpose(taps, (1, 0, 2))[:, None, :, None, :] * jnp.eye(2, dtype=F32)[None, :, None, :, None]
-    band, start = call(band_kernel, [((128, 256), BF16), ((MODES, FRAMES), F32)], 0, 2)(
-        taps.reshape(16, 128), start_basis.T
-    )
-    edge = ((112, 3 * HALF), BF16)
-    x, edge_a, edge_b = call(halo_kernel, [tile, edge, edge], 1, 5)(parity, got_a, got_b, x, rim)
-    got_a = lax.ppermute(edge_a, "col", pairs(size_col, 0))
-    got_b = lax.ppermute(edge_b, "col", pairs(size_col, 1))
+    rows = pltpu.VMEM(((FRAMES + 1) * ROWS, COLS), F32)
+    send_a, send_b, x, rim = call(own_kernel, [send, send, tile, rim], 1, [rows])(video)
+    got_a = lax.ppermute(send_a, "row", near)
+    got_b = lax.ppermute(send_b, "row", far)
+
+    (band,) = call(band_kernel, [((128, 256), BF16)], 1, [pltpu.VMEM((16, 128), F32)])(
+        jnp.transpose(filters, (0, 2, 1, 3))
+    )
+    x, side = call(halo_kernel, [tile, ((112, 3 * HALF), BF16)], 5)(got_a, got_b, x, rim, band)
+    side = lax.ppermute(side, "col", to_left)
     feats_shape = ((BLOCKS, 16, FRAMES), BF16)
-    (inner,) = call(inner_kernel, [feats_shape], 0, 2)(band, x)
-    part = ((HALF + 8, HALF), F32)
-    feats, mine, other = call(edge_kernel, [feats_shape, part, part], 1, 6)(parity, band, x, got_a, got_b, inner)
-
-    mine = mine + lax.ppermute(other, "row", pairs(size_row, 0))
-    for axis, size, step in (("row", size_row, 2), ("col", size_col, 1)):
-        while step < size:
-            mine = mine + lax.ppermute(mine, axis, [(i, i ^ step) for i in range(size)])
-            step *= 2
-    other = lax.ppermute(mine, "row", pairs(size_row, 0))
+    inner, first = call(inner_kernel, [feats_shape, ((16, FRAMES), BF16)], 2)(band, x)
+    part = ((SUMMED + 16, HALF), F32)
+    feats, mine, other = call(edge_kernel, [feats_shape, part, part], 5)(band, x, side, inner, first)
+
+    mine = mine + lax.ppermute(other, "row", near)
+    summed = lax.broadcasted_iota(jnp.int32, mine.shape, 0) < SUMMED
+    step = 2
+    while step < size_row:
+        got = lax.ppermute(mine, "row", [(i, i ^ step) for i in range(size_row)])
+        mine = jnp.where(summed, mine + got, mine)
+        step *= 2
+    step = 1
+    col = lax.axis_index("col")
+    before = jnp.zeros((16, HALF), F32)
+    start = start_basis.T
+    while step < size_col:
+        if 2 * step >= size_col:
+            mine, start = lax.optimization_barrier((mine, start))
+            (start,) = call(start_kernel, [((MODES, FRAMES), F32)], 1)(start)
+        got = lax.ppermute(mine, "col", [(i, i ^ step) for i in range(size_col)])
+        mine = jnp.where(summed, mine + got, got)
+        before = jnp.where((col & (2 * step - 1)) == step, got[SUMMED:], before)
+        step *= 2
+    other = lax.ppermute(mine, "row", near)
 
     features = ORIENT * (size_row * ROWS // 4) * (size_col * COLS // 4)
     kernel = functools.partial(basis_kernel, 1.0 / features)
     basis, modes = call(
         kernel,
         [((MODES, FRAMES), F32), ((ROWS // 4, COLS // 4, ORIENT * MODES), F32)],
-        1,
-        5,
+        6,
         [pltpu.VMEM((FRAMES, 2 * MODES), F32), pltpu.VMEM((128, 128), F32)],
-    )(parity, mine, other, start, feats)
+    )(mine, other, start, feats, first, before)
     return basis.T, modes
 
 

time: 47.6 us -> 41.8 us (0.88)
  starting transfers between devices: 18 us -> 14.5 us
  Pallas kernels: 13.9 us -> 11.5 us
  local copies, waits for them, and re-layouts: 3.48 us -> 1.78 us
  waiting for transfers between devices: 11 us -> 12.7 us
    ppermute x9 -> x8, starting transfers between devices: 18 us -> 14.5 us  [the longest x1 5.22 us: on_device(): mine = mine + lax.ppermute(other, 'row', near)]
    pallas_call x5 -> x6, Pallas kernels: 7 us -> 5.21 us  [the longest x1 3.04 us: on_device(): call(inner_kernel, [feats_shape, ((16, FRAMES), BF16)], 2)(band, x)]
    ppermute x9 -> x8, waiting for transfers between devices: 11 us -> 12.7 us  [the longest x2 5.26 us: on_device(): got = lax.ppermute(mine, 'col', [(i, i ^ step) for i in range(size_col)])]
    unnamed x11 -> x6, local copies, waits for them, and re-layouts: 3.3 us -> 1.78 us
    pallas_call x1, Pallas kernels: 6.85 us -> 6.31 us  [on_device(): call(kernel, [((MODES, FRAMES), F32), ((ROWS // 4, COLS // 4, ORIENT * MO...]
  transfers between devices with their start and end apart: 9 -> 8, of which waited for: 5 -> 6; matrix products, arithmetic and copies ran while one was open for 2% -> 0% of each run, Pallas kernels for 6% -> 9%
where the time goes in v4:
time: 41.8 us; the launch traced here: 41.6 us
  starting transfers between devices  14.5 us (35%)
  waiting for transfers between devices  12.7 us (30%)
  Pallas kernels  11.5 us (28%)
  local copies, waits for them, and re-layouts  1.78 us (4%)
  between operations  0.76 us (2%)
    pallas_call x1, Pallas kernels, on_device(): call(kernel, [((MODES, FRAMES), F32), ((ROWS // 4, COLS // 4, ORIENT * MO...  6.31 us
    ppermute x2, waiting for transfers between devices, on_device(): got = lax.ppermute(mine, 'col', [(i, i ^ step) for i in range(size_col)])  5.26 us
    ppermute x1, starting transfers between devices, on_device(): mine = mine + lax.ppermute(other, 'row', near)  5.22 us
    ppermute x2, starting transfers between devices, on_device(): got = lax.ppermute(mine, 'col', [(i, i ^ step) for i in range(size_col)])  4.3 us
    pallas_call x1, Pallas kernels, on_device(): call(inner_kernel, [feats_shape, ((16, FRAMES), BF16)], 2)(band, x)  3.04 us
    ppermute x1, waiting for transfers between devices, on_device(): got = lax.ppermute(mine, 'row', [(i, i ^ step) for i in range(size_row)])  2.67 us
    ppermute x1, waiting for transfers between devices, on_device(): side = lax.ppermute(side, 'col', to_left)  2.61 us
    ppermute x1, starting transfers between devices, on_device(): got = lax.ppermute(mine, 'row', [(i, i ^ step) for i in range(size_row)])  2.44 us
  transfers between devices with their start and end apart: 8, of which 6 were waited for; matrix products, arithmetic and copies ran while one was open for 0% of the time, Pallas kernels for 9%

profile of v4, /device:TPU:0, one launch (start us, length us, event | category | flops | bytes accessed | tf_op | source)
XLA Modules:
  0.0 41.6 jit_solution(2350658140285346986)
XLA Ops:
  0.6 0.0 copy-start
  0.6 1.0 %copy-done = bf16[257,8,128]{2,1,0:T(8,128)(2,1)S(1)} copy-done((bf16[257,8,128]{2,1,0:T(8,128)(2,1)S(1)}, bf16[257,8,128]{2,1,0:T(8,128)(2,1)}, u32[]{:S(2)}) %copy-start) | copy-done | bytes 526360
  1.7 0.6 %shard_map.51 = (bf16[400,256]{1,0:T(8,128)(2,1)S(1)}, bf16[400,256]{1,0:T(8,128)(2,1)S(1)}, bf16[16,112,384]{2,1,0:T(8,128)(2,1)S(1)}, f32[2,128,384]{2,1,0:T(8,128)S(1)}) custom-call(bf16[257,8,128]{2,1,0:T(8,128)(2,1)S(1)} %copy-done), custom_call_target="tpu_custom_call" | custom-call | tf_op jit(solution)/shard_map/pallas_call | solution.py:302
  2.3 0.5 %collective-permute-start = (bf16[400,256]{1,0:T(8,128)(2,1)S(1)}, bf16[400,256]{1,0:T(8,128)(2,1)S(1)}, u32[]{:S(2)}, u32[]{:S(2)}) collective-permute-start(bf16[400,256]{1,0:T(8,128)(2,1)S(1)} %get-tuple-element.17), channel_id=1, source_target_pairs={{0,4},{4,0},{8,12},{12,8},{1,5},{5,1},{9,13},{13,9},{2,6},{6,2},{1... | collective-permute-start | bytes 614408 | tf_op jit(solution)/shard_map/ppermute | solution.py:303
  2.8 0.7 %collective-permute-start.1 = (bf16[400,256]{1,0:T(8,128)(2,1)S(1)}, bf16[400,256]{1,0:T(8,128)(2,1)S(1)}, u32[]{:S(2)}, u32[]{:S(2)}) collective-permute-start(bf16[400,256]{1,0:T(8,128)(2,1)S(1)} %get-tuple-element.18), channel_id=1, source_target_pairs={{4,8},{8,4},{5,9},{9,5},{6,10},{10,6},{7,11},{11,7},{20,24},{24,20... | collective-permute-start | bytes 614408 | tf_op jit(solution)/shard_map/ppermute | solution.py:304
  3.5 0.0 copy-start.2
  3.5 0.7 %copy-done.2 = f32[4,2,7,7]{3,1,2,0:T(2,128)S(1)} copy-done((f32[4,2,7,7]{3,1,2,0:T(2,128)S(1)}, f32[4,2,7,7]{3,1,2,0:T(2,128)}, u32[]{:S(2)}) %copy-start.2) | copy-done | bytes 1592
  4.3 0.4 shard_map.50.band_ref
  4.6 0.0 collective-permute-done.a_ref
  4.6 0.0 collective-permute-done.1.b_ref
  4.7 0.3 shard_map.52
  5.0 1.3 %collective-permute-start.2 = (bf16[112,384]{1,0:T(8,128)(2,1)S(1)}, bf16[112,384]{1,0:T(8,128)(2,1)S(1)}, u32[]{:S(2)}, u32[]{:S(2)}) collective-permute-start(bf16[112,384]{1,0:T(8,128)(2,1)S(1)} %get-tuple-element.22), channel_id=1, source_target_pairs={{1,0},{2,1},{3,2},{5,4},{6,5},{7,6},{9,8},{10,9},{11,10},{13,12},{... | collective-permute-start | bytes 258056 | tf_op jit(solution)/shard_map/ppermute | solution.py:310
  6.3 3.0 %shard_map.53 = (bf16[16,16,256]{2,1,0:T(8,128)(2,1)S(1)}, bf16[16,256]{1,0:T(8,128)(2,1)S(1)}) custom-call(bf16[128,256]{1,0:T(8,128)(2,1)S(1)} %shard_map.50.band_ref, bf16[16,112,384]{2,1,0:T(8,128)(2,1)S(1)} %get-tuple-element.21.x_ref), custom_call_target="tpu_custom_call" | custom-call | tf_op jit(solution)/shard_map/pallas_call | solution.py:312
  9.3 0.0 copy-start.1
  9.3 2.6 %collective-permute-done.2.side_ref = bf16[112,384]{1,0:T(8,128)(2,1)S(1)} collective-permute-done((bf16[112,384]{1,0:T(8,128)(2,1)S(1)}, bf16[112,384]{1,0:T(8,128)(2,1)S(1)}, u32[]{:S(2)}, u32[]{:S(2)}) %collective-permute-start.2) | collective-permute-done | bytes 86048 | tf_op jit(solution)/shard_map/ppermute | solution.py:310
  12.0 0.6 %shard_map.54 = (bf16[16,16,256]{2,1,0:T(8,128)(2,1)S(1)}, f32[152,128]{1,0:T(8,128)S(1)}, f32[152,128]{1,0:T(8,128)S(1)}) custom-call(bf16[128,256]{1,0:T(8,128)(2,1)S(1)} %shard_map.50.band_ref, bf16[16,112,384]{2,1,0:T(8,128)(2,1)S(1)} %get-tuple-element.21.x_ref, bf16[112,384]{1,0:T(8,128)(2,1)S(1)} %collective-permute-done.2.side_ref, ...), custom_call_target="tpu_custom_call" | custom-call | tf_op jit(solution)/shard_map/pallas_call | solution.py:314
  12.5 5.2 %collective-permute-start.3 = (f32[152,128]{1,0:T(8,128)S(1)}, f32[152,128]{1,0:T(8,128)S(1)}, u32[]{:S(2)}, u32[]{:S(2)}) collective-permute-start(f32[152,128]{1,0:T(8,128)S(1)} %get-tuple-element.26), channel_id=1, source_target_pairs={{0,4},{4,0},{8,12},{12,8},{1,5},{5,1},{9,13},{13,9},{2,6},{6,2},{1... | collective-permute-start | bytes 233480 | tf_op jit(solution)/shard_map/ppermute | solution.py:316
  17.8 0.9 %collective-permute-done.3 = f32[152,128]{1,0:T(8,128)S(1)} collective-permute-done((f32[152,128]{1,0:T(8,128)S(1)}, f32[152,128]{1,0:T(8,128)S(1)}, u32[]{:S(2)}, u32[]{:S(2)}) %collective-permute-start.3) | collective-permute-done | bytes 77856 | tf_op jit(solution)/shard_map/ppermute | solution.py:316
  18.7 2.4 %collective-permute-start.4 = (f32[152,128]{1,0:T(8,128)S(1)}, f32[152,128]{1,0:T(8,128)S(1)}, u32[]{:S(2)}, u32[]{:S(2)}) collective-permute-start(f32[152,128]{1,0:T(8,128)S(1)} %add.12), channel_id=1, source_target_pairs={{0,8},{4,12},{8,0},{12,4},{1,9},{5,13},{9,1},{13,5},{2,10},{6,14},... | collective-permute-start | bytes 233480 | tf_op jit(solution)/shard_map/ppermute | solution.py:320
  21.1 2.7 %collective-permute-done.4 = f32[152,128]{1,0:T(8,128)S(1)} collective-permute-done((f32[152,128]{1,0:T(8,128)S(1)}, f32[152,128]{1,0:T(8,128)S(1)}, u32[]{:S(2)}, u32[]{:S(2)}) %collective-permute-start.4) | collective-permute-done | bytes 77856 | tf_op jit(solution)/shard_map/ppermute | solution.py:320
  23.8 0.1 add_select_fusion.2
  23.9 1.6 %collective-permute-start.5 = (f32[152,128]{1,0:T(8,128)S(1)}, f32[152,128]{1,0:T(8,128)S(1)}, u32[]{:S(2)}, u32[]{:S(2)}) collective-permute-start(f32[152,128]{1,0:T(8,128)S(1)} %add_select_fusion.2), channel_id=1, source_target_pairs={{0,1},{1,0},{2,3},{3,2},{4,5},{5,4},{6,7},{7,6},{8,9},{9,8},{10,11... | collective-permute-start | bytes 233480 | tf_op jit(solution)/shard_map/ppermute | solution.py:331
  25.5 2.8 %collective-permute-done.5 = f32[152,128]{1,0:T(8,128)S(1)} collective-permute-done((f32[152,128]{1,0:T(8,128)S(1)}, f32[152,128]{1,0:T(8,128)S(1)}, u32[]{:S(2)}, u32[]{:S(2)}) %collective-permute-start.5) | collective-permute-done | bytes 77856 | tf_op jit(solution)/shard_map/ppermute | solution.py:331
  28.4 0.1 add_select_fusion.1
  28.5 2.7 %collective-permute-start.6 = (f32[152,128]{1,0:T(8,128)S(1)}, f32[152,128]{1,0:T(8,128)S(1)}, u32[]{:S(2)}, u32[]{:S(2)}) collective-permute-start(f32[152,128]{1,0:T(8,128)S(1)} %add_select_fusion.1), channel_id=1, source_target_pairs={{0,2},{1,3},{2,0},{3,1},{4,6},{5,7},{6,4},{7,5},{8,10},{9,11},{10,... | collective-permute-start | bytes 233480 | tf_op jit(solution)/shard_map/ppermute | solution.py:331
  31.1 0.0 copy-done.1
  31.1 0.3 shard_map.55.start_ref
  31.4 2.4 %collective-permute-done.6 = f32[152,128]{1,0:T(8,128)S(1)} collective-permute-done((f32[152,128]{1,0:T(8,128)S(1)}, f32[152,128]{1,0:T(8,128)S(1)}, u32[]{:S(2)}, u32[]{:S(2)}) %collective-permute-start.6) | collective-permute-done | bytes 77856 | tf_op jit(solution)/shard_map/ppermute | solution.py:331
  33.8 0.1 add_select_fusion.mine_ref
  33.9 0.1 collective-permute-start.7
  34.0 1.2 %collective-permute-done.7.other_ref = f32[152,128]{1,0:T(8,128)S(1)} collective-permute-done((f32[152,128]{1,0:T(8,128)S(1)}, f32[152,128]{1,0:T(8,128)S(1)}, u32[]{:S(2)}, u32[]{:S(2)}) %collective-permute-start.7) | collective-permute-done | bytes 77856 | tf_op jit(solution)/shard_map/ppermute | solution.py:335
  35.3 6.3 %shard_map.56 = (f32[64,256]{1,0:T(8,128)}, f32[2,32,256]{2,1,0:T(8,128)}) custom-call(f32[152,128]{1,0:T(8,128)S(1)} %add_select_fusion.mine_ref, f32[152,128]{1,0:T(8,128)S(1)} %collective-permute-done.7.other_ref, f32[64,256]{1,0:T(8,128)S(1)} %shard_map.55.start_ref, bf16[16,16,256]{2,1,0:T(8,128)(2,1)S(1)} %get-tuple-element.29.feats_ref, ...), custom_call_target="tpu_custom_call" | custom-call | tf_op jit(solution)/shard_map/pallas_call | solution.py:339
  (3 shorter events, 0.0 us)
Async XLA Ops:
  0.6 1.0 %copy-start = (bf16[257,8,128]{2,1,0:T(8,128)(2,1)S(1)}, bf16[257,8,128]{2,1,0:T(8,128)(2,1)}, u32[]{:S(2)}) copy-start(bf16[257,8,128]{2,1,0:T(8,128)(2,1)} %video_ref.1) | copy-start | bytes 1579012
  2.3 2.3 %collective-permute-start = (bf16[400,256]{1,0:T(8,128)(2,1)S(1)}, bf16[400,256]{1,0:T(8,128)(2,1)S(1)}, u32[]{:S(2)}, u32[]{:S(2)}) collective-permute-start(bf16[400,256]{1,0:T(8,128)(2,1)S(1)} %get-tuple-element.17), channel_id=1, source_target_pairs={{0,4},{4,0},{8,12},{12,8},{1,5},{5,1},{9,13},{13,9},{2,6},{6,2},{1... | collective-permute-start | bytes 614408 | tf_op jit(solution)/shard_map/ppermute | solution.py:303
  2.8 1.8 %collective-permute-start.1 = (bf16[400,256]{1,0:T(8,128)(2,1)S(1)}, bf16[400,256]{1,0:T(8,128)(2,1)S(1)}, u32[]{:S(2)}, u32[]{:S(2)}) collective-permute-start(bf16[400,256]{1,0:T(8,128)(2,1)S(1)} %get-tuple-element.18), channel_id=1, source_target_pairs={{4,8},{8,4},{5,9},{9,5},{6,10},{10,6},{7,11},{11,7},{20,24},{24,20... | collective-permute-start | bytes 614408 | tf_op jit(solution)/shard_map/ppermute | solution.py:304
  3.5 0.8 %copy-start.2 = (f32[4,2,7,7]{3,1,2,0:T(2,128)S(1)}, f32[4,2,7,7]{3,1,2,0:T(2,128)}, u32[]{:S(2)}) copy-start(f32[4,2,7,7]{3,1,2,0:T(2,128)} %param.4) | copy-start | bytes 4708
  5.0 7.0 %collective-permute-start.2 = (bf16[112,384]{1,0:T(8,128)(2,1)S(1)}, bf16[112,384]{1,0:T(8,128)(2,1)S(1)}, u32[]{:S(2)}, u32[]{:S(2)}) collective-permute-start(bf16[112,384]{1,0:T(8,128)(2,1)S(1)} %get-tuple-element.22), channel_id=1, source_target_pairs={{1,0},{2,1},{3,2},{5,4},{6,5},{7,6},{9,8},{10,9},{11,10},{13,12},{... | collective-permute-start | bytes 258056 | tf_op jit(solution)/shard_map/ppermute | solution.py:310
  9.3 21.8 %copy-start.1 = (f32[256,64]{0,1:T(8,128)S(1)}, f32[256,64]{0,1:T(8,128)}, u32[]{:S(2)}) copy-start(f32[256,64]{0,1:T(8,128)} %param.5) | copy-start | bytes 196612
  12.5 6.1 %collective-permute-start.3 = (f32[152,128]{1,0:T(8,128)S(1)}, f32[152,128]{1,0:T(8,128)S(1)}, u32[]{:S(2)}, u32[]{:S(2)}) collective-permute-start(f32[152,128]{1,0:T(8,128)S(1)} %get-tuple-element.26), channel_id=1, source_target_pairs={{0,4},{4,0},{8,12},{12,8},{1,5},{5,1},{9,13},{13,9},{2,6},{6,2},{1... | collective-permute-start | bytes 233480 | tf_op jit(solution)/shard_map/ppermute | solution.py:316
  18.7 5.1 %collective-permute-start.4 = (f32[152,128]{1,0:T(8,128)S(1)}, f32[152,128]{1,0:T(8,128)S(1)}, u32[]{:S(2)}, u32[]{:S(2)}) collective-permute-start(f32[152,128]{1,0:T(8,128)S(1)} %add.12), channel_id=1, source_target_pairs={{0,8},{4,12},{8,0},{12,4},{1,9},{5,13},{9,1},{13,5},{2,10},{6,14},... | collective-permute-start | bytes 233480 | tf_op jit(solution)/shard_map/ppermute | solution.py:320
  23.9 4.5 %collective-permute-start.5 = (f32[152,128]{1,0:T(8,128)S(1)}, f32[152,128]{1,0:T(8,128)S(1)}, u32[]{:S(2)}, u32[]{:S(2)}) collective-permute-start(f32[152,128]{1,0:T(8,128)S(1)} %add_select_fusion.2), channel_id=1, source_target_pairs={{0,1},{1,0},{2,3},{3,2},{4,5},{5,4},{6,7},{7,6},{8,9},{9,8},{10,11... | collective-permute-start | bytes 233480 | tf_op jit(solution)/shard_map/ppermute | solution.py:331
  28.5 5.4 %collective-permute-start.6 = (f32[152,128]{1,0:T(8,128)S(1)}, f32[152,128]{1,0:T(8,128)S(1)}, u32[]{:S(2)}, u32[]{:S(2)}) collective-permute-start(f32[152,128]{1,0:T(8,128)S(1)} %add_select_fusion.1), channel_id=1, source_target_pairs={{0,2},{1,3},{2,0},{3,1},{4,6},{5,7},{6,4},{7,5},{8,10},{9,11},{10,... | collective-permute-start | bytes 233480 | tf_op jit(solution)/shard_map/ppermute | solution.py:331
  33.9 1.3 %collective-permute-start.7 = (f32[152,128]{1,0:T(8,128)S(1)}, f32[152,128]{1,0:T(8,128)S(1)}, u32[]{:S(2)}, u32[]{:S(2)}) collective-permute-start(f32[152,128]{1,0:T(8,128)S(1)} %add_select_fusion.mine_ref), channel_id=1, source_target_pairs={{0,4},{4,0},{8,12},{12,8},{1,5},{5,1},{9,13},{13,9},{2,6},{6,2},{1... | collective-permute-start | bytes 233480 | tf_op jit(solution)/shard_map/ppermute | solution.py:335

commit v5 on v4

--- a/solution.py
+++ b/solution.py
@@ -38,29 +38,52 @@
     return (lax.axis_index(axis) & 1) == 0
 
 
-def own_kernel(video_ref, send_a_ref, send_b_ref, x_ref, rim_ref, rows_ref):
+def send_kernel(video_ref, rows_ref, send_a_ref, send_b_ref):
     even = is_even("row")
     rows_ref[...] = video_ref[...].astype(F32).reshape(rows_ref.shape)
+    for group in range(2):
+        lanes = slice(HALF * group, HALF * group + HALF)
+        for i in range(REACH):
+            first, last = turned(rows_ref, i, group), turned(rows_ref, ROWS - REACH + i, group)
+            at = slice(COLS * i, COLS * i + COLS)
+            send_a_ref[at, lanes] = jnp.where(even, last, first).astype(BF16)
+            send_b_ref[at, lanes] = jnp.where(even, first, last).astype(BF16)
     fill = jnp.zeros((8, COLS), F32)
-    for group in range(3):
-        lanes = slice(HALF * group, HALF * group + HALF)
-        tiles = [turned(rows_ref, row, group) for row in range(ROWS)]
-        if group < 2:
-            for i in range(REACH):
-                first, last = tiles[i], tiles[ROWS - REACH + i]
-                at = slice(COLS * i, COLS * i + COLS)
-                send_a_ref[at, lanes] = jnp.where(even, last, first).astype(BF16)
-                send_b_ref[at, lanes] = jnp.where(even, first, last).astype(BF16)
-        for pair in range(3):
-            x_ref[:, 32 + 16 * pair : 48 + 16 * pair, lanes] = blocked(tiles[2 * pair + 1], tiles[2 * pair + 2])
-        rim_ref[0, :, lanes] = tiles[0]
-        rim_ref[1, :, lanes] = tiles[ROWS - 1]
     final = rows_ref[FRAMES * ROWS : FRAMES * ROWS + ROWS, :]
     shifted = pltpu.roll(final, REACH, 0)
     first, last = (jnp.concatenate([part, fill], axis=0).astype(BF16) for part in (final, shifted))
     for ref, chosen in ((send_a_ref, jnp.where(even, last, first)), (send_b_ref, jnp.where(even, first, last))):
         ref[REACH * COLS : REACH * COLS + 16, 0:COLS] = chosen
         ref[REACH * COLS : REACH * COLS + 16, COLS : 2 * COLS] = chosen
+
+
+def own_kernel(rows_ref, a_ref, x_ref, rim_ref, side_ref, diag_ref):
+    even = is_even("row")
+    fill = jnp.zeros((8, HALF), F32)
+    near = expanded(a_ref[...].astype(F32), 8)
+    for group in range(3):
+        lanes = slice(HALF * group, HALF * group + HALF)
+        tiles = [turned(rows_ref, row, group) for row in range(ROWS)]
+        for pair in range(3):
+            x_ref[:, 32 + 16 * pair : 48 + 16 * pair, lanes] = blocked(tiles[2 * pair + 1], tiles[2 * pair + 2])
+        rim_ref[0, :, lanes] = tiles[0]
+        rim_ref[1, :, lanes] = tiles[ROWS - 1]
+        heads = [tile[:8] for tile in tiles]
+        sent = heads + [row[group] for row in near] + [fill]
+        side_ref[:, lanes] = jnp.concatenate(sent, axis=0).astype(BF16)
+        chosen = [jnp.where(even, heads[i], heads[ROWS - REACH + i]) for i in range(REACH)] + [fill]
+        diag_ref[:, lanes] = jnp.concatenate(chosen, axis=0).astype(BF16)
+
+
+def expanded(got, count):
+    final = lax.broadcasted_iota(jnp.int32, (count, HALF), 1) == HALF - 1
+    ends = got[REACH * COLS : REACH * COLS + 8, :COLS].T
+    rows = []
+    for i in range(REACH):
+        tile = got[COLS * i : COLS * i + count]
+        late = jnp.where(final, ends[:count, i : i + 1], pltpu.roll(tile[:, :HALF], HALF - 1, 1))
+        rows.append([tile[:, :HALF], tile[:, HALF:], late])
+    return rows
 
 
 def band_kernel(filters_ref, band_ref, taps_ref):
@@ -101,21 +124,11 @@
     return jnp.where(frame == 2 * (lane & (HALF - 1)) + (lane >> 7), 1.0, 0.0).astype(F32)
 
 
-def halo_kernel(a_ref, b_ref, x_in_ref, rim_ref, band_ref, x_ref, side_ref):
+def halo_kernel(a_ref, b_ref, x_in_ref, rim_ref, band_ref, x_ref):
     even = is_even("row")
     got_a, got_b = a_ref[...], b_ref[...]
-    final = lax.broadcasted_iota(jnp.int32, (COLS, HALF), 1) == HALF - 1
-    sides = []
-    for got in (jnp.where(even, got_b, got_a), jnp.where(even, got_a, got_b)):
-        got = got.astype(F32)
-        ends = got[REACH * COLS : REACH * COLS + 8, :COLS].T
-        rows = []
-        for i in range(REACH):
-            tile = got[COLS * i : COLS * i + COLS]
-            late = jnp.where(final, ends[:, i : i + 1], pltpu.roll(tile[:, :HALF], HALF - 1, 1))
-            rows.append([tile[:, :HALF], tile[:, HALF:], late])
-        sides.append(rows)
-    above, below = sides
+    above = expanded(jnp.where(even, got_b, got_a).astype(F32), COLS)
+    below = expanded(jnp.where(even, got_a, got_b).astype(F32), COLS)
     for group in range(3):
         lanes = slice(HALF * group, HALF * group + HALF)
         x_ref[:, 0:16, lanes] = blocked(above[0][group], above[1][group])
@@ -123,7 +136,6 @@
         x_ref[:, 80:96, lanes] = blocked(rim_ref[1, :, lanes], below[0][group])
         x_ref[:, 96:112, lanes] = blocked(below[1][group], below[2][group])
     x_ref[:, 32:80, :] = x_in_ref[:, 32:80, :]
-    side_ref[...] = x_ref[0]
 
 
 def block_feats(band_ref, left, right):
@@ -171,8 +183,12 @@
     start_ref[...] = jnp.where(second_cells() & begins, start, 0.0).astype(BF16)
 
 
-def edge_kernel(band_ref, x_ref, side_ref, inner_ref, start_ref, feats_ref, mine_ref, other_ref):
-    edge = block_feats(band_ref, x_ref[BLOCKS - 1], side_ref[...])
+def edge_kernel(band_ref, x_ref, side_ref, diag_ref, inner_ref, start_ref, feats_ref, mine_ref, other_ref):
+    even = is_even("row")
+    side = side_ref[...].astype(F32)
+    near, far = side[8 * ROWS : 8 * ROWS + 8 * REACH], diag_ref[...].astype(F32)[: 8 * REACH]
+    rows = [jnp.where(even, far, near), side[: 8 * ROWS], jnp.where(even, near, far)]
+    edge = block_feats(band_ref, x_ref[BLOCKS - 1], jnp.concatenate(rows, axis=0).astype(BF16))
     ends = lax.axis_index("col") == lax.axis_size("col") - 1
     feats_ref[0 : BLOCKS - 1] = inner_ref[0 : BLOCKS - 1]
     edge = jnp.where(second_cells() & ends, 0.0, edge).astype(BF16)
@@ -295,23 +311,27 @@
     near, far = pairs(size_row, 0), pairs(size_row, 1)
     to_left = [(i + 1, i) for i in range(size_col - 1)]
 
+    across = [(a * size_col + i, b * size_col + j) for a, b in far for i, j in to_left]
     send = ((REACH * COLS + 16, FRAMES), BF16)
     tile = ((BLOCKS, 112, 3 * HALF), BF16)
     rim = ((2, COLS, 3 * HALF), F32)
-    rows = pltpu.VMEM(((FRAMES + 1) * ROWS, COLS), F32)
-    send_a, send_b, x, rim = call(own_kernel, [send, send, tile, rim], 1, [rows])(video)
+    rows = (((FRAMES + 1) * ROWS, COLS), F32)
+    rows, send_a, send_b = call(send_kernel, [rows, send, send], 1)(video)
     got_a = lax.ppermute(send_a, "row", near)
     got_b = lax.ppermute(send_b, "row", far)
+    outs = [tile, rim, ((96, 3 * HALF), BF16), ((32, 3 * HALF), BF16)]
+    x, rim, side, diag = call(own_kernel, outs, 2)(rows, got_a)
+    side = lax.ppermute(side, "col", to_left)
+    diag = lax.ppermute(diag, ("row", "col"), across)
 
     (band,) = call(band_kernel, [((128, 256), BF16)], 1, [pltpu.VMEM((16, 128), F32)])(
         jnp.transpose(filters, (0, 2, 1, 3))
     )
-    x, side = call(halo_kernel, [tile, ((112, 3 * HALF), BF16)], 5)(got_a, got_b, x, rim, band)
-    side = lax.ppermute(side, "col", to_left)
+    (x,) = call(halo_kernel, [tile], 5)(got_a, got_b, x, rim, band)
     feats_shape = ((BLOCKS, 16, FRAMES), BF16)
     inner, first = call(inner_kernel, [feats_shape, ((16, FRAMES), BF16)], 2)(band, x)
     part = ((SUMMED + 16, HALF), F32)
-    feats, mine, other = call(edge_kernel, [feats_shape, part, part], 5)(band, x, side, inner, first)
+    feats, mine, other = call(edge_kernel, [feats_shape, part, part], 6)(band, x, side, diag, inner, first)
 
     mine = mine + lax.ppermute(other, "row", near)
     summed = lax.broadcasted_iota(jnp.int32, mine.shape, 0) < SUMMED

time: 41.8 us -> 40.1 us (0.959)
  starting transfers between devices: 14.5 us -> 13.7 us
  waiting for transfers between devices: 12.7 us -> 11.9 us
  local copies, waits for them, and re-layouts: 1.78 us -> 1.05 us
    ppermute x1, starting transfers between devices: 5.22 us -> 3.7 us  [on_device(): mine = mine + lax.ppermute(other, 'row', near)]
    ppermute x2, starting transfers between devices: 4.3 us -> 5.57 us  [on_device(): got = lax.ppermute(mine, 'col', [(i, i ^ step) for i in range(size_col)])]
    ppermute x1, starting transfers between devices: 2.44 us -> 1.22 us  [on_device(): got = lax.ppermute(mine, 'row', [(i, i ^ step) for i in range(size_row)])]
    ppermute x1, waiting for transfers between devices: 2.61 us -> 1.4 us  [on_device(): side = lax.ppermute(side, 'col', to_left)]
    ppermute x1, waiting for transfers between devices: 2.67 us -> 3.45 us  [on_device(): got = lax.ppermute(mine, 'row', [(i, i ^ step) for i in range(size_row)])]
    ppermute x2, waiting for transfers between devices: 5.26 us -> 4.49 us  [on_device(): got = lax.ppermute(mine, 'col', [(i, i ^ step) for i in range(size_col)])]
    unnamed x6, local copies, waits for them, and re-layouts: 1.78 us -> 1.05 us
    ppermute x0 -> x1, starting transfers between devices: none -> 0.66 us  [on_device(): diag = lax.ppermute(diag, ('row', 'col'), across)]
  transfers between devices with their start and end apart: 8 -> 9, of which waited for: 6 -> 7; matrix products, arithmetic and copies ran while one was open for 0% -> 0% of each run, Pallas kernels for 9% -> 12%
where the time goes in v5:
time: 40.1 us; the launch traced here: 39.5 us
  starting transfers between devices  13.7 us (34%)
  waiting for transfers between devices  11.9 us (30%)
  Pallas kernels  11.8 us (29%)
  local copies, waits for them, and re-layouts  1.05 us (3%)
  between operations  0.77 us (2%)
    pallas_call x1, Pallas kernels, on_device(): call(kernel, [((MODES, FRAMES), F32), ((ROWS // 4, COLS // 4, ORIENT * MO...  6.31 us
    ppermute x2, starting transfers between devices, on_device(): got = lax.ppermute(mine, 'col', [(i, i ^ step) for i in range(size_col)])  5.57 us
    ppermute x2, waiting for transfers between devices, on_device(): got = lax.ppermute(mine, 'col', [(i, i ^ step) for i in range(size_col)])  4.49 us
    ppermute x1, starting transfers between devices, on_device(): mine = mine + lax.ppermute(other, 'row', near)  3.7 us
    ppermute x1, waiting for transfers between devices, on_device(): got = lax.ppermute(mine, 'row', [(i, i ^ step) for i in range(size_row)])  3.45 us
    pallas_call x1, Pallas kernels, on_device(): call(inner_kernel, [feats_shape, ((16, FRAMES), BF16)], 2)(band, x)  3.07 us
    ppermute x1, waiting for transfers between devices, on_device(): side = lax.ppermute(side, 'col', to_left)  1.4 us
    ppermute x1, starting transfers between devices, on_device(): side = lax.ppermute(side, 'col', to_left)  1.29 us
  transfers between devices with their start and end apart: 9, of which 7 were waited for; matrix products, arithmetic and copies ran while one was open for 0% of the time, Pallas kernels for 12%

profile of v5, /device:TPU:0, one launch (start us, length us, event | category | flops | bytes accessed | tf_op | source)
XLA Modules:
  0.0 39.5 jit_solution(18062236483517339823)
XLA Ops:
  0.6 0.0 copy-start
  0.6 1.0 %copy-done = bf16[257,8,128]{2,1,0:T(8,128)(2,1)S(1)} copy-done((bf16[257,8,128]{2,1,0:T(8,128)(2,1)S(1)}, bf16[257,8,128]{2,1,0:T(8,128)(2,1)}, u32[]{:S(2)}) %copy-start) | copy-done | bytes 526360
  1.7 0.0 copy-start.2
  1.7 0.4 shard_map.51
  2.0 0.5 %collective-permute-start = (bf16[400,256]{1,0:T(8,128)(2,1)S(1)}, bf16[400,256]{1,0:T(8,128)(2,1)S(1)}, u32[]{:S(2)}, u32[]{:S(2)}) collective-permute-start(bf16[400,256]{1,0:T(8,128)(2,1)S(1)} %get-tuple-element.18), channel_id=1, source_target_pairs={{0,4},{4,0},{8,12},{12,8},{1,5},{5,1},{9,13},{13,9},{2,6},{6,2},{1... | collective-permute-start | bytes 614408 | tf_op jit(solution)/shard_map/ppermute | solution.py:320
  2.6 0.7 %collective-permute-start.1 = (bf16[400,256]{1,0:T(8,128)(2,1)S(1)}, bf16[400,256]{1,0:T(8,128)(2,1)S(1)}, u32[]{:S(2)}, u32[]{:S(2)}) collective-permute-start(bf16[400,256]{1,0:T(8,128)(2,1)S(1)} %get-tuple-element.19), channel_id=1, source_target_pairs={{4,8},{8,4},{5,9},{9,5},{6,10},{10,6},{7,11},{11,7},{20,24},{24,20... | collective-permute-start | bytes 614408 | tf_op jit(solution)/shard_map/ppermute | solution.py:321
  3.2 0.4 %collective-permute-done.a_ref = bf16[400,256]{1,0:T(8,128)(2,1)S(1)} collective-permute-done((bf16[400,256]{1,0:T(8,128)(2,1)S(1)}, bf16[400,256]{1,0:T(8,128)(2,1)S(1)}, u32[]{:S(2)}, u32[]{:S(2)}) %collective-permute-start) | collective-permute-done | bytes 204832 | tf_op jit(solution)/shard_map/ppermute | solution.py:320
  3.6 0.6 %shard_map.52 = (bf16[16,112,384]{2,1,0:T(8,128)(2,1)S(1)}, f32[2,128,384]{2,1,0:T(8,128)S(1)}, bf16[96,384]{1,0:T(8,128)(2,1)S(1)}, bf16[32,384]{1,0:T(8,128)(2,1)S(1)}) custom-call(f32[2056,128]{1,0:T(8,128)S(1)} %get-tuple-element.20.rows_ref, bf16[400,256]{1,0:T(8,128)(2,1)S(1)} %collective-permute-done.a_ref), custom_call_target="tpu_custom_call" | custom-call | tf_op jit(solution)/shard_map/pallas_call | solution.py:323
  4.2 1.3 %collective-permute-start.2 = (bf16[96,384]{1,0:T(8,128)(2,1)S(1)}, bf16[96,384]{1,0:T(8,128)(2,1)S(1)}, u32[]{:S(2)}, u32[]{:S(2)}) collective-permute-start(bf16[96,384]{1,0:T(8,128)(2,1)S(1)} %get-tuple-element.23), channel_id=1, source_target_pairs={{1,0},{2,1},{3,2},{5,4},{6,5},{7,6},{9,8},{10,9},{11,10},{13,12},{... | collective-permute-start | bytes 221192 | tf_op jit(solution)/shard_map/ppermute | solution.py:324
  5.5 0.7 %collective-permute-start.3 = (bf16[32,384]{1,0:T(8,128)(2,1)S(1)}, bf16[32,384]{1,0:T(8,128)(2,1)S(1)}, u32[]{:S(2)}, u32[]{:S(2)}) collective-permute-start(bf16[32,384]{1,0:T(8,128)(2,1)S(1)} %get-tuple-element.24), channel_id=1, source_target_pairs={{5,8},{6,9},{7,10},{9,4},{10,5},{11,6},{21,24},{22,25},{23,26},{25... | collective-permute-start | bytes 73736 | tf_op jit(solution)/shard_map/ppermute | solution.py:325
  6.2 0.0 copy-done.2
  6.2 0.4 shard_map.50.band_ref
  6.6 0.0 collective-permute-done.1.b_ref
  6.6 0.3 shard_map.53.x_ref
  6.9 3.1 %shard_map.54 = (bf16[16,16,256]{2,1,0:T(8,128)(2,1)S(1)}, bf16[16,256]{1,0:T(8,128)(2,1)S(1)}) custom-call(bf16[128,256]{1,0:T(8,128)(2,1)S(1)} %shard_map.50.band_ref, bf16[16,112,384]{2,1,0:T(8,128)(2,1)S(1)} %shard_map.53.x_ref), custom_call_target="tpu_custom_call" | custom-call | tf_op jit(solution)/shard_map/pallas_call | solution.py:332
  10.0 0.0 copy-start.1
  10.0 0.0 collective-permute-done.3.diag_ref
  10.0 1.4 %collective-permute-done.2.side_ref = bf16[96,384]{1,0:T(8,128)(2,1)S(1)} collective-permute-done((bf16[96,384]{1,0:T(8,128)(2,1)S(1)}, bf16[96,384]{1,0:T(8,128)(2,1)S(1)}, u32[]{:S(2)}, u32[]{:S(2)}) %collective-permute-start.2) | collective-permute-done | bytes 73760 | tf_op jit(solution)/shard_map/ppermute | solution.py:324
  11.4 0.6 %shard_map.55 = (bf16[16,16,256]{2,1,0:T(8,128)(2,1)S(1)}, f32[152,128]{1,0:T(8,128)S(1)}, f32[152,128]{1,0:T(8,128)S(1)}) custom-call(bf16[128,256]{1,0:T(8,128)(2,1)S(1)} %shard_map.50.band_ref, bf16[16,112,384]{2,1,0:T(8,128)(2,1)S(1)} %shard_map.53.x_ref, bf16[96,384]{1,0:T(8,128)(2,1)S(1)} %collective-permute-done.2.side_ref, ...), custom_call_target="tpu_custom_call" | custom-call | tf_op jit(solution)/shard_map/pallas_call | solution.py:334
  12.0 3.7 %collective-permute-start.4 = (f32[152,128]{1,0:T(8,128)S(1)}, f32[152,128]{1,0:T(8,128)S(1)}, u32[]{:S(2)}, u32[]{:S(2)}) collective-permute-start(f32[152,128]{1,0:T(8,128)S(1)} %get-tuple-element.28), channel_id=1, source_target_pairs={{0,4},{4,0},{8,12},{12,8},{1,5},{5,1},{9,13},{13,9},{2,6},{6,2},{1... | collective-permute-start | bytes 233480 | tf_op jit(solution)/shard_map/ppermute | solution.py:336
  15.7 0.9 %collective-permute-done.4 = f32[152,128]{1,0:T(8,128)S(1)} collective-permute-done((f32[152,128]{1,0:T(8,128)S(1)}, f32[152,128]{1,0:T(8,128)S(1)}, u32[]{:S(2)}, u32[]{:S(2)}) %collective-permute-start.4) | collective-permute-done | bytes 77856 | tf_op jit(solution)/shard_map/ppermute | solution.py:336
  16.6 1.2 %collective-permute-start.5 = (f32[152,128]{1,0:T(8,128)S(1)}, f32[152,128]{1,0:T(8,128)S(1)}, u32[]{:S(2)}, u32[]{:S(2)}) collective-permute-start(f32[152,128]{1,0:T(8,128)S(1)} %add.12), channel_id=1, source_target_pairs={{0,8},{4,12},{8,0},{12,4},{1,9},{5,13},{9,1},{13,5},{2,10},{6,14},... | collective-permute-start | bytes 233480 | tf_op jit(solution)/shard_map/ppermute | solution.py:340
  17.8 3.5 %collective-permute-done.5 = f32[152,128]{1,0:T(8,128)S(1)} collective-permute-done((f32[152,128]{1,0:T(8,128)S(1)}, f32[152,128]{1,0:T(8,128)S(1)}, u32[]{:S(2)}, u32[]{:S(2)}) %collective-permute-start.5) | collective-permute-done | bytes 77856 | tf_op jit(solution)/shard_map/ppermute | solution.py:340
  21.3 0.1 add_select_fusion.2
  21.4 2.4 %collective-permute-start.6 = (f32[152,128]{1,0:T(8,128)S(1)}, f32[152,128]{1,0:T(8,128)S(1)}, u32[]{:S(2)}, u32[]{:S(2)}) collective-permute-start(f32[152,128]{1,0:T(8,128)S(1)} %add_select_fusion.2), channel_id=1, source_target_pairs={{0,1},{1,0},{2,3},{3,2},{4,5},{5,4},{6,7},{7,6},{8,9},{9,8},{10,11... | collective-permute-start | bytes 233480 | tf_op jit(solution)/shard_map/ppermute | solution.py:351
  23.8 2.4 %collective-permute-done.6 = f32[152,128]{1,0:T(8,128)S(1)} collective-permute-done((f32[152,128]{1,0:T(8,128)S(1)}, f32[152,128]{1,0:T(8,128)S(1)}, u32[]{:S(2)}, u32[]{:S(2)}) %collective-permute-start.6) | collective-permute-done | bytes 77856 | tf_op jit(solution)/shard_map/ppermute | solution.py:351
  26.2 0.1 add_select_fusion.1
  26.3 3.1 %collective-permute-start.7 = (f32[152,128]{1,0:T(8,128)S(1)}, f32[152,128]{1,0:T(8,128)S(1)}, u32[]{:S(2)}, u32[]{:S(2)}) collective-permute-start(f32[152,128]{1,0:T(8,128)S(1)} %add_select_fusion.1), channel_id=1, source_target_pairs={{0,2},{1,3},{2,0},{3,1},{4,6},{5,7},{6,4},{7,5},{8,10},{9,11},{10,... | collective-permute-start | bytes 233480 | tf_op jit(solution)/shard_map/ppermute | solution.py:351
  29.4 0.0 copy-done.1
  29.4 0.3 shard_map.56.start_ref
  29.7 2.1 %collective-permute-done.7 = f32[152,128]{1,0:T(8,128)S(1)} collective-permute-done((f32[152,128]{1,0:T(8,128)S(1)}, f32[152,128]{1,0:T(8,128)S(1)}, u32[]{:S(2)}, u32[]{:S(2)}) %collective-permute-start.7) | collective-permute-done | bytes 77856 | tf_op jit(solution)/shard_map/ppermute | solution.py:351
  31.8 0.1 add_select_fusion.mine_ref
  31.9 0.1 collective-permute-start.8
  32.0 1.2 %collective-permute-done.8.other_ref = f32[152,128]{1,0:T(8,128)S(1)} collective-permute-done((f32[152,128]{1,0:T(8,128)S(1)}, f32[152,128]{1,0:T(8,128)S(1)}, u32[]{:S(2)}, u32[]{:S(2)}) %collective-permute-start.8) | collective-permute-done | bytes 77856 | tf_op jit(solution)/shard_map/ppermute | solution.py:355
  33.2 6.3 %shard_map.57 = (f32[64,256]{1,0:T(8,128)}, f32[2,32,256]{2,1,0:T(8,128)}) custom-call(f32[152,128]{1,0:T(8,128)S(1)} %add_select_fusion.mine_ref, f32[152,128]{1,0:T(8,128)S(1)} %collective-permute-done.8.other_ref, f32[64,256]{1,0:T(8,128)S(1)} %shard_map.56.start_ref, bf16[16,16,256]{2,1,0:T(8,128)(2,1)S(1)} %get-tuple-element.31.feats_ref, ...), custom_call_target="tpu_custom_call" | custom-call | tf_op jit(solution)/shard_map/pallas_call | solution.py:359
  (3 shorter events, 0.0 us)
Async XLA Ops:
  0.6 1.0 %copy-start = (bf16[257,8,128]{2,1,0:T(8,128)(2,1)S(1)}, bf16[257,8,128]{2,1,0:T(8,128)(2,1)}, u32[]{:S(2)}) copy-start(bf16[257,8,128]{2,1,0:T(8,128)(2,1)} %video_ref.1) | copy-start | bytes 1579012
  1.7 4.5 %copy-start.2 = (f32[4,2,7,7]{3,1,2,0:T(2,128)S(1)}, f32[4,2,7,7]{3,1,2,0:T(2,128)}, u32[]{:S(2)}) copy-start(f32[4,2,7,7]{3,1,2,0:T(2,128)} %param.4) | copy-start | bytes 4708
  2.0 1.6 %collective-permute-start = (bf16[400,256]{1,0:T(8,128)(2,1)S(1)}, bf16[400,256]{1,0:T(8,128)(2,1)S(1)}, u32[]{:S(2)}, u32[]{:S(2)}) collective-permute-start(bf16[400,256]{1,0:T(8,128)(2,1)S(1)} %get-tuple-element.18), channel_id=1, source_target_pairs={{0,4},{4,0},{8,12},{12,8},{1,5},{5,1},{9,13},{13,9},{2,6},{6,2},{1... | collective-permute-start | bytes 614408 | tf_op jit(solution)/shard_map/ppermute | solution.py:320
  2.6 4.0 %collective-permute-start.1 = (bf16[400,256]{1,0:T(8,128)(2,1)S(1)}, bf16[400,256]{1,0:T(8,128)(2,1)S(1)}, u32[]{:S(2)}, u32[]{:S(2)}) collective-permute-start(bf16[400,256]{1,0:T(8,128)(2,1)S(1)} %get-tuple-element.19), channel_id=1, source_target_pairs={{4,8},{8,4},{5,9},{9,5},{6,10},{10,6},{7,11},{11,7},{20,24},{24,20... | collective-permute-start | bytes 614408 | tf_op jit(solution)/shard_map/ppermute | solution.py:321
  4.2 7.2 %collective-permute-start.2 = (bf16[96,384]{1,0:T(8,128)(2,1)S(1)}, bf16[96,384]{1,0:T(8,128)(2,1)S(1)}, u32[]{:S(2)}, u32[]{:S(2)}) collective-permute-start(bf16[96,384]{1,0:T(8,128)(2,1)S(1)} %get-tuple-element.23), channel_id=1, source_target_pairs={{1,0},{2,1},{3,2},{5,4},{6,5},{7,6},{9,8},{10,9},{11,10},{13,12},{... | collective-permute-start | bytes 221192 | tf_op jit(solution)/shard_map/ppermute | solution.py:324
  5.5 4.5 %collective-permute-start.3 = (bf16[32,384]{1,0:T(8,128)(2,1)S(1)}, bf16[32,384]{1,0:T(8,128)(2,1)S(1)}, u32[]{:S(2)}, u32[]{:S(2)}) collective-permute-start(bf16[32,384]{1,0:T(8,128)(2,1)S(1)} %get-tuple-element.24), channel_id=1, source_target_pairs={{5,8},{6,9},{7,10},{9,4},{10,5},{11,6},{21,24},{22,25},{23,26},{25... | collective-permute-start | bytes 73736 | tf_op jit(solution)/shard_map/ppermute | solution.py:325
  10.0 19.5 %copy-start.1 = (f32[256,64]{0,1:T(8,128)S(1)}, f32[256,64]{0,1:T(8,128)}, u32[]{:S(2)}) copy-start(f32[256,64]{0,1:T(8,128)} %param.5) | copy-start | bytes 196612
  12.0 4.6 %collective-permute-start.4 = (f32[152,128]{1,0:T(8,128)S(1)}, f32[152,128]{1,0:T(8,128)S(1)}, u32[]{:S(2)}, u32[]{:S(2)}) collective-permute-start(f32[152,128]{1,0:T(8,128)S(1)} %get-tuple-element.28), channel_id=1, source_target_pairs={{0,4},{4,0},{8,12},{12,8},{1,5},{5,1},{9,13},{13,9},{2,6},{6,2},{1... | collective-permute-start | bytes 233480 | tf_op jit(solution)/shard_map/ppermute | solution.py:336
  16.6 4.7 %collective-permute-start.5 = (f32[152,128]{1,0:T(8,128)S(1)}, f32[152,128]{1,0:T(8,128)S(1)}, u32[]{:S(2)}, u32[]{:S(2)}) collective-permute-start(f32[152,128]{1,0:T(8,128)S(1)} %add.12), channel_id=1, source_target_pairs={{0,8},{4,12},{8,0},{12,4},{1,9},{5,13},{9,1},{13,5},{2,10},{6,14},... | collective-permute-start | bytes 233480 | tf_op jit(solution)/shard_map/ppermute | solution.py:340
  21.4 4.8 %collective-permute-start.6 = (f32[152,128]{1,0:T(8,128)S(1)}, f32[152,128]{1,0:T(8,128)S(1)}, u32[]{:S(2)}, u32[]{:S(2)}) collective-permute-start(f32[152,128]{1,0:T(8,128)S(1)} %add_select_fusion.2), channel_id=1, source_target_pairs={{0,1},{1,0},{2,3},{3,2},{4,5},{5,4},{6,7},{7,6},{8,9},{9,8},{10,11... | collective-permute-start | bytes 233480 | tf_op jit(solution)/shard_map/ppermute | solution.py:351
  26.3 5.5 %collective-permute-start.7 = (f32[152,128]{1,0:T(8,128)S(1)}, f32[152,128]{1,0:T(8,128)S(1)}, u32[]{:S(2)}, u32[]{:S(2)}) collective-permute-start(f32[152,128]{1,0:T(8,128)S(1)} %add_select_fusion.1), channel_id=1, source_target_pairs={{0,2},{1,3},{2,0},{3,1},{4,6},{5,7},{6,4},{7,5},{8,10},{9,11},{10,... | collective-permute-start | bytes 233480 | tf_op jit(solution)/shard_map/ppermute | solution.py:351
  31.9 1.3 %collective-permute-start.8 = (f32[152,128]{1,0:T(8,128)S(1)}, f32[152,128]{1,0:T(8,128)S(1)}, u32[]{:S(2)}, u32[]{:S(2)}) collective-permute-start(f32[152,128]{1,0:T(8,128)S(1)} %add_select_fusion.mine_ref), channel_id=1, source_target_pairs={{0,4},{4,0},{8,12},{12,8},{1,5},{5,1},{9,13},{13,9},{2,6},{6,2},{1... | collective-permute-start | bytes 233480 | tf_op jit(solution)/shard_map/ppermute | solution.py:355

commit v6 on v5

--- a/solution.py
+++ b/solution.py
@@ -18,6 +18,7 @@
 COLS = 128
 SUMMED = HALF + 8
 BLOCKS = 16
+UNROLL = 4
 F32 = jnp.float32
 BF16 = jnp.bfloat16
 HIGHEST = lax.Precision.HIGHEST
@@ -124,18 +125,19 @@
     return jnp.where(frame == 2 * (lane & (HALF - 1)) + (lane >> 7), 1.0, 0.0).astype(F32)
 
 
-def halo_kernel(a_ref, b_ref, x_in_ref, rim_ref, band_ref, x_ref):
+def place_halo(a_ref, b_ref, x_in_ref, rim_ref, x_ref):
     even = is_even("row")
     got_a, got_b = a_ref[...], b_ref[...]
     above = expanded(jnp.where(even, got_b, got_a).astype(F32), COLS)
     below = expanded(jnp.where(even, got_a, got_b).astype(F32), COLS)
     for group in range(3):
         lanes = slice(HALF * group, HALF * group + HALF)
-        x_ref[:, 0:16, lanes] = blocked(above[0][group], above[1][group])
-        x_ref[:, 16:32, lanes] = blocked(above[2][group], rim_ref[0, :, lanes])
-        x_ref[:, 80:96, lanes] = blocked(rim_ref[1, :, lanes], below[0][group])
-        x_ref[:, 96:112, lanes] = blocked(below[1][group], below[2][group])
-    x_ref[:, 32:80, :] = x_in_ref[:, 32:80, :]
+        x_ref[1:, 0:16, lanes] = blocked(above[0][group], above[1][group])
+        x_ref[1:, 16:32, lanes] = blocked(above[2][group], rim_ref[0, :, lanes])
+        x_ref[1:, 80:96, lanes] = blocked(rim_ref[1, :, lanes], below[0][group])
+        x_ref[1:, 96:112, lanes] = blocked(below[1][group], below[2][group])
+    x_ref[1:, 32:80, :] = x_in_ref[:, 32:80, :]
+    x_ref[0] = jnp.zeros((112, 3 * HALF), BF16)
 
 
 def block_feats(band_ref, left, right):
@@ -170,31 +172,30 @@
     return (lax.broadcasted_iota(jnp.int32, (16, FRAMES), 0) & 4) == 4
 
 
-def inner_kernel(band_ref, x_ref, feats_ref, start_ref):
+def inner_kernel(a_ref, b_ref, x_in_ref, rim_ref, band_ref, feats_ref, x_ref):
+    place_halo(a_ref, b_ref, x_in_ref, rim_ref, x_ref)
+
     def body(step, carry):
-        for i in range(3):
-            block = 3 * step + i
+        for i in range(UNROLL):
+            block = UNROLL * step + i
             feats_ref[block] = block_feats(band_ref, x_ref[block], x_ref[block + 1]).astype(BF16)
         return carry
 
-    lax.fori_loop(0, (BLOCKS - 1) // 3, body, 0)
-    start = block_feats(band_ref, jnp.zeros((112, 3 * HALF), BF16), x_ref[0])
+    lax.fori_loop(0, BLOCKS // UNROLL, body, 0)
     begins = lax.axis_index("col") == 0
-    start_ref[...] = jnp.where(second_cells() & begins, start, 0.0).astype(BF16)
-
-
-def edge_kernel(band_ref, x_ref, side_ref, diag_ref, inner_ref, start_ref, feats_ref, mine_ref, other_ref):
+    feats_ref[0] = jnp.where(second_cells() & begins, feats_ref[0].astype(F32), 0.0).astype(BF16)
+
+
+def edge_kernel(band_ref, x_ref, side_ref, diag_ref, inner_ref, edge_ref, mine_ref, other_ref, passed_ref):
     even = is_even("row")
     side = side_ref[...].astype(F32)
     near, far = side[8 * ROWS : 8 * ROWS + 8 * REACH], diag_ref[...].astype(F32)[: 8 * REACH]
     rows = [jnp.where(even, far, near), side[: 8 * ROWS], jnp.where(even, near, far)]
-    edge = block_feats(band_ref, x_ref[BLOCKS - 1], jnp.concatenate(rows, axis=0).astype(BF16))
+    edge = block_feats(band_ref, x_ref[BLOCKS], jnp.concatenate(rows, axis=0).astype(BF16))
     ends = lax.axis_index("col") == lax.axis_size("col") - 1
-    feats_ref[0 : BLOCKS - 1] = inner_ref[0 : BLOCKS - 1]
     edge = jnp.where(second_cells() & ends, 0.0, edge).astype(BF16)
-    feats_ref[BLOCKS - 1] = edge
-    edge = edge.astype(F32)
-    flat = jnp.concatenate([feats_ref[...].reshape(16 * BLOCKS, FRAMES), start_ref[...]], axis=0)
+    edge_ref[...] = edge
+    flat = jnp.concatenate([inner_ref[...].reshape(16 * BLOCKS, FRAMES), edge], axis=0)
     gram = lax.dot_general(flat, flat, (((0,), (0,)), ((), ())), preferred_element_type=F32)
     top, cross, low = gram[:HALF, :HALF], gram[:HALF, HALF:], gram[HALF:, HALF:]
     i = lax.broadcasted_iota(jnp.int32, (HALF, HALF), 0)
@@ -205,12 +206,12 @@
     spare = jnp.broadcast_to(diagonal, (8, HALF))
     mine_ref[0:HALF] = jnp.where(first, cross, folded)
     mine_ref[HALF:SUMMED] = spare
-    passed = jnp.where(second_cells()[:8], edge[:8], pltpu.roll(edge[8:], 4, 0))
-    mine_ref[SUMMED : SUMMED + 8] = passed[:, :HALF]
-    mine_ref[SUMMED + 8 : SUMMED + 16] = passed[:, HALF:]
     other_ref[0:HALF] = jnp.where(first, folded, cross)
     other_ref[HALF:SUMMED] = spare
-    other_ref[SUMMED : SUMMED + 16] = jnp.zeros((16, HALF), F32)
+    edge = edge.astype(F32)
+    passed = jnp.where(second_cells()[:8], edge[:8], pltpu.roll(edge[8:], 4, 0))
+    passed_ref[0:8] = passed[:, :HALF]
+    passed_ref[8:16] = passed[:, HALF:]
 
 
 def inverse_factor(inner):
@@ -221,28 +222,42 @@
     work = jnp.concatenate([jnp.where(i == j, 1.0, 0.0), inner], axis=1)
     work = [work[8 * v : 8 * v + 8] for v in range(count)]
     sub = lax.broadcasted_iota(jnp.int32, shape, 0)
+
+    def columns(b):
+        lanes = [MODES + 8 * b + m for m in range(8)]
+        return {v: [jnp.broadcast_to(work[v][:, k : k + 1], shape) for k in lanes] for v in range(b, count)}
+
+    def spread(tile, row):
+        return jnp.broadcast_to(tile[row : row + 1], shape)
+
+    cols = columns(0)
     done = []
     for b in range(count):
-        lane = MODES + 8 * b
-        cols = [[jnp.broadcast_to(work[v][:, lane + m : lane + m + 1], shape) for v in range(b, count)] for m in range(8)]
+        ahead = columns(b + 1)
         scale = jnp.zeros(shape, F32)
         for m in range(8):
-            lead = cols[m][0]
-            pivot = jnp.broadcast_to(lead[m : m + 1], shape)
+            lead = cols[b][m]
+            pivot = spread(lead, m)
             inverse = 1.0 / pivot
             scale = jnp.where(sub == m, lax.rsqrt(pivot), scale)
-            row = jnp.broadcast_to(work[b][m : m + 1], shape) * inverse
+            row = spread(work[b], m) * inverse
             for q in range(m + 1, 8):
-                times = jnp.broadcast_to(lead[q : q + 1], shape) * inverse
-                cols[q] = [c - d * times for c, d in zip(cols[q], cols[m])]
+                times = spread(lead, q) * inverse
+                for v in cols:
+                    cols[v][q] = cols[v][q] - cols[v][m] * times
+            for q in range(8 if ahead else 0):
+                times = spread(cols[b + 1][m], q) * inverse
+                for v in ahead:
+                    ahead[v][q] = ahead[v][q] - cols[v][m] * times
             work[b] = work[b] - jnp.where(sub > m, lead, 0.0) * row
             for v in range(b + 1, count):
-                work[v] = work[v] - cols[m][v - b] * row
+                work[v] = work[v] - cols[v][m] * row
         done.append(work[b] * scale)
+        cols = ahead
     return jnp.concatenate(done, axis=0)[:, :MODES]
 
 
-def basis_kernel(scale, mine_ref, other_ref, start_ref, feats_ref, first_ref, before_ref, basis_ref, modes_ref, rows_ref, out_ref):
+def basis_kernel(scale, mine_ref, other_ref, start_ref, inner_ref, edge_ref, before_ref, basis_ref, modes_ref, rows_ref, out_ref):
     first = is_even("row")
     mine, other = mine_ref[...], other_ref[...]
     cross = jnp.where(first, mine, other)[:HALF]
@@ -268,9 +283,9 @@
     twice = jnp.concatenate([basis, basis], axis=0)
     before = jnp.concatenate([before_ref[:8], before_ref[8:]], axis=1)
     before = jnp.concatenate([before, pltpu.roll(before, 4, 0)], axis=0)
-    before = jnp.where(lax.axis_index("col") == 0, first_ref[...].astype(F32), before)
-    cell = jnp.where(second_cells(), before, feats_ref[BLOCKS - 1].astype(F32)).astype(BF16)
-    flat = jnp.concatenate([feats_ref[0 : BLOCKS - 1].reshape(16 * BLOCKS - 16, FRAMES), cell], axis=0)
+    before = jnp.where(lax.axis_index("col") == 0, inner_ref[0].astype(F32), before)
+    cell = jnp.where(second_cells(), before, edge_ref[...].astype(F32)).astype(BF16)
+    flat = jnp.concatenate([inner_ref[1:].reshape(16 * BLOCKS - 16, FRAMES), cell], axis=0)
     rows_ref[...] = lax.dot_general(
         flat, twice.astype(BF16), (((1,), (1,)), ((), ())), preferred_element_type=F32
     )
@@ -314,6 +329,7 @@
     across = [(a * size_col + i, b * size_col + j) for a, b in far for i, j in to_left]
     send = ((REACH * COLS + 16, FRAMES), BF16)
     tile = ((BLOCKS, 112, 3 * HALF), BF16)
+    tiles = ((BLOCKS + 1, 112, 3 * HALF), BF16)
     rim = ((2, COLS, 3 * HALF), F32)
     rows = (((FRAMES + 1) * ROWS, COLS), F32)
     rows, send_a, send_b = call(send_kernel, [rows, send, send], 1)(video)
@@ -327,19 +343,19 @@
     (band,) = call(band_kernel, [((128, 256), BF16)], 1, [pltpu.VMEM((16, 128), F32)])(
         jnp.transpose(filters, (0, 2, 1, 3))
     )
-    (x,) = call(halo_kernel, [tile], 5)(got_a, got_b, x, rim, band)
-    feats_shape = ((BLOCKS, 16, FRAMES), BF16)
-    inner, first = call(inner_kernel, [feats_shape, ((16, FRAMES), BF16)], 2)(band, x)
-    part = ((SUMMED + 16, HALF), F32)
-    feats, mine, other = call(edge_kernel, [feats_shape, part, part], 6)(band, x, side, diag, inner, first)
+    inner, x = call(inner_kernel, [((BLOCKS, 16, FRAMES), BF16), tiles], 5)(got_a, got_b, x, rim, band)
+    part, passed = ((SUMMED, HALF), F32), ((16, HALF), F32)
+    edge, mine, other, passed = call(edge_kernel, [((16, FRAMES), BF16), part, part, passed], 5)(
+        band, x, side, diag, inner
+    )
 
     mine = mine + lax.ppermute(other, "row", near)
-    summed = lax.broadcasted_iota(jnp.int32, mine.shape, 0) < SUMMED
     step = 2
     while step < size_row:
-        got = lax.ppermute(mine, "row", [(i, i ^ step) for i in range(size_row)])
-        mine = jnp.where(summed, mine + got, mine)
+        mine = mine + lax.ppermute(mine, "row", [(i, i ^ step) for i in range(size_row)])
         step *= 2
+    mine = jnp.concatenate([mine, passed], axis=0)
+    summed = lax.broadcasted_iota(jnp.int32, mine.shape, 0) < SUMMED
     step = 1
     col = lax.axis_index("col")
     before = jnp.zeros((16, HALF), F32)
@@ -352,6 +368,7 @@
         mine = jnp.where(summed, mine + got, got)
         before = jnp.where((col & (2 * step - 1)) == step, got[SUMMED:], before)
         step *= 2
+    mine = mine[:SUMMED]
     other = lax.ppermute(mine, "row", near)
 
     features = ORIENT * (size_row * ROWS // 4) * (size_col * COLS // 4)
@@ -361,7 +378,7 @@
         [((MODES, FRAMES), F32), ((ROWS // 4, COLS // 4, ORIENT * MODES), F32)],
         6,
         [pltpu.VMEM((FRAMES, 2 * MODES), F32), pltpu.VMEM((128, 128), F32)],
-    )(mine, other, start, feats, first, before)
+    )(mine, other, start, inner, edge, before)
     return basis.T, modes
 
 

time: 40.1 us -> 38.5 us (0.960)
  Pallas kernels: 11.8 us -> 10.5 us
    pallas_call x1, Pallas kernels: 6.31 us -> 5.36 us  [on_device(): call(kernel, [((MODES, FRAMES), F32), ((ROWS // 4, COLS // 4, ORIENT * MO...]
    pallas_call x3 -> x2, Pallas kernels: 3.95 us -> 3.54 us  [the longest x1 2.98 us: on_device(): call(inner_kernel, [((BLOCKS, 16, FRAMES), BF16), tiles], 5)]
    ppermute x1, waiting for transfers between devices: 1.4 us -> 1.8 us  [on_device(): side = lax.ppermute(side, 'col', to_left)]
  transfers between devices with their start and end apart: 9 -> 9, of which waited for: 7 -> 7; matrix products, arithmetic and copies ran while one was open for 0% -> 0% of each run, Pallas kernels for 12% -> 11%
where the time goes in v6:
time: 38.5 us; the launch traced here: 38.3 us
  starting transfers between devices  13.6 us (35%)
  waiting for transfers between devices  12.1 us (31%)
  Pallas kernels  10.5 us (27%)
  local copies, waits for them, and re-layouts  1.05 us (3%)
  between operations  0.77 us (2%)
    ppermute x2, starting transfers between devices, on_device(): got = lax.ppermute(mine, 'col', [(i, i ^ step) for i in range(size_col)])  5.53 us
    pallas_call x1, Pallas kernels, on_device(): call(kernel, [((MODES, FRAMES), F32), ((ROWS // 4, COLS // 4, ORIENT * MO...  5.36 us
    ppermute x2, waiting for transfers between devices, on_device(): got = lax.ppermute(mine, 'col', [(i, i ^ step) for i in range(size_col)])  4.48 us
    ppermute x1, starting transfers between devices, on_device(): mine = mine + lax.ppermute(other, 'row', near)  3.7 us
    ppermute x1, waiting for transfers between devices, on_device(): lax.ppermute(mine, 'row', [(i, i ^ step) for i in range(size_row)])  3.29 us
    pallas_call x1, Pallas kernels, on_device(): call(inner_kernel, [((BLOCKS, 16, FRAMES), BF16), tiles], 5)  2.98 us
    ppermute x1, waiting for transfers between devices, on_device(): side = lax.ppermute(side, 'col', to_left)  1.8 us
    ppermute x1, starting transfers between devices, on_device(): side = lax.ppermute(side, 'col', to_left)  1.29 us
  transfers between devices with their start and end apart: 9, of which 7 were waited for; matrix products, arithmetic and copies ran while one was open for 0% of the time, Pallas kernels for 11%

profile of v6, /device:TPU:0, one launch (start us, length us, event | category | flops | bytes accessed | tf_op | source)
XLA Modules:
  0.0 38.3 jit_solution(10001856266610934284)
XLA Ops:
  0.6 0.0 copy-start
  0.6 1.0 %copy-done = bf16[257,8,128]{2,1,0:T(8,128)(2,1)S(1)} copy-done((bf16[257,8,128]{2,1,0:T(8,128)(2,1)S(1)}, bf16[257,8,128]{2,1,0:T(8,128)(2,1)}, u32[]{:S(2)}) %copy-start) | copy-done | bytes 526360
  1.7 0.0 copy-start.2
  1.7 0.4 shard_map.51
  2.0 0.5 %collective-permute-start = (bf16[400,256]{1,0:T(8,128)(2,1)S(1)}, bf16[400,256]{1,0:T(8,128)(2,1)S(1)}, u32[]{:S(2)}, u32[]{:S(2)}) collective-permute-start(bf16[400,256]{1,0:T(8,128)(2,1)S(1)} %get-tuple-element.19), channel_id=1, source_target_pairs={{0,4},{4,0},{8,12},{12,8},{1,5},{5,1},{9,13},{13,9},{2,6},{6,2},{1... | collective-permute-start | bytes 614408 | tf_op jit(solution)/shard_map/ppermute | solution.py:336
  2.6 0.7 %collective-permute-start.1 = (bf16[400,256]{1,0:T(8,128)(2,1)S(1)}, bf16[400,256]{1,0:T(8,128)(2,1)S(1)}, u32[]{:S(2)}, u32[]{:S(2)}) collective-permute-start(bf16[400,256]{1,0:T(8,128)(2,1)S(1)} %get-tuple-element.20), channel_id=1, source_target_pairs={{4,8},{8,4},{5,9},{9,5},{6,10},{10,6},{7,11},{11,7},{20,24},{24,20... | collective-permute-start | bytes 614408 | tf_op jit(solution)/shard_map/ppermute | solution.py:337
  3.2 0.4 %collective-permute-done.a_ref = bf16[400,256]{1,0:T(8,128)(2,1)S(1)} collective-permute-done((bf16[400,256]{1,0:T(8,128)(2,1)S(1)}, bf16[400,256]{1,0:T(8,128)(2,1)S(1)}, u32[]{:S(2)}, u32[]{:S(2)}) %collective-permute-start) | collective-permute-done | bytes 204832 | tf_op jit(solution)/shard_map/ppermute | solution.py:336
  3.6 0.6 %shard_map.52 = (bf16[16,112,384]{2,1,0:T(8,128)(2,1)S(1)}, f32[2,128,384]{2,1,0:T(8,128)S(1)}, bf16[96,384]{1,0:T(8,128)(2,1)S(1)}, bf16[32,384]{1,0:T(8,128)(2,1)S(1)}) custom-call(f32[2056,128]{1,0:T(8,128)S(1)} %get-tuple-element.21.rows_ref, bf16[400,256]{1,0:T(8,128)(2,1)S(1)} %collective-permute-done.a_ref), custom_call_target="tpu_custom_call" | custom-call | tf_op jit(solution)/shard_map/pallas_call | solution.py:339
  4.2 1.3 %collective-permute-start.2 = (bf16[96,384]{1,0:T(8,128)(2,1)S(1)}, bf16[96,384]{1,0:T(8,128)(2,1)S(1)}, u32[]{:S(2)}, u32[]{:S(2)}) collective-permute-start(bf16[96,384]{1,0:T(8,128)(2,1)S(1)} %get-tuple-element.25), channel_id=1, source_target_pairs={{1,0},{2,1},{3,2},{5,4},{6,5},{7,6},{9,8},{10,9},{11,10},{13,12},{... | collective-permute-start | bytes 221192 | tf_op jit(solution)/shard_map/ppermute | solution.py:340
  5.5 0.7 %collective-permute-start.3 = (bf16[32,384]{1,0:T(8,128)(2,1)S(1)}, bf16[32,384]{1,0:T(8,128)(2,1)S(1)}, u32[]{:S(2)}, u32[]{:S(2)}) collective-permute-start(bf16[32,384]{1,0:T(8,128)(2,1)S(1)} %get-tuple-element.26), channel_id=1, source_target_pairs={{5,8},{6,9},{7,10},{9,4},{10,5},{11,6},{21,24},{22,25},{23,26},{25... | collective-permute-start | bytes 73736 | tf_op jit(solution)/shard_map/ppermute | solution.py:341
  6.2 0.0 copy-done.2
  6.2 0.4 shard_map.50.band_ref
  6.6 0.0 collective-permute-done.1.b_ref
  6.6 3.0 %shard_map.53 = (bf16[16,16,256]{2,1,0:T(8,128)(2,1)S(1)}, bf16[17,112,384]{2,1,0:T(8,128)(2,1)S(1)}) custom-call(bf16[400,256]{1,0:T(8,128)(2,1)S(1)} %collective-permute-done.a_ref, bf16[400,256]{1,0:T(8,128)(2,1)S(1)} %collective-permute-done.1.b_ref, bf16[16,112,384]{2,1,0:T(8,128)(2,1)S(1)} %get-tuple-element.22.x_in_ref, ...), custom_call_target="tpu_custom_call" | custom-call | tf_op jit(solution)/shard_map/pallas_call | solution.py:346
  9.6 0.0 copy-start.1
  9.6 0.0 collective-permute-done.3.diag_ref
  9.6 1.8 %collective-permute-done.2.side_ref = bf16[96,384]{1,0:T(8,128)(2,1)S(1)} collective-permute-done((bf16[96,384]{1,0:T(8,128)(2,1)S(1)}, bf16[96,384]{1,0:T(8,128)(2,1)S(1)}, u32[]{:S(2)}, u32[]{:S(2)}) %collective-permute-start.2) | collective-permute-done | bytes 73760 | tf_op jit(solution)/shard_map/ppermute | solution.py:340
  11.4 0.6 %shard_map.54 = (bf16[16,256]{1,0:T(8,128)(2,1)S(1)}, f32[136,128]{1,0:T(8,128)S(1)}, f32[136,128]{1,0:T(8,128)S(1)}, f32[16,128]{1,0:T(8,128)S(1)}) custom-call(bf16[128,256]{1,0:T(8,128)(2,1)S(1)} %shard_map.50.band_ref, bf16[17,112,384]{2,1,0:T(8,128)(2,1)S(1)} %get-tuple-element.24.x_ref, bf16[96,384]{1,0:T(8,128)(2,1)S(1)} %collective-permute-done.2.side_ref, ...), custom_call_target="tpu_custom_call" | custom-call | tf_op jit(solution)/shard_map/pallas_call | solution.py:348
  12.0 3.7 %collective-permute-start.4 = (f32[136,128]{1,0:T(8,128)S(1)}, f32[136,128]{1,0:T(8,128)S(1)}, u32[]{:S(2)}, u32[]{:S(2)}) collective-permute-start(f32[136,128]{1,0:T(8,128)S(1)} %get-tuple-element.29), channel_id=1, source_target_pairs={{0,4},{4,0},{8,12},{12,8},{1,5},{5,1},{9,13},{13,9},{2,6},{6,2},{1... | collective-permute-start | bytes 208904 | tf_op jit(solution)/shard_map/ppermute | solution.py:352
  15.7 0.9 %collective-permute-done.4 = f32[136,128]{1,0:T(8,128)S(1)} collective-permute-done((f32[136,128]{1,0:T(8,128)S(1)}, f32[136,128]{1,0:T(8,128)S(1)}, u32[]{:S(2)}, u32[]{:S(2)}) %collective-permute-start.4) | collective-permute-done | bytes 69664 | tf_op jit(solution)/shard_map/ppermute | solution.py:352
  16.6 1.2 %collective-permute-start.5 = (f32[136,128]{1,0:T(8,128)S(1)}, f32[136,128]{1,0:T(8,128)S(1)}, u32[]{:S(2)}, u32[]{:S(2)}) collective-permute-start(f32[136,128]{1,0:T(8,128)S(1)} %add.12), channel_id=1, source_target_pairs={{0,8},{4,12},{8,0},{12,4},{1,9},{5,13},{9,1},{13,5},{2,10},{6,14},... | collective-permute-start | bytes 208904 | tf_op jit(solution)/shard_map/ppermute | solution.py:355
  17.8 3.3 %collective-permute-done.5 = f32[136,128]{1,0:T(8,128)S(1)} collective-permute-done((f32[136,128]{1,0:T(8,128)S(1)}, f32[136,128]{1,0:T(8,128)S(1)}, u32[]{:S(2)}, u32[]{:S(2)}) %collective-permute-start.5) | collective-permute-done | bytes 69664 | tf_op jit(solution)/shard_map/ppermute | solution.py:355
  21.1 2.4 %collective-permute-start.6 = (f32[152,128]{1,0:T(8,128)S(1)}, f32[152,128]{1,0:T(8,128)S(1)}, u32[]{:S(2)}, u32[]{:S(2)}) collective-permute-start(f32[152,128]{1,0:T(8,128)S(1)} %pad_maximum_fusion), channel_id=1, source_target_pairs={{0,1},{1,0},{2,3},{3,2},{4,5},{5,4},{6,7},{7,6},{8,9},{9,8},{10,11... | collective-permute-start | bytes 233480 | tf_op jit(solution)/shard_map/ppermute | solution.py:367
  23.6 2.4 %collective-permute-done.6 = f32[152,128]{1,0:T(8,128)S(1)} collective-permute-done((f32[152,128]{1,0:T(8,128)S(1)}, f32[152,128]{1,0:T(8,128)S(1)}, u32[]{:S(2)}, u32[]{:S(2)}) %collective-permute-start.6) | collective-permute-done | bytes 77856 | tf_op jit(solution)/shard_map/ppermute | solution.py:367
  25.9 0.1 add_select_fusion
  26.0 3.1 %collective-permute-start.7 = (f32[152,128]{1,0:T(8,128)S(1)}, f32[152,128]{1,0:T(8,128)S(1)}, u32[]{:S(2)}, u32[]{:S(2)}) collective-permute-start(f32[152,128]{1,0:T(8,128)S(1)} %add_select_fusion), channel_id=1, source_target_pairs={{0,2},{1,3},{2,0},{3,1},{4,6},{5,7},{6,4},{7,5},{8,10},{9,11},{10,... | collective-permute-start | bytes 233480 | tf_op jit(solution)/shard_map/ppermute | solution.py:367
  29.1 0.0 copy-done.1
  29.1 0.3 shard_map.55.start_ref
  29.4 2.1 %collective-permute-done.7 = f32[152,128]{1,0:T(8,128)S(1)} collective-permute-done((f32[152,128]{1,0:T(8,128)S(1)}, f32[152,128]{1,0:T(8,128)S(1)}, u32[]{:S(2)}, u32[]{:S(2)}) %collective-permute-start.7) | collective-permute-done | bytes 77856 | tf_op jit(solution)/shard_map/ppermute | solution.py:367
  31.5 0.1 add_select_fusion.1.mine_ref
  31.6 0.1 collective-permute-start.8
  31.7 1.2 %collective-permute-done.8.other_ref = f32[136,128]{1,0:T(8,128)S(1)} collective-permute-done((f32[136,128]{1,0:T(8,128)S(1)}, f32[136,128]{1,0:T(8,128)S(1)}, u32[]{:S(2)}, u32[]{:S(2)}) %collective-permute-start.8) | collective-permute-done | bytes 69664 | tf_op jit(solution)/shard_map/ppermute | solution.py:372
  32.9 5.4 %shard_map.56 = (f32[64,256]{1,0:T(8,128)}, f32[2,32,256]{2,1,0:T(8,128)}) custom-call(f32[136,128]{1,0:T(8,128)S(1)} %add_select_fusion.1.mine_ref, f32[136,128]{1,0:T(8,128)S(1)} %collective-permute-done.8.other_ref, f32[64,256]{1,0:T(8,128)S(1)} %shard_map.55.start_ref, bf16[16,16,256]{2,1,0:T(8,128)(2,1)S(1)} %get-tuple-element.27.inner_ref, ...), custom_call_target="tpu_custom_call" | custom-call | tf_op jit(solution)/shard_map/pallas_call | solution.py:376
  (5 shorter events, 0.0 us)
Async XLA Ops:
  0.6 1.0 %copy-start = (bf16[257,8,128]{2,1,0:T(8,128)(2,1)S(1)}, bf16[257,8,128]{2,1,0:T(8,128)(2,1)}, u32[]{:S(2)}) copy-start(bf16[257,8,128]{2,1,0:T(8,128)(2,1)} %video_ref.1) | copy-start | bytes 1579012
  1.7 4.5 %copy-start.2 = (f32[4,2,7,7]{3,1,2,0:T(2,128)S(1)}, f32[4,2,7,7]{3,1,2,0:T(2,128)}, u32[]{:S(2)}) copy-start(f32[4,2,7,7]{3,1,2,0:T(2,128)} %param.4) | copy-start | bytes 4708
  2.0 1.6 %collective-permute-start = (bf16[400,256]{1,0:T(8,128)(2,1)S(1)}, bf16[400,256]{1,0:T(8,128)(2,1)S(1)}, u32[]{:S(2)}, u32[]{:S(2)}) collective-permute-start(bf16[400,256]{1,0:T(8,128)(2,1)S(1)} %get-tuple-element.19), channel_id=1, source_target_pairs={{0,4},{4,0},{8,12},{12,8},{1,5},{5,1},{9,13},{13,9},{2,6},{6,2},{1... | collective-permute-start | bytes 614408 | tf_op jit(solution)/shard_map/ppermute | solution.py:336
  2.6 4.0 %collective-permute-start.1 = (bf16[400,256]{1,0:T(8,128)(2,1)S(1)}, bf16[400,256]{1,0:T(8,128)(2,1)S(1)}, u32[]{:S(2)}, u32[]{:S(2)}) collective-permute-start(bf16[400,256]{1,0:T(8,128)(2,1)S(1)} %get-tuple-element.20), channel_id=1, source_target_pairs={{4,8},{8,4},{5,9},{9,5},{6,10},{10,6},{7,11},{11,7},{20,24},{24,20... | collective-permute-start | bytes 614408 | tf_op jit(solution)/shard_map/ppermute | solution.py:337
  4.2 7.2 %collective-permute-start.2 = (bf16[96,384]{1,0:T(8,128)(2,1)S(1)}, bf16[96,384]{1,0:T(8,128)(2,1)S(1)}, u32[]{:S(2)}, u32[]{:S(2)}) collective-permute-start(bf16[96,384]{1,0:T(8,128)(2,1)S(1)} %get-tuple-element.25), channel_id=1, source_target_pairs={{1,0},{2,1},{3,2},{5,4},{6,5},{7,6},{9,8},{10,9},{11,10},{13,12},{... | collective-permute-start | bytes 221192 | tf_op jit(solution)/shard_map/ppermute | solution.py:340
  5.5 4.1 %collective-permute-start.3 = (bf16[32,384]{1,0:T(8,128)(2,1)S(1)}, bf16[32,384]{1,0:T(8,128)(2,1)S(1)}, u32[]{:S(2)}, u32[]{:S(2)}) collective-permute-start(bf16[32,384]{1,0:T(8,128)(2,1)S(1)} %get-tuple-element.26), channel_id=1, source_target_pairs={{5,8},{6,9},{7,10},{9,4},{10,5},{11,6},{21,24},{22,25},{23,26},{25... | collective-permute-start | bytes 73736 | tf_op jit(solution)/shard_map/ppermute | solution.py:341
  9.6 19.5 %copy-start.1 = (f32[256,64]{0,1:T(8,128)S(1)}, f32[256,64]{0,1:T(8,128)}, u32[]{:S(2)}) copy-start(f32[256,64]{0,1:T(8,128)} %param.5) | copy-start | bytes 196612
  12.0 4.6 %collective-permute-start.4 = (f32[136,128]{1,0:T(8,128)S(1)}, f32[136,128]{1,0:T(8,128)S(1)}, u32[]{:S(2)}, u32[]{:S(2)}) collective-permute-start(f32[136,128]{1,0:T(8,128)S(1)} %get-tuple-element.29), channel_id=1, source_target_pairs={{0,4},{4,0},{8,12},{12,8},{1,5},{5,1},{9,13},{13,9},{2,6},{6,2},{1... | collective-permute-start | bytes 208904 | tf_op jit(solution)/shard_map/ppermute | solution.py:352
  16.6 4.5 %collective-permute-start.5 = (f32[136,128]{1,0:T(8,128)S(1)}, f32[136,128]{1,0:T(8,128)S(1)}, u32[]{:S(2)}, u32[]{:S(2)}) collective-permute-start(f32[136,128]{1,0:T(8,128)S(1)} %add.12), channel_id=1, source_target_pairs={{0,8},{4,12},{8,0},{12,4},{1,9},{5,13},{9,1},{13,5},{2,10},{6,14},... | collective-permute-start | bytes 208904 | tf_op jit(solution)/shard_map/ppermute | solution.py:355
  21.1 4.8 %collective-permute-start.6 = (f32[152,128]{1,0:T(8,128)S(1)}, f32[152,128]{1,0:T(8,128)S(1)}, u32[]{:S(2)}, u32[]{:S(2)}) collective-permute-start(f32[152,128]{1,0:T(8,128)S(1)} %pad_maximum_fusion), channel_id=1, source_target_pairs={{0,1},{1,0},{2,3},{3,2},{4,5},{5,4},{6,7},{7,6},{8,9},{9,8},{10,11... | collective-permute-start | bytes 233480 | tf_op jit(solution)/shard_map/ppermute | solution.py:367
  26.0 5.5 %collective-permute-start.7 = (f32[152,128]{1,0:T(8,128)S(1)}, f32[152,128]{1,0:T(8,128)S(1)}, u32[]{:S(2)}, u32[]{:S(2)}) collective-permute-start(f32[152,128]{1,0:T(8,128)S(1)} %add_select_fusion), channel_id=1, source_target_pairs={{0,2},{1,3},{2,0},{3,1},{4,6},{5,7},{6,4},{7,5},{8,10},{9,11},{10,... | collective-permute-start | bytes 233480 | tf_op jit(solution)/shard_map/ppermute | solution.py:367
  31.6 1.3 %collective-permute-start.8 = (f32[136,128]{1,0:T(8,128)S(1)}, f32[136,128]{1,0:T(8,128)S(1)}, u32[]{:S(2)}, u32[]{:S(2)}) collective-permute-start(f32[136,128]{1,0:T(8,128)S(1)} %add_select_fusion.1.mine_ref), channel_id=1, source_target_pairs={{0,4},{4,0},{8,12},{12,8},{1,5},{5,1},{9,13},{13,9},{2,6},{6,2},{1... | collective-permute-start | bytes 208904 | tf_op jit(solution)/shard_map/ppermute | solution.py:372

commit v7 on v6

--- a/solution.py
+++ b/solution.py
@@ -19,6 +19,7 @@
 SUMMED = HALF + 8
 BLOCKS = 16
 UNROLL = 4
+AHEAD = 3
 F32 = jnp.float32
 BF16 = jnp.bfloat16
 HIGHEST = lax.Precision.HIGHEST
@@ -39,13 +40,15 @@
     return (lax.axis_index(axis) & 1) == 0
 
 
-def send_kernel(video_ref, rows_ref, send_a_ref, send_b_ref):
+def send_kernel(video_ref, rows_ref, send_a_ref, send_b_ref, heads_ref):
     even = is_even("row")
     rows_ref[...] = video_ref[...].astype(F32).reshape(rows_ref.shape)
     for group in range(2):
         lanes = slice(HALF * group, HALF * group + HALF)
+        tiles = [turned(rows_ref, row, group) for row in range(ROWS)]
+        heads_ref[:, lanes] = jnp.concatenate([tile[:8] for tile in tiles], axis=0)
         for i in range(REACH):
-            first, last = turned(rows_ref, i, group), turned(rows_ref, ROWS - REACH + i, group)
+            first, last = tiles[i], tiles[ROWS - REACH + i]
             at = slice(COLS * i, COLS * i + COLS)
             send_a_ref[at, lanes] = jnp.where(even, last, first).astype(BF16)
             send_b_ref[at, lanes] = jnp.where(even, first, last).astype(BF16)
@@ -58,33 +61,34 @@
         ref[REACH * COLS : REACH * COLS + 16, COLS : 2 * COLS] = chosen
 
 
-def own_kernel(rows_ref, a_ref, x_ref, rim_ref, side_ref, diag_ref):
+def side_kernel(rows_ref, heads_ref, a_ref, side_ref, diag_ref):
     even = is_even("row")
     fill = jnp.zeros((8, HALF), F32)
+    ends = rows_ref[FRAMES * ROWS : FRAMES * ROWS + ROWS, :]
+    heads = in_groups([heads_ref[8 * i : 8 * i + 8] for i in range(ROWS)], ends)
     near = expanded(a_ref[...].astype(F32), 8)
     for group in range(3):
         lanes = slice(HALF * group, HALF * group + HALF)
-        tiles = [turned(rows_ref, row, group) for row in range(ROWS)]
-        for pair in range(3):
-            x_ref[:, 32 + 16 * pair : 48 + 16 * pair, lanes] = blocked(tiles[2 * pair + 1], tiles[2 * pair + 2])
-        rim_ref[0, :, lanes] = tiles[0]
-        rim_ref[1, :, lanes] = tiles[ROWS - 1]
-        heads = [tile[:8] for tile in tiles]
-        sent = heads + [row[group] for row in near] + [fill]
+        sent = [row[group] for row in heads + near] + [fill]
         side_ref[:, lanes] = jnp.concatenate(sent, axis=0).astype(BF16)
-        chosen = [jnp.where(even, heads[i], heads[ROWS - REACH + i]) for i in range(REACH)] + [fill]
-        diag_ref[:, lanes] = jnp.concatenate(chosen, axis=0).astype(BF16)
-
-
-def expanded(got, count):
+        chosen = [jnp.where(even, heads[i][group], heads[ROWS - REACH + i][group]) for i in range(REACH)]
+        diag_ref[:, lanes] = jnp.concatenate(chosen + [fill], axis=0).astype(BF16)
+
+
+def in_groups(tiles, ends):
+    count = tiles[0].shape[0]
     final = lax.broadcasted_iota(jnp.int32, (count, HALF), 1) == HALF - 1
-    ends = got[REACH * COLS : REACH * COLS + 8, :COLS].T
+    ends = ends.T
     rows = []
-    for i in range(REACH):
-        tile = got[COLS * i : COLS * i + count]
+    for i, tile in enumerate(tiles):
         late = jnp.where(final, ends[:count, i : i + 1], pltpu.roll(tile[:, :HALF], HALF - 1, 1))
         rows.append([tile[:, :HALF], tile[:, HALF:], late])
     return rows
+
+
+def expanded(got, count):
+    tiles = [got[COLS * i : COLS * i + count] for i in range(REACH)]
+    return in_groups(tiles, got[REACH * COLS : REACH * COLS + 8, :COLS])
 
 
 def band_kernel(filters_ref, band_ref, taps_ref):
@@ -115,8 +119,12 @@
             band_ref[start : start + 16, 128:256] = rolled[16:]
 
 
+def dot(a, b):
+    return jnp.dot(a, b, precision=HIGHEST, preferred_element_type=F32)
+
+
 def start_kernel(start_ref, basis_ref):
-    basis_ref[...] = jnp.dot(start_ref[...], frame_order(0), precision=HIGHEST, preferred_element_type=F32)
+    basis_ref[...] = dot(start_ref[...], frame_order(0))
 
 
 def frame_order(axis):
@@ -125,19 +133,18 @@
     return jnp.where(frame == 2 * (lane & (HALF - 1)) + (lane >> 7), 1.0, 0.0).astype(F32)
 
 
-def place_halo(a_ref, b_ref, x_in_ref, rim_ref, x_ref):
+def place_rows(a_ref, b_ref, rows_ref, x_ref):
     even = is_even("row")
     got_a, got_b = a_ref[...], b_ref[...]
     above = expanded(jnp.where(even, got_b, got_a).astype(F32), COLS)
     below = expanded(jnp.where(even, got_a, got_b).astype(F32), COLS)
+    x_ref[0] = jnp.zeros((112, 3 * HALF), BF16)
     for group in range(3):
-        lanes = slice(HALF * group, HALF * group + HALF)
-        x_ref[1:, 0:16, lanes] = blocked(above[0][group], above[1][group])
-        x_ref[1:, 16:32, lanes] = blocked(above[2][group], rim_ref[0, :, lanes])
-        x_ref[1:, 80:96, lanes] = blocked(rim_ref[1, :, lanes], below[0][group])
-        x_ref[1:, 96:112, lanes] = blocked(below[1][group], below[2][group])
-    x_ref[1:, 32:80, :] = x_in_ref[:, 32:80, :]
-    x_ref[0] = jnp.zeros((112, 3 * HALF), BF16)
+        own = [turned(rows_ref, row, group) for row in range(ROWS)]
+        tiles = [row[group] for row in above] + own + [row[group] for row in below]
+        for pair in range(len(tiles) // 2):
+            at = slice(16 * pair, 16 * pair + 16)
+            x_ref[1:, at, HALF * group : HALF * group + HALF] = blocked(tiles[2 * pair], tiles[2 * pair + 1])
 
 
 def block_feats(band_ref, left, right):
@@ -172,8 +179,8 @@
     return (lax.broadcasted_iota(jnp.int32, (16, FRAMES), 0) & 4) == 4
 
 
-def inner_kernel(a_ref, b_ref, x_in_ref, rim_ref, band_ref, feats_ref, x_ref):
-    place_halo(a_ref, b_ref, x_in_ref, rim_ref, x_ref)
+def inner_kernel(a_ref, b_ref, rows_ref, band_ref, feats_ref, x_ref):
+    place_rows(a_ref, b_ref, rows_ref, x_ref)
 
     def body(step, carry):
         for i in range(UNROLL):
@@ -223,23 +230,24 @@
     work = [work[8 * v : 8 * v + 8] for v in range(count)]
     sub = lax.broadcasted_iota(jnp.int32, shape, 0)
 
-    def columns(b):
+    def columns(b, first, last):
         lanes = [MODES + 8 * b + m for m in range(8)]
-        return {v: [jnp.broadcast_to(work[v][:, k : k + 1], shape) for k in lanes] for v in range(b, count)}
+        return {v: [jnp.broadcast_to(work[v][:, k : k + 1], shape) for k in lanes] for v in range(first, last)}
 
     def spread(tile, row):
         return jnp.broadcast_to(tile[row : row + 1], shape)
 
-    cols = columns(0)
+    cols = columns(0, 0, count)
     done = []
     for b in range(count):
-        ahead = columns(b + 1)
-        scale = jnp.zeros(shape, F32)
+        near = min(count, b + 1 + AHEAD)
+        ahead = columns(b + 1, b + 1, near)
+        scale = jnp.ones(shape, F32)
         for m in range(8):
             lead = cols[b][m]
             pivot = spread(lead, m)
             inverse = 1.0 / pivot
-            scale = jnp.where(sub == m, lax.rsqrt(pivot), scale)
+            scale = jnp.where(sub == m, pivot, scale)
             row = spread(work[b], m) * inverse
             for q in range(m + 1, 8):
                 times = spread(lead, q) * inverse
@@ -252,8 +260,8 @@
             work[b] = work[b] - jnp.where(sub > m, lead, 0.0) * row
             for v in range(b + 1, count):
                 work[v] = work[v] - cols[v][m] * row
-        done.append(work[b] * scale)
-        cols = ahead
+        done.append(work[b] * lax.rsqrt(scale))
+        cols = {**ahead, **columns(b + 1, near, count)}
     return jnp.concatenate(done, axis=0)[:, :MODES]
 
 
@@ -272,14 +280,18 @@
         [jnp.concatenate([top, cross], axis=1), jnp.concatenate([cross.T, low], axis=1)], axis=0
     )
     gram = gram * scale
-    basis = start_ref[...]
+    stacked = dot(start_ref[...], gram)
     for sweep in range(SWEEPS):
-        stacked = jnp.dot(basis, gram, precision=HIGHEST, preferred_element_type=F32)
         inner = lax.dot_general(
             stacked, stacked, (((1,), (1,)), ((), ())), precision=HIGHEST, preferred_element_type=F32
         )
-        basis = jnp.dot(inverse_factor(inner), stacked, precision=HIGHEST, preferred_element_type=F32)
-    basis_ref[...] = jnp.dot(basis, frame_order(1), precision=HIGHEST, preferred_element_type=F32)
+        if sweep < SWEEPS - 1:
+            beside = dot(stacked, gram)
+        else:
+            beside = jnp.concatenate([stacked, dot(stacked, frame_order(1))], axis=1)
+        stacked = dot(inverse_factor(inner), beside)
+    basis = stacked[:, :FRAMES]
+    basis_ref[...] = stacked[:, FRAMES:]
     twice = jnp.concatenate([basis, basis], axis=0)
     before = jnp.concatenate([before_ref[:8], before_ref[8:]], axis=1)
     before = jnp.concatenate([before, pltpu.roll(before, 4, 0)], axis=0)
@@ -328,22 +340,20 @@
 
     across = [(a * size_col + i, b * size_col + j) for a, b in far for i, j in to_left]
     send = ((REACH * COLS + 16, FRAMES), BF16)
-    tile = ((BLOCKS, 112, 3 * HALF), BF16)
     tiles = ((BLOCKS + 1, 112, 3 * HALF), BF16)
-    rim = ((2, COLS, 3 * HALF), F32)
     rows = (((FRAMES + 1) * ROWS, COLS), F32)
-    rows, send_a, send_b = call(send_kernel, [rows, send, send], 1)(video)
+    rows, send_a, send_b, heads = call(send_kernel, [rows, send, send, ((8 * ROWS, FRAMES), F32)], 1)(video)
     got_a = lax.ppermute(send_a, "row", near)
     got_b = lax.ppermute(send_b, "row", far)
-    outs = [tile, rim, ((96, 3 * HALF), BF16), ((32, 3 * HALF), BF16)]
-    x, rim, side, diag = call(own_kernel, outs, 2)(rows, got_a)
+    outs = [((96, 3 * HALF), BF16), ((32, 3 * HALF), BF16)]
+    side, diag = call(side_kernel, outs, 3)(rows, heads, got_a)
     side = lax.ppermute(side, "col", to_left)
     diag = lax.ppermute(diag, ("row", "col"), across)
 
     (band,) = call(band_kernel, [((128, 256), BF16)], 1, [pltpu.VMEM((16, 128), F32)])(
         jnp.transpose(filters, (0, 2, 1, 3))
     )
-    inner, x = call(inner_kernel, [((BLOCKS, 16, FRAMES), BF16), tiles], 5)(got_a, got_b, x, rim, band)
+    inner, x = call(inner_kernel, [((BLOCKS, 16, FRAMES), BF16), tiles], 4)(got_a, got_b, rows, band)
     part, passed = ((SUMMED, HALF), F32), ((16, HALF), F32)
     edge, mine, other, passed = call(edge_kernel, [((16, FRAMES), BF16), part, part, passed], 5)(
         band, x, side, diag, inner

time: 38.5 us -> 38 us (0.987)
  waiting for transfers between devices: 12.1 us -> 11.3 us
  Pallas kernels: 10.5 us -> 10 us
  starting transfers between devices: 13.6 us -> 14.1 us
    pallas_call x1, Pallas kernels: 5.36 us -> 4.72 us  [on_device(): call(kernel, [((MODES, FRAMES), F32), ((ROWS // 4, COLS // 4, ORIENT * MO...]
    ppermute x1, waiting for transfers between devices: 1.8 us -> 1.28 us  [on_device(): side = lax.ppermute(side, 'col', to_left)]
where the time goes in v7:
time: 38 us; the launch traced here: 37.5 us
  starting transfers between devices  14.1 us (37%)
  waiting for transfers between devices  11.3 us (30%)
  Pallas kernels  10 us (26%)
  local copies, waits for them, and re-layouts  1.05 us (3%)
  between operations  0.78 us (2%)
    ppermute x2, starting transfers between devices, on_device(): got = lax.ppermute(mine, 'col', [(i, i ^ step) for i in range(size_col)])  5.69 us
    pallas_call x1, Pallas kernels, on_device(): call(kernel, [((MODES, FRAMES), F32), ((ROWS // 4, COLS // 4, ORIENT * MO...  4.72 us
    ppermute x2, waiting for transfers between devices, on_device(): got = lax.ppermute(mine, 'col', [(i, i ^ step) for i in range(size_col)])  4.48 us
    ppermute x1, starting transfers between devices, on_device(): mine = mine + lax.ppermute(other, 'row', near)  3.7 us
    pallas_call x1, Pallas kernels, on_device(): call(inner_kernel, [((BLOCKS, 16, FRAMES), BF16), tiles], 4)  3.5 us
    ppermute x1, waiting for transfers between devices, on_device(): lax.ppermute(mine, 'row', [(i, i ^ step) for i in range(size_row)])  3.03 us
    ppermute x1, starting transfers between devices, on_device(): lax.ppermute(mine, 'row', [(i, i ^ step) for i in range(size_row)])  1.47 us
    ppermute x1, starting transfers between devices, on_device(): side = lax.ppermute(side, 'col', to_left)  1.29 us
  transfers between devices with their start and end apart: 9, of which 7 were waited for; matrix products, arithmetic and copies ran while one was open for 0% of the time, Pallas kernels for 11%

profile of v7, /device:TPU:0, one launch (start us, length us, event | category | flops | bytes accessed | tf_op | source)
XLA Modules:
  0.0 37.5 jit_solution(10635005668758727230)
XLA Ops:
  0.6 0.0 copy-start
  0.6 1.0 %copy-done = bf16[257,8,128]{2,1,0:T(8,128)(2,1)S(1)} copy-done((bf16[257,8,128]{2,1,0:T(8,128)(2,1)S(1)}, bf16[257,8,128]{2,1,0:T(8,128)(2,1)}, u32[]{:S(2)}) %copy-start) | copy-done | bytes 526360
  1.7 0.0 copy-start.2
  1.7 0.4 %shard_map.51 = (f32[2056,128]{1,0:T(8,128)S(1)}, bf16[400,256]{1,0:T(8,128)(2,1)S(1)}, bf16[400,256]{1,0:T(8,128)(2,1)S(1)}, f32[64,256]{1,0:T(8,128)S(1)}) custom-call(bf16[257,8,128]{2,1,0:T(8,128)(2,1)S(1)} %copy-done), custom_call_target="tpu_custom_call" | custom-call | tf_op jit(solution)/shard_map/pallas_call | solution.py:345
  2.1 0.5 %collective-permute-start = (bf16[400,256]{1,0:T(8,128)(2,1)S(1)}, bf16[400,256]{1,0:T(8,128)(2,1)S(1)}, u32[]{:S(2)}, u32[]{:S(2)}) collective-permute-start(bf16[400,256]{1,0:T(8,128)(2,1)S(1)} %get-tuple-element.18), channel_id=1, source_target_pairs={{0,4},{4,0},{8,12},{12,8},{1,5},{5,1},{9,13},{13,9},{2,6},{6,2},{1... | collective-permute-start | bytes 614408 | tf_op jit(solution)/shard_map/ppermute | solution.py:346
  2.6 0.7 %collective-permute-start.1 = (bf16[400,256]{1,0:T(8,128)(2,1)S(1)}, bf16[400,256]{1,0:T(8,128)(2,1)S(1)}, u32[]{:S(2)}, u32[]{:S(2)}) collective-permute-start(bf16[400,256]{1,0:T(8,128)(2,1)S(1)} %get-tuple-element.19), channel_id=1, source_target_pairs={{4,8},{8,4},{5,9},{9,5},{6,10},{10,6},{7,11},{11,7},{20,24},{24,20... | collective-permute-start | bytes 614408 | tf_op jit(solution)/shard_map/ppermute | solution.py:347
  3.3 0.4 %collective-permute-done.a_ref = bf16[400,256]{1,0:T(8,128)(2,1)S(1)} collective-permute-done((bf16[400,256]{1,0:T(8,128)(2,1)S(1)}, bf16[400,256]{1,0:T(8,128)(2,1)S(1)}, u32[]{:S(2)}, u32[]{:S(2)}) %collective-permute-start) | collective-permute-done | bytes 204832 | tf_op jit(solution)/shard_map/ppermute | solution.py:346
  3.7 0.2 shard_map.53
  3.9 1.3 %collective-permute-start.2 = (bf16[96,384]{1,0:T(8,128)(2,1)S(1)}, bf16[96,384]{1,0:T(8,128)(2,1)S(1)}, u32[]{:S(2)}, u32[]{:S(2)}) collective-permute-start(bf16[96,384]{1,0:T(8,128)(2,1)S(1)} %get-tuple-element.23), channel_id=1, source_target_pairs={{1,0},{2,1},{3,2},{5,4},{6,5},{7,6},{9,8},{10,9},{11,10},{13,12},{... | collective-permute-start | bytes 221192 | tf_op jit(solution)/shard_map/ppermute | solution.py:350
  5.2 0.7 %collective-permute-start.3 = (bf16[32,384]{1,0:T(8,128)(2,1)S(1)}, bf16[32,384]{1,0:T(8,128)(2,1)S(1)}, u32[]{:S(2)}, u32[]{:S(2)}) collective-permute-start(bf16[32,384]{1,0:T(8,128)(2,1)S(1)} %get-tuple-element.24), channel_id=1, source_target_pairs={{5,8},{6,9},{7,10},{9,4},{10,5},{11,6},{21,24},{22,25},{23,26},{25... | collective-permute-start | bytes 73736 | tf_op jit(solution)/shard_map/ppermute | solution.py:351
  5.9 0.0 copy-done.2
  5.9 0.4 %shard_map.50.band_ref = bf16[128,256]{1,0:T(8,128)(2,1)S(1)} custom-call(f32[4,7,2,7]{3,2,1,0:T(2,128)S(1)} %bitcast.5), custom_call_target="tpu_custom_call" | custom-call | tf_op jit(solution)/shard_map/pallas_call | solution.py:353
  6.2 0.0 collective-permute-done.1.b_ref
  6.3 3.5 %shard_map.52 = (bf16[16,16,256]{2,1,0:T(8,128)(2,1)S(1)}, bf16[17,112,384]{2,1,0:T(8,128)(2,1)S(1)}) custom-call(bf16[400,256]{1,0:T(8,128)(2,1)S(1)} %collective-permute-done.a_ref, bf16[400,256]{1,0:T(8,128)(2,1)S(1)} %collective-permute-done.1.b_ref, f32[2056,128]{1,0:T(8,128)S(1)} %get-tuple-element.20.rows_ref, bf16[128,256]{1,0:T(8,128)(2,1)S(1)} %shard_map.50.band_ref), custom_call_target="tpu_custom_call" | custom-call | tf_op jit(solution)/shard_map/pallas_call | solution.py:356
  9.8 0.0 copy-start.1
  9.8 0.0 collective-permute-done.3.diag_ref
  9.8 1.3 %collective-permute-done.2.side_ref = bf16[96,384]{1,0:T(8,128)(2,1)S(1)} collective-permute-done((bf16[96,384]{1,0:T(8,128)(2,1)S(1)}, bf16[96,384]{1,0:T(8,128)(2,1)S(1)}, u32[]{:S(2)}, u32[]{:S(2)}) %collective-permute-start.2) | collective-permute-done | bytes 73760 | tf_op jit(solution)/shard_map/ppermute | solution.py:350
  11.1 0.6 %shard_map.54 = (bf16[16,256]{1,0:T(8,128)(2,1)S(1)}, f32[136,128]{1,0:T(8,128)S(1)}, f32[136,128]{1,0:T(8,128)S(1)}, f32[16,128]{1,0:T(8,128)S(1)}) custom-call(bf16[128,256]{1,0:T(8,128)(2,1)S(1)} %shard_map.50.band_ref, bf16[17,112,384]{2,1,0:T(8,128)(2,1)S(1)} %get-tuple-element.21.x_ref, bf16[96,384]{1,0:T(8,128)(2,1)S(1)} %collective-permute-done.2.side_ref, ...), custom_call_target="tpu_custom_call" | custom-call | tf_op jit(solution)/shard_map/pallas_call | solution.py:358
  11.6 3.7 %collective-permute-start.4 = (f32[136,128]{1,0:T(8,128)S(1)}, f32[136,128]{1,0:T(8,128)S(1)}, u32[]{:S(2)}, u32[]{:S(2)}) collective-permute-start(f32[136,128]{1,0:T(8,128)S(1)} %get-tuple-element.27), channel_id=1, source_target_pairs={{0,4},{4,0},{8,12},{12,8},{1,5},{5,1},{9,13},{13,9},{2,6},{6,2},{1... | collective-permute-start | bytes 208904 | tf_op jit(solution)/shard_map/ppermute | solution.py:362
  15.3 0.9 %collective-permute-done.4 = f32[136,128]{1,0:T(8,128)S(1)} collective-permute-done((f32[136,128]{1,0:T(8,128)S(1)}, f32[136,128]{1,0:T(8,128)S(1)}, u32[]{:S(2)}, u32[]{:S(2)}) %collective-permute-start.4) | collective-permute-done | bytes 69664 | tf_op jit(solution)/shard_map/ppermute | solution.py:362
  16.2 1.5 %collective-permute-start.5 = (f32[136,128]{1,0:T(8,128)S(1)}, f32[136,128]{1,0:T(8,128)S(1)}, u32[]{:S(2)}, u32[]{:S(2)}) collective-permute-start(f32[136,128]{1,0:T(8,128)S(1)} %add.12), channel_id=1, source_target_pairs={{0,8},{4,12},{8,0},{12,4},{1,9},{5,13},{9,1},{13,5},{2,10},{6,14},... | collective-permute-start | bytes 208904 | tf_op jit(solution)/shard_map/ppermute | solution.py:365
  17.7 3.0 %collective-permute-done.5 = f32[136,128]{1,0:T(8,128)S(1)} collective-permute-done((f32[136,128]{1,0:T(8,128)S(1)}, f32[136,128]{1,0:T(8,128)S(1)}, u32[]{:S(2)}, u32[]{:S(2)}) %collective-permute-start.5) | collective-permute-done | bytes 69664 | tf_op jit(solution)/shard_map/ppermute | solution.py:365
  20.8 2.4 %collective-permute-start.6 = (f32[152,128]{1,0:T(8,128)S(1)}, f32[152,128]{1,0:T(8,128)S(1)}, u32[]{:S(2)}, u32[]{:S(2)}) collective-permute-start(f32[152,128]{1,0:T(8,128)S(1)} %pad_maximum_fusion), channel_id=1, source_target_pairs={{0,1},{1,0},{2,3},{3,2},{4,5},{5,4},{6,7},{7,6},{8,9},{9,8},{10,11... | collective-permute-start | bytes 233480 | tf_op jit(solution)/shard_map/ppermute | solution.py:377
  23.2 2.4 %collective-permute-done.6 = f32[152,128]{1,0:T(8,128)S(1)} collective-permute-done((f32[152,128]{1,0:T(8,128)S(1)}, f32[152,128]{1,0:T(8,128)S(1)}, u32[]{:S(2)}, u32[]{:S(2)}) %collective-permute-start.6) | collective-permute-done | bytes 77856 | tf_op jit(solution)/shard_map/ppermute | solution.py:377
  25.6 0.1 add_select_fusion
  25.7 3.3 %collective-permute-start.7 = (f32[152,128]{1,0:T(8,128)S(1)}, f32[152,128]{1,0:T(8,128)S(1)}, u32[]{:S(2)}, u32[]{:S(2)}) collective-permute-start(f32[152,128]{1,0:T(8,128)S(1)} %add_select_fusion), channel_id=1, source_target_pairs={{0,2},{1,3},{2,0},{3,1},{4,6},{5,7},{6,4},{7,5},{8,10},{9,11},{10,... | collective-permute-start | bytes 233480 | tf_op jit(solution)/shard_map/ppermute | solution.py:377
  28.9 0.0 copy-done.1
  28.9 0.3 shard_map.55.start_ref
  29.2 2.1 %collective-permute-done.7 = f32[152,128]{1,0:T(8,128)S(1)} collective-permute-done((f32[152,128]{1,0:T(8,128)S(1)}, f32[152,128]{1,0:T(8,128)S(1)}, u32[]{:S(2)}, u32[]{:S(2)}) %collective-permute-start.7) | collective-permute-done | bytes 77856 | tf_op jit(solution)/shard_map/ppermute | solution.py:377
  31.3 0.1 add_select_fusion.1.mine_ref
  31.4 0.1 collective-permute-start.8
  31.5 1.2 %collective-permute-done.8.other_ref = f32[136,128]{1,0:T(8,128)S(1)} collective-permute-done((f32[136,128]{1,0:T(8,128)S(1)}, f32[136,128]{1,0:T(8,128)S(1)}, u32[]{:S(2)}, u32[]{:S(2)}) %collective-permute-start.8) | collective-permute-done | bytes 69664 | tf_op jit(solution)/shard_map/ppermute | solution.py:382
  32.7 4.7 %shard_map.56 = (f32[64,256]{1,0:T(8,128)}, f32[2,32,256]{2,1,0:T(8,128)}) custom-call(f32[136,128]{1,0:T(8,128)S(1)} %add_select_fusion.1.mine_ref, f32[136,128]{1,0:T(8,128)S(1)} %collective-permute-done.8.other_ref, f32[64,256]{1,0:T(8,128)S(1)} %shard_map.55.start_ref, bf16[16,16,256]{2,1,0:T(8,128)(2,1)S(1)} %get-tuple-element.25.inner_ref, ...), custom_call_target="tpu_custom_call" | custom-call | tf_op jit(solution)/shard_map/pallas_call | solution.py:386
  (5 shorter events, 0.0 us)
Async XLA Ops:
  0.6 1.0 %copy-start = (bf16[257,8,128]{2,1,0:T(8,128)(2,1)S(1)}, bf16[257,8,128]{2,1,0:T(8,128)(2,1)}, u32[]{:S(2)}) copy-start(bf16[257,8,128]{2,1,0:T(8,128)(2,1)} %video_ref.1) | copy-start | bytes 1579012
  1.7 4.2 %copy-start.2 = (f32[4,2,7,7]{3,1,2,0:T(2,128)S(1)}, f32[4,2,7,7]{3,1,2,0:T(2,128)}, u32[]{:S(2)}) copy-start(f32[4,2,7,7]{3,1,2,0:T(2,128)} %param.4) | copy-start | bytes 4708
  2.1 1.6 %collective-permute-start = (bf16[400,256]{1,0:T(8,128)(2,1)S(1)}, bf16[400,256]{1,0:T(8,128)(2,1)S(1)}, u32[]{:S(2)}, u32[]{:S(2)}) collective-permute-start(bf16[400,256]{1,0:T(8,128)(2,1)S(1)} %get-tuple-element.18), channel_id=1, source_target_pairs={{0,4},{4,0},{8,12},{12,8},{1,5},{5,1},{9,13},{13,9},{2,6},{6,2},{1... | collective-permute-start | bytes 614408 | tf_op jit(solution)/shard_map/ppermute | solution.py:346
  2.6 3.6 %collective-permute-start.1 = (bf16[400,256]{1,0:T(8,128)(2,1)S(1)}, bf16[400,256]{1,0:T(8,128)(2,1)S(1)}, u32[]{:S(2)}, u32[]{:S(2)}) collective-permute-start(bf16[400,256]{1,0:T(8,128)(2,1)S(1)} %get-tuple-element.19), channel_id=1, source_target_pairs={{4,8},{8,4},{5,9},{9,5},{6,10},{10,6},{7,11},{11,7},{20,24},{24,20... | collective-permute-start | bytes 614408 | tf_op jit(solution)/shard_map/ppermute | solution.py:347
  3.9 7.2 %collective-permute-start.2 = (bf16[96,384]{1,0:T(8,128)(2,1)S(1)}, bf16[96,384]{1,0:T(8,128)(2,1)S(1)}, u32[]{:S(2)}, u32[]{:S(2)}) collective-permute-start(bf16[96,384]{1,0:T(8,128)(2,1)S(1)} %get-tuple-element.23), channel_id=1, source_target_pairs={{1,0},{2,1},{3,2},{5,4},{6,5},{7,6},{9,8},{10,9},{11,10},{13,12},{... | collective-permute-start | bytes 221192 | tf_op jit(solution)/shard_map/ppermute | solution.py:350
  5.2 4.6 %collective-permute-start.3 = (bf16[32,384]{1,0:T(8,128)(2,1)S(1)}, bf16[32,384]{1,0:T(8,128)(2,1)S(1)}, u32[]{:S(2)}, u32[]{:S(2)}) collective-permute-start(bf16[32,384]{1,0:T(8,128)(2,1)S(1)} %get-tuple-element.24), channel_id=1, source_target_pairs={{5,8},{6,9},{7,10},{9,4},{10,5},{11,6},{21,24},{22,25},{23,26},{25... | collective-permute-start | bytes 73736 | tf_op jit(solution)/shard_map/ppermute | solution.py:351
  9.8 19.2 %copy-start.1 = (f32[256,64]{0,1:T(8,128)S(1)}, f32[256,64]{0,1:T(8,128)}, u32[]{:S(2)}) copy-start(f32[256,64]{0,1:T(8,128)} %param.5) | copy-start | bytes 196612
  11.6 4.6 %collective-permute-start.4 = (f32[136,128]{1,0:T(8,128)S(1)}, f32[136,128]{1,0:T(8,128)S(1)}, u32[]{:S(2)}, u32[]{:S(2)}) collective-permute-start(f32[136,128]{1,0:T(8,128)S(1)} %get-tuple-element.27), channel_id=1, source_target_pairs={{0,4},{4,0},{8,12},{12,8},{1,5},{5,1},{9,13},{13,9},{2,6},{6,2},{1... | collective-permute-start | bytes 208904 | tf_op jit(solution)/shard_map/ppermute | solution.py:362
  16.2 4.5 %collective-permute-start.5 = (f32[136,128]{1,0:T(8,128)S(1)}, f32[136,128]{1,0:T(8,128)S(1)}, u32[]{:S(2)}, u32[]{:S(2)}) collective-permute-start(f32[136,128]{1,0:T(8,128)S(1)} %add.12), channel_id=1, source_target_pairs={{0,8},{4,12},{8,0},{12,4},{1,9},{5,13},{9,1},{13,5},{2,10},{6,14},... | collective-permute-start | bytes 208904 | tf_op jit(solution)/shard_map/ppermute | solution.py:365
  20.8 4.8 %collective-permute-start.6 = (f32[152,128]{1,0:T(8,128)S(1)}, f32[152,128]{1,0:T(8,128)S(1)}, u32[]{:S(2)}, u32[]{:S(2)}) collective-permute-start(f32[152,128]{1,0:T(8,128)S(1)} %pad_maximum_fusion), channel_id=1, source_target_pairs={{0,1},{1,0},{2,3},{3,2},{4,5},{5,4},{6,7},{7,6},{8,9},{9,8},{10,11... | collective-permute-start | bytes 233480 | tf_op jit(solution)/shard_map/ppermute | solution.py:377
  25.7 5.6 %collective-permute-start.7 = (f32[152,128]{1,0:T(8,128)S(1)}, f32[152,128]{1,0:T(8,128)S(1)}, u32[]{:S(2)}, u32[]{:S(2)}) collective-permute-start(f32[152,128]{1,0:T(8,128)S(1)} %add_select_fusion), channel_id=1, source_target_pairs={{0,2},{1,3},{2,0},{3,1},{4,6},{5,7},{6,4},{7,5},{8,10},{9,11},{10,... | collective-permute-start | bytes 233480 | tf_op jit(solution)/shard_map/ppermute | solution.py:377
  31.4 1.3 %collective-permute-start.8 = (f32[136,128]{1,0:T(8,128)S(1)}, f32[136,128]{1,0:T(8,128)S(1)}, u32[]{:S(2)}, u32[]{:S(2)}) collective-permute-start(f32[136,128]{1,0:T(8,128)S(1)} %add_select_fusion.1.mine_ref), channel_id=1, source_target_pairs={{0,4},{4,0},{8,12},{12,8},{1,5},{5,1},{9,13},{13,9},{2,6},{6,2},{1... | collective-permute-start | bytes 208904 | tf_op jit(solution)/shard_map/ppermute | solution.py:382

commit v8 on v7

--- a/solution.py
+++ b/solution.py
@@ -18,7 +18,7 @@
 COLS = 128
 SUMMED = HALF + 8
 BLOCKS = 16
-UNROLL = 4
+UNROLL = 8
 AHEAD = 3
 F32 = jnp.float32
 BF16 = jnp.bfloat16
@@ -91,7 +91,7 @@
     return in_groups(tiles, got[REACH * COLS : REACH * COLS + 8, :COLS])
 
 
-def band_kernel(filters_ref, band_ref, taps_ref):
+def make_band(filters_ref, band_ref, taps_ref):
     taps_ref[...] = jnp.zeros((16, 128), F32)
     for orient in range(ORIENT):
         for part in range(2):
@@ -179,7 +179,8 @@
     return (lax.broadcasted_iota(jnp.int32, (16, FRAMES), 0) & 4) == 4
 
 
-def inner_kernel(a_ref, b_ref, rows_ref, band_ref, feats_ref, x_ref):
+def inner_kernel(a_ref, b_ref, rows_ref, filters_ref, feats_ref, x_ref, band_ref, taps_ref):
+    make_band(filters_ref, band_ref, taps_ref)
     place_rows(a_ref, b_ref, rows_ref, x_ref)
 
     def body(step, carry):
@@ -350,10 +351,10 @@
     side = lax.ppermute(side, "col", to_left)
     diag = lax.ppermute(diag, ("row", "col"), across)
 
-    (band,) = call(band_kernel, [((128, 256), BF16)], 1, [pltpu.VMEM((16, 128), F32)])(
-        jnp.transpose(filters, (0, 2, 1, 3))
-    )
-    inner, x = call(inner_kernel, [((BLOCKS, 16, FRAMES), BF16), tiles], 4)(got_a, got_b, rows, band)
+    outs = [((BLOCKS, 16, FRAMES), BF16), tiles, ((128, 256), BF16)]
+    inner, x, band = call(inner_kernel, outs, 4, [pltpu.VMEM((16, 128), F32)])(
+        got_a, got_b, rows, jnp.transpose(filters, (0, 2, 1, 3))
+    )
     part, passed = ((SUMMED, HALF), F32), ((16, HALF), F32)
     edge, mine, other, passed = call(edge_kernel, [((16, FRAMES), BF16), part, part, passed], 5)(
         band, x, side, diag, inner

time: 38 us -> 37.7 us (level)
  waiting for transfers between devices: 11.3 us -> 11.7 us
    pallas_call x2 -> x1, Pallas kernels: 3.88 us -> 3.51 us  [on_device(): call(inner_kernel, outs, 4, [pltpu.VMEM((16, 128), F32)])]
where the time goes in v8:
time: 37.7 us; the launch traced here: 37.3 us
  starting transfers between devices  13.9 us (37%)
  waiting for transfers between devices  11.7 us (31%)
  Pallas kernels  9.66 us (26%)
  local copies, waits for them, and re-layouts  1.05 us (3%)
  between operations  0.78 us (2%)
    ppermute x2, starting transfers between devices, on_device(): got = lax.ppermute(mine, 'col', [(i, i ^ step) for i in range(size_col)])  5.52 us
    pallas_call x1, Pallas kernels, on_device(): call(kernel, [((MODES, FRAMES), F32), ((ROWS // 4, COLS // 4, ORIENT * MO...  4.72 us
    ppermute x2, waiting for transfers between devices, on_device(): got = lax.ppermute(mine, 'col', [(i, i ^ step) for i in range(size_col)])  4.48 us
    ppermute x1, starting transfers between devices, on_device(): mine = mine + lax.ppermute(other, 'row', near)  3.7 us
    pallas_call x1, Pallas kernels, on_device(): call(inner_kernel, outs, 4, [pltpu.VMEM((16, 128), F32)])  3.51 us
    ppermute x1, waiting for transfers between devices, on_device(): lax.ppermute(mine, 'row', [(i, i ^ step) for i in range(size_row)])  3.02 us
    ppermute x1, waiting for transfers between devices, on_device(): side = lax.ppermute(side, 'col', to_left)  1.65 us
    ppermute x1, starting transfers between devices, on_device(): lax.ppermute(mine, 'row', [(i, i ^ step) for i in range(size_row)])  1.48 us
  transfers between devices with their start and end apart: 9, of which 7 were waited for; matrix products, arithmetic and copies ran while one was open for 0% of the time, Pallas kernels for 11%

profile of v8, /device:TPU:0, one launch (start us, length us, event | category | flops | bytes accessed | tf_op | source)
XLA Modules:
  0.0 37.3 jit_solution(3999503372333430867)
XLA Ops:
  0.6 0.0 copy-start
  0.6 1.0 %copy-done = bf16[257,8,128]{2,1,0:T(8,128)(2,1)S(1)} copy-done((bf16[257,8,128]{2,1,0:T(8,128)(2,1)S(1)}, bf16[257,8,128]{2,1,0:T(8,128)(2,1)}, u32[]{:S(2)}) %copy-start) | copy-done | bytes 526360
  1.7 0.0 copy-start.2
  1.7 0.5 %shard_map.50 = (f32[2056,128]{1,0:T(8,128)S(1)}, bf16[400,256]{1,0:T(8,128)(2,1)S(1)}, bf16[400,256]{1,0:T(8,128)(2,1)S(1)}, f32[64,256]{1,0:T(8,128)S(1)}) custom-call(bf16[257,8,128]{2,1,0:T(8,128)(2,1)S(1)} %copy-done), custom_call_target="tpu_custom_call" | custom-call | tf_op jit(solution)/shard_map/pallas_call | solution.py:346
  2.1 0.5 %collective-permute-start = (bf16[400,256]{1,0:T(8,128)(2,1)S(1)}, bf16[400,256]{1,0:T(8,128)(2,1)S(1)}, u32[]{:S(2)}, u32[]{:S(2)}) collective-permute-start(bf16[400,256]{1,0:T(8,128)(2,1)S(1)} %get-tuple-element.19), channel_id=1, source_target_pairs={{0,4},{4,0},{8,12},{12,8},{1,5},{5,1},{9,13},{13,9},{2,6},{6,2},{1... | collective-permute-start | bytes 614408 | tf_op jit(solution)/shard_map/ppermute | solution.py:347
  2.7 0.7 %collective-permute-start.1 = (bf16[400,256]{1,0:T(8,128)(2,1)S(1)}, bf16[400,256]{1,0:T(8,128)(2,1)S(1)}, u32[]{:S(2)}, u32[]{:S(2)}) collective-permute-start(bf16[400,256]{1,0:T(8,128)(2,1)S(1)} %get-tuple-element.20), channel_id=1, source_target_pairs={{4,8},{8,4},{5,9},{9,5},{6,10},{10,6},{7,11},{11,7},{20,24},{24,20... | collective-permute-start | bytes 614408 | tf_op jit(solution)/shard_map/ppermute | solution.py:348
  3.3 0.4 %collective-permute-done.a_ref = bf16[400,256]{1,0:T(8,128)(2,1)S(1)} collective-permute-done((bf16[400,256]{1,0:T(8,128)(2,1)S(1)}, bf16[400,256]{1,0:T(8,128)(2,1)S(1)}, u32[]{:S(2)}, u32[]{:S(2)}) %collective-permute-start) | collective-permute-done | bytes 204832 | tf_op jit(solution)/shard_map/ppermute | solution.py:347
  3.7 0.2 shard_map.52
  3.9 1.3 %collective-permute-start.2 = (bf16[96,384]{1,0:T(8,128)(2,1)S(1)}, bf16[96,384]{1,0:T(8,128)(2,1)S(1)}, u32[]{:S(2)}, u32[]{:S(2)}) collective-permute-start(bf16[96,384]{1,0:T(8,128)(2,1)S(1)} %get-tuple-element.25), channel_id=1, source_target_pairs={{1,0},{2,1},{3,2},{5,4},{6,5},{7,6},{9,8},{10,9},{11,10},{13,12},{... | collective-permute-start | bytes 221192 | tf_op jit(solution)/shard_map/ppermute | solution.py:351
  5.2 0.7 %collective-permute-start.3 = (bf16[32,384]{1,0:T(8,128)(2,1)S(1)}, bf16[32,384]{1,0:T(8,128)(2,1)S(1)}, u32[]{:S(2)}, u32[]{:S(2)}) collective-permute-start(bf16[32,384]{1,0:T(8,128)(2,1)S(1)} %get-tuple-element.26), channel_id=1, source_target_pairs={{5,8},{6,9},{7,10},{9,4},{10,5},{11,6},{21,24},{22,25},{23,26},{25... | collective-permute-start | bytes 73736 | tf_op jit(solution)/shard_map/ppermute | solution.py:352
  5.9 0.0 collective-permute-done.1.b_ref
  5.9 0.0 copy-done.2
  5.9 3.5 %shard_map.51 = (bf16[16,16,256]{2,1,0:T(8,128)(2,1)S(1)}, bf16[17,112,384]{2,1,0:T(8,128)(2,1)S(1)}, bf16[128,256]{1,0:T(8,128)(2,1)S(1)}) custom-call(bf16[400,256]{1,0:T(8,128)(2,1)S(1)} %collective-permute-done.a_ref, bf16[400,256]{1,0:T(8,128)(2,1)S(1)} %collective-permute-done.1.b_ref, f32[2056,128]{1,0:T(8,128)S(1)} %get-tuple-element.21.rows_ref, ...), custom_call_target="tpu_custom_call" | custom-call | tf_op jit(solution)/shard_map/pallas_call | solution.py:355
  9.4 0.0 copy-start.1
  9.4 0.0 collective-permute-done.3.diag_ref
  9.4 1.6 %collective-permute-done.2.side_ref = bf16[96,384]{1,0:T(8,128)(2,1)S(1)} collective-permute-done((bf16[96,384]{1,0:T(8,128)(2,1)S(1)}, bf16[96,384]{1,0:T(8,128)(2,1)S(1)}, u32[]{:S(2)}, u32[]{:S(2)}) %collective-permute-start.2) | collective-permute-done | bytes 73760 | tf_op jit(solution)/shard_map/ppermute | solution.py:351
  11.1 0.6 %shard_map.53 = (bf16[16,256]{1,0:T(8,128)(2,1)S(1)}, f32[136,128]{1,0:T(8,128)S(1)}, f32[136,128]{1,0:T(8,128)S(1)}, f32[16,128]{1,0:T(8,128)S(1)}) custom-call(bf16[128,256]{1,0:T(8,128)(2,1)S(1)} %get-tuple-element.22.band_ref, bf16[17,112,384]{2,1,0:T(8,128)(2,1)S(1)} %get-tuple-element.23.x_ref, bf16[96,384]{1,0:T(8,128)(2,1)S(1)} %collective-permute-done.2.side_ref, ...), custom_call_target="tpu_custom_call" | custom-call | tf_op jit(solution)/shard_map/pallas_call | solution.py:359
  11.6 3.7 %collective-permute-start.4 = (f32[136,128]{1,0:T(8,128)S(1)}, f32[136,128]{1,0:T(8,128)S(1)}, u32[]{:S(2)}, u32[]{:S(2)}) collective-permute-start(f32[136,128]{1,0:T(8,128)S(1)} %get-tuple-element.29), channel_id=1, source_target_pairs={{0,4},{4,0},{8,12},{12,8},{1,5},{5,1},{9,13},{13,9},{2,6},{6,2},{1... | collective-permute-start | bytes 208904 | tf_op jit(solution)/shard_map/ppermute | solution.py:363
  15.3 0.9 %collective-permute-done.4 = f32[136,128]{1,0:T(8,128)S(1)} collective-permute-done((f32[136,128]{1,0:T(8,128)S(1)}, f32[136,128]{1,0:T(8,128)S(1)}, u32[]{:S(2)}, u32[]{:S(2)}) %collective-permute-start.4) | collective-permute-done | bytes 69664 | tf_op jit(solution)/shard_map/ppermute | solution.py:363
  16.3 1.5 %collective-permute-start.5 = (f32[136,128]{1,0:T(8,128)S(1)}, f32[136,128]{1,0:T(8,128)S(1)}, u32[]{:S(2)}, u32[]{:S(2)}) collective-permute-start(f32[136,128]{1,0:T(8,128)S(1)} %add.12), channel_id=1, source_target_pairs={{0,8},{4,12},{8,0},{12,4},{1,9},{5,13},{9,1},{13,5},{2,10},{6,14},... | collective-permute-start | bytes 208904 | tf_op jit(solution)/shard_map/ppermute | solution.py:366
  17.7 3.0 %collective-permute-done.5 = f32[136,128]{1,0:T(8,128)S(1)} collective-permute-done((f32[136,128]{1,0:T(8,128)S(1)}, f32[136,128]{1,0:T(8,128)S(1)}, u32[]{:S(2)}, u32[]{:S(2)}) %collective-permute-start.5) | collective-permute-done | bytes 69664 | tf_op jit(solution)/shard_map/ppermute | solution.py:366
  20.8 2.4 %collective-permute-start.6 = (f32[152,128]{1,0:T(8,128)S(1)}, f32[152,128]{1,0:T(8,128)S(1)}, u32[]{:S(2)}, u32[]{:S(2)}) collective-permute-start(f32[152,128]{1,0:T(8,128)S(1)} %pad_maximum_fusion), channel_id=1, source_target_pairs={{0,1},{1,0},{2,3},{3,2},{4,5},{5,4},{6,7},{7,6},{8,9},{9,8},{10,11... | collective-permute-start | bytes 233480 | tf_op jit(solution)/shard_map/ppermute | solution.py:378
  23.2 2.4 %collective-permute-done.6 = f32[152,128]{1,0:T(8,128)S(1)} collective-permute-done((f32[152,128]{1,0:T(8,128)S(1)}, f32[152,128]{1,0:T(8,128)S(1)}, u32[]{:S(2)}, u32[]{:S(2)}) %collective-permute-start.6) | collective-permute-done | bytes 77856 | tf_op jit(solution)/shard_map/ppermute | solution.py:378
  25.6 0.1 add_select_fusion
  25.7 3.1 %collective-permute-start.7 = (f32[152,128]{1,0:T(8,128)S(1)}, f32[152,128]{1,0:T(8,128)S(1)}, u32[]{:S(2)}, u32[]{:S(2)}) collective-permute-start(f32[152,128]{1,0:T(8,128)S(1)} %add_select_fusion), channel_id=1, source_target_pairs={{0,2},{1,3},{2,0},{3,1},{4,6},{5,7},{6,4},{7,5},{8,10},{9,11},{10,... | collective-permute-start | bytes 233480 | tf_op jit(solution)/shard_map/ppermute | solution.py:378
  28.8 0.0 copy-done.1
  28.8 0.3 shard_map.54.start_ref
  29.1 2.1 %collective-permute-done.7 = f32[152,128]{1,0:T(8,128)S(1)} collective-permute-done((f32[152,128]{1,0:T(8,128)S(1)}, f32[152,128]{1,0:T(8,128)S(1)}, u32[]{:S(2)}, u32[]{:S(2)}) %collective-permute-start.7) | collective-permute-done | bytes 77856 | tf_op jit(solution)/shard_map/ppermute | solution.py:378
  31.2 0.1 add_select_fusion.1.mine_ref
  31.3 0.1 collective-permute-start.8
  31.4 1.2 %collective-permute-done.8.other_ref = f32[136,128]{1,0:T(8,128)S(1)} collective-permute-done((f32[136,128]{1,0:T(8,128)S(1)}, f32[136,128]{1,0:T(8,128)S(1)}, u32[]{:S(2)}, u32[]{:S(2)}) %collective-permute-start.8) | collective-permute-done | bytes 69664 | tf_op jit(solution)/shard_map/ppermute | solution.py:383
  32.6 4.7 %shard_map.55 = (f32[64,256]{1,0:T(8,128)}, f32[2,32,256]{2,1,0:T(8,128)}) custom-call(f32[136,128]{1,0:T(8,128)S(1)} %add_select_fusion.1.mine_ref, f32[136,128]{1,0:T(8,128)S(1)} %collective-permute-done.8.other_ref, f32[64,256]{1,0:T(8,128)S(1)} %shard_map.54.start_ref, bf16[16,16,256]{2,1,0:T(8,128)(2,1)S(1)} %get-tuple-element.27.inner_ref, ...), custom_call_target="tpu_custom_call" | custom-call | tf_op jit(solution)/shard_map/pallas_call | solution.py:387
  (5 shorter events, 0.0 us)
Async XLA Ops:
  0.6 1.0 %copy-start = (bf16[257,8,128]{2,1,0:T(8,128)(2,1)S(1)}, bf16[257,8,128]{2,1,0:T(8,128)(2,1)}, u32[]{:S(2)}) copy-start(bf16[257,8,128]{2,1,0:T(8,128)(2,1)} %video_ref.1) | copy-start | bytes 1579012
  1.7 4.2 %copy-start.2 = (f32[4,2,7,7]{3,1,2,0:T(2,128)S(1)}, f32[4,2,7,7]{3,1,2,0:T(2,128)}, u32[]{:S(2)}) copy-start(f32[4,2,7,7]{3,1,2,0:T(2,128)} %param.4) | copy-start | bytes 4708
  2.1 1.6 %collective-permute-start = (bf16[400,256]{1,0:T(8,128)(2,1)S(1)}, bf16[400,256]{1,0:T(8,128)(2,1)S(1)}, u32[]{:S(2)}, u32[]{:S(2)}) collective-permute-start(bf16[400,256]{1,0:T(8,128)(2,1)S(1)} %get-tuple-element.19), channel_id=1, source_target_pairs={{0,4},{4,0},{8,12},{12,8},{1,5},{5,1},{9,13},{13,9},{2,6},{6,2},{1... | collective-permute-start | bytes 614408 | tf_op jit(solution)/shard_map/ppermute | solution.py:347
  2.7 3.2 %collective-permute-start.1 = (bf16[400,256]{1,0:T(8,128)(2,1)S(1)}, bf16[400,256]{1,0:T(8,128)(2,1)S(1)}, u32[]{:S(2)}, u32[]{:S(2)}) collective-permute-start(bf16[400,256]{1,0:T(8,128)(2,1)S(1)} %get-tuple-element.20), channel_id=1, source_target_pairs={{4,8},{8,4},{5,9},{9,5},{6,10},{10,6},{7,11},{11,7},{20,24},{24,20... | collective-permute-start | bytes 614408 | tf_op jit(solution)/shard_map/ppermute | solution.py:348
  3.9 7.2 %collective-permute-start.2 = (bf16[96,384]{1,0:T(8,128)(2,1)S(1)}, bf16[96,384]{1,0:T(8,128)(2,1)S(1)}, u32[]{:S(2)}, u32[]{:S(2)}) collective-permute-start(bf16[96,384]{1,0:T(8,128)(2,1)S(1)} %get-tuple-element.25), channel_id=1, source_target_pairs={{1,0},{2,1},{3,2},{5,4},{6,5},{7,6},{9,8},{10,9},{11,10},{13,12},{... | collective-permute-start | bytes 221192 | tf_op jit(solution)/shard_map/ppermute | solution.py:351
  5.2 4.2 %collective-permute-start.3 = (bf16[32,384]{1,0:T(8,128)(2,1)S(1)}, bf16[32,384]{1,0:T(8,128)(2,1)S(1)}, u32[]{:S(2)}, u32[]{:S(2)}) collective-permute-start(bf16[32,384]{1,0:T(8,128)(2,1)S(1)} %get-tuple-element.26), channel_id=1, source_target_pairs={{5,8},{6,9},{7,10},{9,4},{10,5},{11,6},{21,24},{22,25},{23,26},{25... | collective-permute-start | bytes 73736 | tf_op jit(solution)/shard_map/ppermute | solution.py:352
  9.4 19.4 %copy-start.1 = (f32[256,64]{0,1:T(8,128)S(1)}, f32[256,64]{0,1:T(8,128)}, u32[]{:S(2)}) copy-start(f32[256,64]{0,1:T(8,128)} %param.5) | copy-start | bytes 196612
  11.6 4.6 %collective-permute-start.4 = (f32[136,128]{1,0:T(8,128)S(1)}, f32[136,128]{1,0:T(8,128)S(1)}, u32[]{:S(2)}, u32[]{:S(2)}) collective-permute-start(f32[136,128]{1,0:T(8,128)S(1)} %get-tuple-element.29), channel_id=1, source_target_pairs={{0,4},{4,0},{8,12},{12,8},{1,5},{5,1},{9,13},{13,9},{2,6},{6,2},{1... | collective-permute-start | bytes 208904 | tf_op jit(solution)/shard_map/ppermute | solution.py:363
  16.3 4.5 %collective-permute-start.5 = (f32[136,128]{1,0:T(8,128)S(1)}, f32[136,128]{1,0:T(8,128)S(1)}, u32[]{:S(2)}, u32[]{:S(2)}) collective-permute-start(f32[136,128]{1,0:T(8,128)S(1)} %add.12), channel_id=1, source_target_pairs={{0,8},{4,12},{8,0},{12,4},{1,9},{5,13},{9,1},{13,5},{2,10},{6,14},... | collective-permute-start | bytes 208904 | tf_op jit(solution)/shard_map/ppermute | solution.py:366
  20.8 4.8 %collective-permute-start.6 = (f32[152,128]{1,0:T(8,128)S(1)}, f32[152,128]{1,0:T(8,128)S(1)}, u32[]{:S(2)}, u32[]{:S(2)}) collective-permute-start(f32[152,128]{1,0:T(8,128)S(1)} %pad_maximum_fusion), channel_id=1, source_target_pairs={{0,1},{1,0},{2,3},{3,2},{4,5},{5,4},{6,7},{7,6},{8,9},{9,8},{10,11... | collective-permute-start | bytes 233480 | tf_op jit(solution)/shard_map/ppermute | solution.py:378
  25.7 5.5 %collective-permute-start.7 = (f32[152,128]{1,0:T(8,128)S(1)}, f32[152,128]{1,0:T(8,128)S(1)}, u32[]{:S(2)}, u32[]{:S(2)}) collective-permute-start(f32[152,128]{1,0:T(8,128)S(1)} %add_select_fusion), channel_id=1, source_target_pairs={{0,2},{1,3},{2,0},{3,1},{4,6},{5,7},{6,4},{7,5},{8,10},{9,11},{10,... | collective-permute-start | bytes 233480 | tf_op jit(solution)/shard_map/ppermute | solution.py:378
  31.3 1.3 %collective-permute-start.8 = (f32[136,128]{1,0:T(8,128)S(1)}, f32[136,128]{1,0:T(8,128)S(1)}, u32[]{:S(2)}, u32[]{:S(2)}) collective-permute-start(f32[136,128]{1,0:T(8,128)S(1)} %add_select_fusion.1.mine_ref), channel_id=1, source_target_pairs={{0,4},{4,0},{8,12},{12,8},{1,5},{5,1},{9,13},{13,9},{2,6},{6,2},{1... | collective-permute-start | bytes 208904 | tf_op jit(solution)/shard_map/ppermute | solution.py:383

commit v9 on v8

--- a/solution.py
+++ b/solution.py
@@ -18,7 +18,7 @@
 COLS = 128
 SUMMED = HALF + 8
 BLOCKS = 16
-UNROLL = 8
+UNROLL = 16
 AHEAD = 3
 F32 = jnp.float32
 BF16 = jnp.bfloat16

time: 37.7 us -> 37.5 us (level)
  waiting for transfers between devices: 11.7 us -> 12.4 us
  Pallas kernels: 9.66 us -> 9.26 us
    pallas_call x1, Pallas kernels: 3.51 us -> 3.11 us  [on_device(): call(inner_kernel, outs, 4, [pltpu.VMEM((16, 128), F32)])]
    ppermute x1, waiting for transfers between devices: 1.65 us -> 2.05 us  [on_device(): side = lax.ppermute(side, 'col', to_left)]
  transfers between devices with their start and end apart: 9 -> 9, of which waited for: 7 -> 7; matrix products, arithmetic and copies ran while one was open for 0% -> 0% of each run, Pallas kernels for 11% -> 9%
where the time goes in v9:
time: 37.5 us; the launch traced here: 37.3 us
  starting transfers between devices  13.6 us (36%)
  waiting for transfers between devices  12.4 us (33%)
  Pallas kernels  9.26 us (25%)
  local copies, waits for them, and re-layouts  1.05 us (3%)
  between operations  0.78 us (2%)
    ppermute x2, starting transfers between devices, on_device(): got = lax.ppermute(mine, 'col', [(i, i ^ step) for i in range(size_col)])  5.52 us
    pallas_call x1, Pallas kernels, on_device(): call(kernel, [((MODES, FRAMES), F32), ((ROWS // 4, COLS // 4, ORIENT * MO...  4.72 us
    ppermute x2, waiting for transfers between devices, on_device(): got = lax.ppermute(mine, 'col', [(i, i ^ step) for i in range(size_col)])  4.48 us
    ppermute x1, starting transfers between devices, on_device(): mine = mine + lax.ppermute(other, 'row', near)  3.7 us
    ppermute x1, waiting for transfers between devices, on_device(): lax.ppermute(mine, 'row', [(i, i ^ step) for i in range(size_row)])  3.29 us
    pallas_call x1, Pallas kernels, on_device(): call(inner_kernel, outs, 4, [pltpu.VMEM((16, 128), F32)])  3.11 us
    ppermute x1, waiting for transfers between devices, on_device(): side = lax.ppermute(side, 'col', to_left)  2.05 us
    ppermute x1, starting transfers between devices, on_device(): side = lax.ppermute(side, 'col', to_left)  1.29 us
  transfers between devices with their start and end apart: 9, of which 7 were waited for; matrix products, arithmetic and copies ran while one was open for 0% of the time, Pallas kernels for 9%

profile of v9, /device:TPU:0, one launch (start us, length us, event | category | flops | bytes accessed | tf_op | source)
XLA Modules:
  0.0 37.3 jit_solution(17098662628678746102)
XLA Ops:
  0.6 0.0 copy-start
  0.6 1.0 %copy-done = bf16[257,8,128]{2,1,0:T(8,128)(2,1)S(1)} copy-done((bf16[257,8,128]{2,1,0:T(8,128)(2,1)S(1)}, bf16[257,8,128]{2,1,0:T(8,128)(2,1)}, u32[]{:S(2)}) %copy-start) | copy-done | bytes 526360
  1.7 0.0 copy-start.2
  1.7 0.5 %shard_map.50 = (f32[2056,128]{1,0:T(8,128)S(1)}, bf16[400,256]{1,0:T(8,128)(2,1)S(1)}, bf16[400,256]{1,0:T(8,128)(2,1)S(1)}, f32[64,256]{1,0:T(8,128)S(1)}) custom-call(bf16[257,8,128]{2,1,0:T(8,128)(2,1)S(1)} %copy-done), custom_call_target="tpu_custom_call" | custom-call | tf_op jit(solution)/shard_map/pallas_call | solution.py:346
  2.1 0.5 %collective-permute-start = (bf16[400,256]{1,0:T(8,128)(2,1)S(1)}, bf16[400,256]{1,0:T(8,128)(2,1)S(1)}, u32[]{:S(2)}, u32[]{:S(2)}) collective-permute-start(bf16[400,256]{1,0:T(8,128)(2,1)S(1)} %get-tuple-element.19), channel_id=1, source_target_pairs={{0,4},{4,0},{8,12},{12,8},{1,5},{5,1},{9,13},{13,9},{2,6},{6,2},{1... | collective-permute-start | bytes 614408 | tf_op jit(solution)/shard_map/ppermute | solution.py:347
  2.7 0.7 %collective-permute-start.1 = (bf16[400,256]{1,0:T(8,128)(2,1)S(1)}, bf16[400,256]{1,0:T(8,128)(2,1)S(1)}, u32[]{:S(2)}, u32[]{:S(2)}) collective-permute-start(bf16[400,256]{1,0:T(8,128)(2,1)S(1)} %get-tuple-element.20), channel_id=1, source_target_pairs={{4,8},{8,4},{5,9},{9,5},{6,10},{10,6},{7,11},{11,7},{20,24},{24,20... | collective-permute-start | bytes 614408 | tf_op jit(solution)/shard_map/ppermute | solution.py:348
  3.3 0.4 %collective-permute-done.a_ref = bf16[400,256]{1,0:T(8,128)(2,1)S(1)} collective-permute-done((bf16[400,256]{1,0:T(8,128)(2,1)S(1)}, bf16[400,256]{1,0:T(8,128)(2,1)S(1)}, u32[]{:S(2)}, u32[]{:S(2)}) %collective-permute-start) | collective-permute-done | bytes 204832 | tf_op jit(solution)/shard_map/ppermute | solution.py:347
  3.7 0.2 shard_map.52
  3.9 1.3 %collective-permute-start.2 = (bf16[96,384]{1,0:T(8,128)(2,1)S(1)}, bf16[96,384]{1,0:T(8,128)(2,1)S(1)}, u32[]{:S(2)}, u32[]{:S(2)}) collective-permute-start(bf16[96,384]{1,0:T(8,128)(2,1)S(1)} %get-tuple-element.25), channel_id=1, source_target_pairs={{1,0},{2,1},{3,2},{5,4},{6,5},{7,6},{9,8},{10,9},{11,10},{13,12},{... | collective-permute-start | bytes 221192 | tf_op jit(solution)/shard_map/ppermute | solution.py:351
  5.2 0.7 %collective-permute-start.3 = (bf16[32,384]{1,0:T(8,128)(2,1)S(1)}, bf16[32,384]{1,0:T(8,128)(2,1)S(1)}, u32[]{:S(2)}, u32[]{:S(2)}) collective-permute-start(bf16[32,384]{1,0:T(8,128)(2,1)S(1)} %get-tuple-element.26), channel_id=1, source_target_pairs={{5,8},{6,9},{7,10},{9,4},{10,5},{11,6},{21,24},{22,25},{23,26},{25... | collective-permute-start | bytes 73736 | tf_op jit(solution)/shard_map/ppermute | solution.py:352
  5.9 0.0 collective-permute-done.1.b_ref
  5.9 0.0 copy-done.2
  5.9 3.1 %shard_map.51 = (bf16[16,16,256]{2,1,0:T(8,128)(2,1)S(1)}, bf16[17,112,384]{2,1,0:T(8,128)(2,1)S(1)}, bf16[128,256]{1,0:T(8,128)(2,1)S(1)}) custom-call(bf16[400,256]{1,0:T(8,128)(2,1)S(1)} %collective-permute-done.a_ref, bf16[400,256]{1,0:T(8,128)(2,1)S(1)} %collective-permute-done.1.b_ref, f32[2056,128]{1,0:T(8,128)S(1)} %get-tuple-element.21.rows_ref, ...), custom_call_target="tpu_custom_call" | custom-call | tf_op jit(solution)/shard_map/pallas_call | solution.py:355
  9.0 0.0 copy-start.1
  9.0 0.0 collective-permute-done.3.diag_ref
  9.0 2.0 %collective-permute-done.2.side_ref = bf16[96,384]{1,0:T(8,128)(2,1)S(1)} collective-permute-done((bf16[96,384]{1,0:T(8,128)(2,1)S(1)}, bf16[96,384]{1,0:T(8,128)(2,1)S(1)}, u32[]{:S(2)}, u32[]{:S(2)}) %collective-permute-start.2) | collective-permute-done | bytes 73760 | tf_op jit(solution)/shard_map/ppermute | solution.py:351
  11.1 0.6 %shard_map.53 = (bf16[16,256]{1,0:T(8,128)(2,1)S(1)}, f32[136,128]{1,0:T(8,128)S(1)}, f32[136,128]{1,0:T(8,128)S(1)}, f32[16,128]{1,0:T(8,128)S(1)}) custom-call(bf16[128,256]{1,0:T(8,128)(2,1)S(1)} %get-tuple-element.22.band_ref, bf16[17,112,384]{2,1,0:T(8,128)(2,1)S(1)} %get-tuple-element.23.x_ref, bf16[96,384]{1,0:T(8,128)(2,1)S(1)} %collective-permute-done.2.side_ref, ...), custom_call_target="tpu_custom_call" | custom-call | tf_op jit(solution)/shard_map/pallas_call | solution.py:359
  11.6 3.7 %collective-permute-start.4 = (f32[136,128]{1,0:T(8,128)S(1)}, f32[136,128]{1,0:T(8,128)S(1)}, u32[]{:S(2)}, u32[]{:S(2)}) collective-permute-start(f32[136,128]{1,0:T(8,128)S(1)} %get-tuple-element.29), channel_id=1, source_target_pairs={{0,4},{4,0},{8,12},{12,8},{1,5},{5,1},{9,13},{13,9},{2,6},{6,2},{1... | collective-permute-start | bytes 208904 | tf_op jit(solution)/shard_map/ppermute | solution.py:363
  15.3 0.9 %collective-permute-done.4 = f32[136,128]{1,0:T(8,128)S(1)} collective-permute-done((f32[136,128]{1,0:T(8,128)S(1)}, f32[136,128]{1,0:T(8,128)S(1)}, u32[]{:S(2)}, u32[]{:S(2)}) %collective-permute-start.4) | collective-permute-done | bytes 69664 | tf_op jit(solution)/shard_map/ppermute | solution.py:363
  16.3 1.2 %collective-permute-start.5 = (f32[136,128]{1,0:T(8,128)S(1)}, f32[136,128]{1,0:T(8,128)S(1)}, u32[]{:S(2)}, u32[]{:S(2)}) collective-permute-start(f32[136,128]{1,0:T(8,128)S(1)} %add.12), channel_id=1, source_target_pairs={{0,8},{4,12},{8,0},{12,4},{1,9},{5,13},{9,1},{13,5},{2,10},{6,14},... | collective-permute-start | bytes 208904 | tf_op jit(solution)/shard_map/ppermute | solution.py:366
  17.5 3.3 %collective-permute-done.5 = f32[136,128]{1,0:T(8,128)S(1)} collective-permute-done((f32[136,128]{1,0:T(8,128)S(1)}, f32[136,128]{1,0:T(8,128)S(1)}, u32[]{:S(2)}, u32[]{:S(2)}) %collective-permute-start.5) | collective-permute-done | bytes 69664 | tf_op jit(solution)/shard_map/ppermute | solution.py:366
  20.8 2.4 %collective-permute-start.6 = (f32[152,128]{1,0:T(8,128)S(1)}, f32[152,128]{1,0:T(8,128)S(1)}, u32[]{:S(2)}, u32[]{:S(2)}) collective-permute-start(f32[152,128]{1,0:T(8,128)S(1)} %pad_maximum_fusion), channel_id=1, source_target_pairs={{0,1},{1,0},{2,3},{3,2},{4,5},{5,4},{6,7},{7,6},{8,9},{9,8},{10,11... | collective-permute-start | bytes 233480 | tf_op jit(solution)/shard_map/ppermute | solution.py:378
  23.2 2.4 %collective-permute-done.6 = f32[152,128]{1,0:T(8,128)S(1)} collective-permute-done((f32[152,128]{1,0:T(8,128)S(1)}, f32[152,128]{1,0:T(8,128)S(1)}, u32[]{:S(2)}, u32[]{:S(2)}) %collective-permute-start.6) | collective-permute-done | bytes 77856 | tf_op jit(solution)/shard_map/ppermute | solution.py:378
  25.6 0.1 add_select_fusion
  25.7 3.1 %collective-permute-start.7 = (f32[152,128]{1,0:T(8,128)S(1)}, f32[152,128]{1,0:T(8,128)S(1)}, u32[]{:S(2)}, u32[]{:S(2)}) collective-permute-start(f32[152,128]{1,0:T(8,128)S(1)} %add_select_fusion), channel_id=1, source_target_pairs={{0,2},{1,3},{2,0},{3,1},{4,6},{5,7},{6,4},{7,5},{8,10},{9,11},{10,... | collective-permute-start | bytes 233480 | tf_op jit(solution)/shard_map/ppermute | solution.py:378
  28.8 0.0 copy-done.1
  28.8 0.3 shard_map.54.start_ref
  29.1 2.1 %collective-permute-done.7 = f32[152,128]{1,0:T(8,128)S(1)} collective-permute-done((f32[152,128]{1,0:T(8,128)S(1)}, f32[152,128]{1,0:T(8,128)S(1)}, u32[]{:S(2)}, u32[]{:S(2)}) %collective-permute-start.7) | collective-permute-done | bytes 77856 | tf_op jit(solution)/shard_map/ppermute | solution.py:378
  31.2 0.1 add_select_fusion.1.mine_ref
  31.3 0.1 collective-permute-start.8
  31.4 1.2 %collective-permute-done.8.other_ref = f32[136,128]{1,0:T(8,128)S(1)} collective-permute-done((f32[136,128]{1,0:T(8,128)S(1)}, f32[136,128]{1,0:T(8,128)S(1)}, u32[]{:S(2)}, u32[]{:S(2)}) %collective-permute-start.8) | collective-permute-done | bytes 69664 | tf_op jit(solution)/shard_map/ppermute | solution.py:383
  32.6 4.7 %shard_map.55 = (f32[64,256]{1,0:T(8,128)}, f32[2,32,256]{2,1,0:T(8,128)}) custom-call(f32[136,128]{1,0:T(8,128)S(1)} %add_select_fusion.1.mine_ref, f32[136,128]{1,0:T(8,128)S(1)} %collective-permute-done.8.other_ref, f32[64,256]{1,0:T(8,128)S(1)} %shard_map.54.start_ref, bf16[16,16,256]{2,1,0:T(8,128)(2,1)S(1)} %get-tuple-element.27.inner_ref, ...), custom_call_target="tpu_custom_call" | custom-call | tf_op jit(solution)/shard_map/pallas_call | solution.py:387
  (5 shorter events, 0.0 us)
Async XLA Ops:
  0.6 1.0 %copy-start = (bf16[257,8,128]{2,1,0:T(8,128)(2,1)S(1)}, bf16[257,8,128]{2,1,0:T(8,128)(2,1)}, u32[]{:S(2)}) copy-start(bf16[257,8,128]{2,1,0:T(8,128)(2,1)} %video_ref.1) | copy-start | bytes 1579012
  1.7 4.2 %copy-start.2 = (f32[4,2,7,7]{3,1,2,0:T(2,128)S(1)}, f32[4,2,7,7]{3,1,2,0:T(2,128)}, u32[]{:S(2)}) copy-start(f32[4,2,7,7]{3,1,2,0:T(2,128)} %param.4) | copy-start | bytes 4708
  2.1 1.6 %collective-permute-start = (bf16[400,256]{1,0:T(8,128)(2,1)S(1)}, bf16[400,256]{1,0:T(8,128)(2,1)S(1)}, u32[]{:S(2)}, u32[]{:S(2)}) collective-permute-start(bf16[400,256]{1,0:T(8,128)(2,1)S(1)} %get-tuple-element.19), channel_id=1, source_target_pairs={{0,4},{4,0},{8,12},{12,8},{1,5},{5,1},{9,13},{13,9},{2,6},{6,2},{1... | collective-permute-start | bytes 614408 | tf_op jit(solution)/shard_map/ppermute | solution.py:347
  2.7 3.2 %collective-permute-start.1 = (bf16[400,256]{1,0:T(8,128)(2,1)S(1)}, bf16[400,256]{1,0:T(8,128)(2,1)S(1)}, u32[]{:S(2)}, u32[]{:S(2)}) collective-permute-start(bf16[400,256]{1,0:T(8,128)(2,1)S(1)} %get-tuple-element.20), channel_id=1, source_target_pairs={{4,8},{8,4},{5,9},{9,5},{6,10},{10,6},{7,11},{11,7},{20,24},{24,20... | collective-permute-start | bytes 614408 | tf_op jit(solution)/shard_map/ppermute | solution.py:348
  3.9 7.2 %collective-permute-start.2 = (bf16[96,384]{1,0:T(8,128)(2,1)S(1)}, bf16[96,384]{1,0:T(8,128)(2,1)S(1)}, u32[]{:S(2)}, u32[]{:S(2)}) collective-permute-start(bf16[96,384]{1,0:T(8,128)(2,1)S(1)} %get-tuple-element.25), channel_id=1, source_target_pairs={{1,0},{2,1},{3,2},{5,4},{6,5},{7,6},{9,8},{10,9},{11,10},{13,12},{... | collective-permute-start | bytes 221192 | tf_op jit(solution)/shard_map/ppermute | solution.py:351
  5.2 3.8 %collective-permute-start.3 = (bf16[32,384]{1,0:T(8,128)(2,1)S(1)}, bf16[32,384]{1,0:T(8,128)(2,1)S(1)}, u32[]{:S(2)}, u32[]{:S(2)}) collective-permute-start(bf16[32,384]{1,0:T(8,128)(2,1)S(1)} %get-tuple-element.26), channel_id=1, source_target_pairs={{5,8},{6,9},{7,10},{9,4},{10,5},{11,6},{21,24},{22,25},{23,26},{25... | collective-permute-start | bytes 73736 | tf_op jit(solution)/shard_map/ppermute | solution.py:352
  9.0 19.8 %copy-start.1 = (f32[256,64]{0,1:T(8,128)S(1)}, f32[256,64]{0,1:T(8,128)}, u32[]{:S(2)}) copy-start(f32[256,64]{0,1:T(8,128)} %param.5) | copy-start | bytes 196612
  11.6 4.6 %collective-permute-start.4 = (f32[136,128]{1,0:T(8,128)S(1)}, f32[136,128]{1,0:T(8,128)S(1)}, u32[]{:S(2)}, u32[]{:S(2)}) collective-permute-start(f32[136,128]{1,0:T(8,128)S(1)} %get-tuple-element.29), channel_id=1, source_target_pairs={{0,4},{4,0},{8,12},{12,8},{1,5},{5,1},{9,13},{13,9},{2,6},{6,2},{1... | collective-permute-start | bytes 208904 | tf_op jit(solution)/shard_map/ppermute | solution.py:363
  16.3 4.5 %collective-permute-start.5 = (f32[136,128]{1,0:T(8,128)S(1)}, f32[136,128]{1,0:T(8,128)S(1)}, u32[]{:S(2)}, u32[]{:S(2)}) collective-permute-start(f32[136,128]{1,0:T(8,128)S(1)} %add.12), channel_id=1, source_target_pairs={{0,8},{4,12},{8,0},{12,4},{1,9},{5,13},{9,1},{13,5},{2,10},{6,14},... | collective-permute-start | bytes 208904 | tf_op jit(solution)/shard_map/ppermute | solution.py:366
  20.8 4.8 %collective-permute-start.6 = (f32[152,128]{1,0:T(8,128)S(1)}, f32[152,128]{1,0:T(8,128)S(1)}, u32[]{:S(2)}, u32[]{:S(2)}) collective-permute-start(f32[152,128]{1,0:T(8,128)S(1)} %pad_maximum_fusion), channel_id=1, source_target_pairs={{0,1},{1,0},{2,3},{3,2},{4,5},{5,4},{6,7},{7,6},{8,9},{9,8},{10,11... | collective-permute-start | bytes 233480 | tf_op jit(solution)/shard_map/ppermute | solution.py:378
  25.7 5.5 %collective-permute-start.7 = (f32[152,128]{1,0:T(8,128)S(1)}, f32[152,128]{1,0:T(8,128)S(1)}, u32[]{:S(2)}, u32[]{:S(2)}) collective-permute-start(f32[152,128]{1,0:T(8,128)S(1)} %add_select_fusion), channel_id=1, source_target_pairs={{0,2},{1,3},{2,0},{3,1},{4,6},{5,7},{6,4},{7,5},{8,10},{9,11},{10,... | collective-permute-start | bytes 233480 | tf_op jit(solution)/shard_map/ppermute | solution.py:378
  31.3 1.3 %collective-permute-start.8 = (f32[136,128]{1,0:T(8,128)S(1)}, f32[136,128]{1,0:T(8,128)S(1)}, u32[]{:S(2)}, u32[]{:S(2)}) collective-permute-start(f32[136,128]{1,0:T(8,128)S(1)} %add_select_fusion.1.mine_ref), channel_id=1, source_target_pairs={{0,4},{4,0},{8,12},{12,8},{1,5},{5,1},{9,13},{13,9},{2,6},{6,2},{1... | collective-permute-start | bytes 208904 | tf_op jit(solution)/shard_map/ppermute | solution.py:383

commit v10 on v9

--- a/solution.py
+++ b/solution.py
@@ -63,16 +63,15 @@
 
 def side_kernel(rows_ref, heads_ref, a_ref, side_ref, diag_ref):
     even = is_even("row")
-    fill = jnp.zeros((8, HALF), F32)
     ends = rows_ref[FRAMES * ROWS : FRAMES * ROWS + ROWS, :]
     heads = in_groups([heads_ref[8 * i : 8 * i + 8] for i in range(ROWS)], ends)
     near = expanded(a_ref[...].astype(F32), 8)
     for group in range(3):
         lanes = slice(HALF * group, HALF * group + HALF)
-        sent = [row[group] for row in heads + near] + [fill]
+        sent = [row[group] for row in heads + near]
         side_ref[:, lanes] = jnp.concatenate(sent, axis=0).astype(BF16)
         chosen = [jnp.where(even, heads[i][group], heads[ROWS - REACH + i][group]) for i in range(REACH)]
-        diag_ref[:, lanes] = jnp.concatenate(chosen + [fill], axis=0).astype(BF16)
+        diag_ref[:, lanes] = jnp.concatenate(chosen, axis=0).astype(BF16)
 
 
 def in_groups(tiles, ends):
@@ -197,7 +196,7 @@
 def edge_kernel(band_ref, x_ref, side_ref, diag_ref, inner_ref, edge_ref, mine_ref, other_ref, passed_ref):
     even = is_even("row")
     side = side_ref[...].astype(F32)
-    near, far = side[8 * ROWS : 8 * ROWS + 8 * REACH], diag_ref[...].astype(F32)[: 8 * REACH]
+    near, far = side[8 * ROWS : 8 * ROWS + 8 * REACH], diag_ref[...].astype(F32)
     rows = [jnp.where(even, far, near), side[: 8 * ROWS], jnp.where(even, near, far)]
     edge = block_feats(band_ref, x_ref[BLOCKS], jnp.concatenate(rows, axis=0).astype(BF16))
     ends = lax.axis_index("col") == lax.axis_size("col") - 1
@@ -346,7 +345,7 @@
     rows, send_a, send_b, heads = call(send_kernel, [rows, send, send, ((8 * ROWS, FRAMES), F32)], 1)(video)
     got_a = lax.ppermute(send_a, "row", near)
     got_b = lax.ppermute(send_b, "row", far)
-    outs = [((96, 3 * HALF), BF16), ((32, 3 * HALF), BF16)]
+    outs = [((8 * ROWS + 8 * REACH, 3 * HALF), BF16), ((8 * REACH, 3 * HALF), BF16)]
     side, diag = call(side_kernel, outs, 3)(rows, heads, got_a)
     side = lax.ppermute(side, "col", to_left)
     diag = lax.ppermute(diag, ("row", "col"), across)

time: 37.5 us -> 37.5 us (level)
  no operation moved by 1% of the time
where the time goes in v10:
time: 37.5 us; the launch traced here: 37.3 us
  starting transfers between devices  13.6 us (36%)
  waiting for transfers between devices  12.3 us (33%)
  Pallas kernels  9.25 us (25%)
  local copies, waits for them, and re-layouts  1.05 us (3%)
  between operations  0.78 us (2%)
    ppermute x2, starting transfers between devices, on_device(): got = lax.ppermute(mine, 'col', [(i, i ^ step) for i in range(size_col)])  5.53 us
    pallas_call x1, Pallas kernels, on_device(): call(kernel, [((MODES, FRAMES), F32), ((ROWS // 4, COLS // 4, ORIENT * MO...  4.72 us
    ppermute x2, waiting for transfers between devices, on_device(): got = lax.ppermute(mine, 'col', [(i, i ^ step) for i in range(size_col)])  4.48 us
    ppermute x1, starting transfers between devices, on_device(): mine = mine + lax.ppermute(other, 'row', near)  3.7 us
    ppermute x1, waiting for transfers between devices, on_device(): lax.ppermute(mine, 'row', [(i, i ^ step) for i in range(size_row)])  3.29 us
    pallas_call x1, Pallas kernels, on_device(): call(inner_kernel, outs, 4, [pltpu.VMEM((16, 128), F32)])  3.08 us
    ppermute x1, waiting for transfers between devices, on_device(): side = lax.ppermute(side, 'col', to_left)  2.01 us
    ppermute x1, starting transfers between devices, on_device(): side = lax.ppermute(side, 'col', to_left)  1.29 us
  transfers between devices with their start and end apart: 9, of which 7 were waited for; matrix products, arithmetic and copies ran while one was open for 0% of the time, Pallas kernels for 9%

profile of v10, /device:TPU:0, one launch (start us, length us, event | category | flops | bytes accessed | tf_op | source)
XLA Modules:
  0.0 37.3 jit_solution(16698606547149447568)
XLA Ops:
  0.6 0.0 copy-start
  0.6 1.0 %copy-done = bf16[257,8,128]{2,1,0:T(8,128)(2,1)S(1)} copy-done((bf16[257,8,128]{2,1,0:T(8,128)(2,1)S(1)}, bf16[257,8,128]{2,1,0:T(8,128)(2,1)}, u32[]{:S(2)}) %copy-start) | copy-done | bytes 526360
  1.7 0.0 copy-start.2
  1.7 0.5 %shard_map.50 = (f32[2056,128]{1,0:T(8,128)S(1)}, bf16[400,256]{1,0:T(8,128)(2,1)S(1)}, bf16[400,256]{1,0:T(8,128)(2,1)S(1)}, f32[64,256]{1,0:T(8,128)S(1)}) custom-call(bf16[257,8,128]{2,1,0:T(8,128)(2,1)S(1)} %copy-done), custom_call_target="tpu_custom_call" | custom-call | tf_op jit(solution)/shard_map/pallas_call | solution.py:345
  2.1 0.5 %collective-permute-start = (bf16[400,256]{1,0:T(8,128)(2,1)S(1)}, bf16[400,256]{1,0:T(8,128)(2,1)S(1)}, u32[]{:S(2)}, u32[]{:S(2)}) collective-permute-start(bf16[400,256]{1,0:T(8,128)(2,1)S(1)} %get-tuple-element.19), channel_id=1, source_target_pairs={{0,4},{4,0},{8,12},{12,8},{1,5},{5,1},{9,13},{13,9},{2,6},{6,2},{1... | collective-permute-start | bytes 614408 | tf_op jit(solution)/shard_map/ppermute | solution.py:346
  2.7 0.7 %collective-permute-start.1 = (bf16[400,256]{1,0:T(8,128)(2,1)S(1)}, bf16[400,256]{1,0:T(8,128)(2,1)S(1)}, u32[]{:S(2)}, u32[]{:S(2)}) collective-permute-start(bf16[400,256]{1,0:T(8,128)(2,1)S(1)} %get-tuple-element.20), channel_id=1, source_target_pairs={{4,8},{8,4},{5,9},{9,5},{6,10},{10,6},{7,11},{11,7},{20,24},{24,20... | collective-permute-start | bytes 614408 | tf_op jit(solution)/shard_map/ppermute | solution.py:347
  3.3 0.4 %collective-permute-done.a_ref = bf16[400,256]{1,0:T(8,128)(2,1)S(1)} collective-permute-done((bf16[400,256]{1,0:T(8,128)(2,1)S(1)}, bf16[400,256]{1,0:T(8,128)(2,1)S(1)}, u32[]{:S(2)}, u32[]{:S(2)}) %collective-permute-start) | collective-permute-done | bytes 204832 | tf_op jit(solution)/shard_map/ppermute | solution.py:346
  3.7 0.2 shard_map.52
  3.9 1.3 %collective-permute-start.2 = (bf16[88,384]{1,0:T(8,128)(2,1)S(1)}, bf16[88,384]{1,0:T(8,128)(2,1)S(1)}, u32[]{:S(2)}, u32[]{:S(2)}) collective-permute-start(bf16[88,384]{1,0:T(8,128)(2,1)S(1)} %get-tuple-element.25), channel_id=1, source_target_pairs={{1,0},{2,1},{3,2},{5,4},{6,5},{7,6},{9,8},{10,9},{11,10},{13,12},{... | collective-permute-start | bytes 202760 | tf_op jit(solution)/shard_map/ppermute | solution.py:350
  5.2 0.7 %collective-permute-start.3 = (bf16[24,384]{1,0:T(8,128)(2,1)S(1)}, bf16[24,384]{1,0:T(8,128)(2,1)S(1)}, u32[]{:S(2)}, u32[]{:S(2)}) collective-permute-start(bf16[24,384]{1,0:T(8,128)(2,1)S(1)} %get-tuple-element.26), channel_id=1, source_target_pairs={{5,8},{6,9},{7,10},{9,4},{10,5},{11,6},{21,24},{22,25},{23,26},{25... | collective-permute-start | bytes 55304 | tf_op jit(solution)/shard_map/ppermute | solution.py:351
  5.9 0.0 collective-permute-done.1.b_ref
  5.9 0.0 copy-done.2
  5.9 3.1 %shard_map.51 = (bf16[16,16,256]{2,1,0:T(8,128)(2,1)S(1)}, bf16[17,112,384]{2,1,0:T(8,128)(2,1)S(1)}, bf16[128,256]{1,0:T(8,128)(2,1)S(1)}) custom-call(bf16[400,256]{1,0:T(8,128)(2,1)S(1)} %collective-permute-done.a_ref, bf16[400,256]{1,0:T(8,128)(2,1)S(1)} %collective-permute-done.1.b_ref, f32[2056,128]{1,0:T(8,128)S(1)} %get-tuple-element.21.rows_ref, ...), custom_call_target="tpu_custom_call" | custom-call | tf_op jit(solution)/shard_map/pallas_call | solution.py:354
  9.0 0.0 copy-start.1
  9.0 0.0 collective-permute-done.3.diag_ref
  9.0 2.0 %collective-permute-done.2.side_ref = bf16[88,384]{1,0:T(8,128)(2,1)S(1)} collective-permute-done((bf16[88,384]{1,0:T(8,128)(2,1)S(1)}, bf16[88,384]{1,0:T(8,128)(2,1)S(1)}, u32[]{:S(2)}, u32[]{:S(2)}) %collective-permute-start.2) | collective-permute-done | bytes 67616 | tf_op jit(solution)/shard_map/ppermute | solution.py:350
  11.0 0.6 %shard_map.53 = (bf16[16,256]{1,0:T(8,128)(2,1)S(1)}, f32[136,128]{1,0:T(8,128)S(1)}, f32[136,128]{1,0:T(8,128)S(1)}, f32[16,128]{1,0:T(8,128)S(1)}) custom-call(bf16[128,256]{1,0:T(8,128)(2,1)S(1)} %get-tuple-element.22.band_ref, bf16[17,112,384]{2,1,0:T(8,128)(2,1)S(1)} %get-tuple-element.23.x_ref, bf16[88,384]{1,0:T(8,128)(2,1)S(1)} %collective-permute-done.2.side_ref, ...), custom_call_target="tpu_custom_call" | custom-call | tf_op jit(solution)/shard_map/pallas_call | solution.py:358
  11.6 3.7 %collective-permute-start.4 = (f32[136,128]{1,0:T(8,128)S(1)}, f32[136,128]{1,0:T(8,128)S(1)}, u32[]{:S(2)}, u32[]{:S(2)}) collective-permute-start(f32[136,128]{1,0:T(8,128)S(1)} %get-tuple-element.29), channel_id=1, source_target_pairs={{0,4},{4,0},{8,12},{12,8},{1,5},{5,1},{9,13},{13,9},{2,6},{6,2},{1... | collective-permute-start | bytes 208904 | tf_op jit(solution)/shard_map/ppermute | solution.py:362
  15.3 0.9 %collective-permute-done.4 = f32[136,128]{1,0:T(8,128)S(1)} collective-permute-done((f32[136,128]{1,0:T(8,128)S(1)}, f32[136,128]{1,0:T(8,128)S(1)}, u32[]{:S(2)}, u32[]{:S(2)}) %collective-permute-start.4) | collective-permute-done | bytes 69664 | tf_op jit(solution)/shard_map/ppermute | solution.py:362
  16.2 1.2 %collective-permute-start.5 = (f32[136,128]{1,0:T(8,128)S(1)}, f32[136,128]{1,0:T(8,128)S(1)}, u32[]{:S(2)}, u32[]{:S(2)}) collective-permute-start(f32[136,128]{1,0:T(8,128)S(1)} %add.12), channel_id=1, source_target_pairs={{0,8},{4,12},{8,0},{12,4},{1,9},{5,13},{9,1},{13,5},{2,10},{6,14},... | collective-permute-start | bytes 208904 | tf_op jit(solution)/shard_map/ppermute | solution.py:365
  17.4 3.3 %collective-permute-done.5 = f32[136,128]{1,0:T(8,128)S(1)} collective-permute-done((f32[136,128]{1,0:T(8,128)S(1)}, f32[136,128]{1,0:T(8,128)S(1)}, u32[]{:S(2)}, u32[]{:S(2)}) %collective-permute-start.5) | collective-permute-done | bytes 69664 | tf_op jit(solution)/shard_map/ppermute | solution.py:365
  20.7 2.4 %collective-permute-start.6 = (f32[152,128]{1,0:T(8,128)S(1)}, f32[152,128]{1,0:T(8,128)S(1)}, u32[]{:S(2)}, u32[]{:S(2)}) collective-permute-start(f32[152,128]{1,0:T(8,128)S(1)} %pad_maximum_fusion), channel_id=1, source_target_pairs={{0,1},{1,0},{2,3},{3,2},{4,5},{5,4},{6,7},{7,6},{8,9},{9,8},{10,11... | collective-permute-start | bytes 233480 | tf_op jit(solution)/shard_map/ppermute | solution.py:377
  23.2 2.4 %collective-permute-done.6 = f32[152,128]{1,0:T(8,128)S(1)} collective-permute-done((f32[152,128]{1,0:T(8,128)S(1)}, f32[152,128]{1,0:T(8,128)S(1)}, u32[]{:S(2)}, u32[]{:S(2)}) %collective-permute-start.6) | collective-permute-done | bytes 77856 | tf_op jit(solution)/shard_map/ppermute | solution.py:377
  25.5 0.1 add_select_fusion
  25.6 3.1 %collective-permute-start.7 = (f32[152,128]{1,0:T(8,128)S(1)}, f32[152,128]{1,0:T(8,128)S(1)}, u32[]{:S(2)}, u32[]{:S(2)}) collective-permute-start(f32[152,128]{1,0:T(8,128)S(1)} %add_select_fusion), channel_id=1, source_target_pairs={{0,2},{1,3},{2,0},{3,1},{4,6},{5,7},{6,4},{7,5},{8,10},{9,11},{10,... | collective-permute-start | bytes 233480 | tf_op jit(solution)/shard_map/ppermute | solution.py:377
  28.7 0.0 copy-done.1
  28.7 0.3 shard_map.54.start_ref
  29.0 2.1 %collective-permute-done.7 = f32[152,128]{1,0:T(8,128)S(1)} collective-permute-done((f32[152,128]{1,0:T(8,128)S(1)}, f32[152,128]{1,0:T(8,128)S(1)}, u32[]{:S(2)}, u32[]{:S(2)}) %collective-permute-start.7) | collective-permute-done | bytes 77856 | tf_op jit(solution)/shard_map/ppermute | solution.py:377
  31.1 0.1 add_select_fusion.1.mine_ref
  31.2 0.1 collective-permute-start.8
  31.3 1.2 %collective-permute-done.8.other_ref = f32[136,128]{1,0:T(8,128)S(1)} collective-permute-done((f32[136,128]{1,0:T(8,128)S(1)}, f32[136,128]{1,0:T(8,128)S(1)}, u32[]{:S(2)}, u32[]{:S(2)}) %collective-permute-start.8) | collective-permute-done | bytes 69664 | tf_op jit(solution)/shard_map/ppermute | solution.py:382
  32.5 4.7 %shard_map.55 = (f32[64,256]{1,0:T(8,128)}, f32[2,32,256]{2,1,0:T(8,128)}) custom-call(f32[136,128]{1,0:T(8,128)S(1)} %add_select_fusion.1.mine_ref, f32[136,128]{1,0:T(8,128)S(1)} %collective-permute-done.8.other_ref, f32[64,256]{1,0:T(8,128)S(1)} %shard_map.54.start_ref, bf16[16,16,256]{2,1,0:T(8,128)(2,1)S(1)} %get-tuple-element.27.inner_ref, ...), custom_call_target="tpu_custom_call" | custom-call | tf_op jit(solution)/shard_map/pallas_call | solution.py:386
  (5 shorter events, 0.0 us)
Async XLA Ops:
  0.6 1.0 %copy-start = (bf16[257,8,128]{2,1,0:T(8,128)(2,1)S(1)}, bf16[257,8,128]{2,1,0:T(8,128)(2,1)}, u32[]{:S(2)}) copy-start(bf16[257,8,128]{2,1,0:T(8,128)(2,1)} %video_ref.1) | copy-start | bytes 1579012
  1.7 4.2 %copy-start.2 = (f32[4,2,7,7]{3,1,2,0:T(2,128)S(1)}, f32[4,2,7,7]{3,1,2,0:T(2,128)}, u32[]{:S(2)}) copy-start(f32[4,2,7,7]{3,1,2,0:T(2,128)} %param.4) | copy-start | bytes 4708
  2.1 1.6 %collective-permute-start = (bf16[400,256]{1,0:T(8,128)(2,1)S(1)}, bf16[400,256]{1,0:T(8,128)(2,1)S(1)}, u32[]{:S(2)}, u32[]{:S(2)}) collective-permute-start(bf16[400,256]{1,0:T(8,128)(2,1)S(1)} %get-tuple-element.19), channel_id=1, source_target_pairs={{0,4},{4,0},{8,12},{12,8},{1,5},{5,1},{9,13},{13,9},{2,6},{6,2},{1... | collective-permute-start | bytes 614408 | tf_op jit(solution)/shard_map/ppermute | solution.py:346
  2.7 3.2 %collective-permute-start.1 = (bf16[400,256]{1,0:T(8,128)(2,1)S(1)}, bf16[400,256]{1,0:T(8,128)(2,1)S(1)}, u32[]{:S(2)}, u32[]{:S(2)}) collective-permute-start(bf16[400,256]{1,0:T(8,128)(2,1)S(1)} %get-tuple-element.20), channel_id=1, source_target_pairs={{4,8},{8,4},{5,9},{9,5},{6,10},{10,6},{7,11},{11,7},{20,24},{24,20... | collective-permute-start | bytes 614408 | tf_op jit(solution)/shard_map/ppermute | solution.py:347
  3.9 7.1 %collective-permute-start.2 = (bf16[88,384]{1,0:T(8,128)(2,1)S(1)}, bf16[88,384]{1,0:T(8,128)(2,1)S(1)}, u32[]{:S(2)}, u32[]{:S(2)}) collective-permute-start(bf16[88,384]{1,0:T(8,128)(2,1)S(1)} %get-tuple-element.25), channel_id=1, source_target_pairs={{1,0},{2,1},{3,2},{5,4},{6,5},{7,6},{9,8},{10,9},{11,10},{13,12},{... | collective-permute-start | bytes 202760 | tf_op jit(solution)/shard_map/ppermute | solution.py:350
  5.2 3.8 %collective-permute-start.3 = (bf16[24,384]{1,0:T(8,128)(2,1)S(1)}, bf16[24,384]{1,0:T(8,128)(2,1)S(1)}, u32[]{:S(2)}, u32[]{:S(2)}) collective-permute-start(bf16[24,384]{1,0:T(8,128)(2,1)S(1)} %get-tuple-element.26), channel_id=1, source_target_pairs={{5,8},{6,9},{7,10},{9,4},{10,5},{11,6},{21,24},{22,25},{23,26},{25... | collective-permute-start | bytes 55304 | tf_op jit(solution)/shard_map/ppermute | solution.py:351
  9.0 19.7 %copy-start.1 = (f32[256,64]{0,1:T(8,128)S(1)}, f32[256,64]{0,1:T(8,128)}, u32[]{:S(2)}) copy-start(f32[256,64]{0,1:T(8,128)} %param.5) | copy-start | bytes 196612
  11.6 4.6 %collective-permute-start.4 = (f32[136,128]{1,0:T(8,128)S(1)}, f32[136,128]{1,0:T(8,128)S(1)}, u32[]{:S(2)}, u32[]{:S(2)}) collective-permute-start(f32[136,128]{1,0:T(8,128)S(1)} %get-tuple-element.29), channel_id=1, source_target_pairs={{0,4},{4,0},{8,12},{12,8},{1,5},{5,1},{9,13},{13,9},{2,6},{6,2},{1... | collective-permute-start | bytes 208904 | tf_op jit(solution)/shard_map/ppermute | solution.py:362
  16.2 4.5 %collective-permute-start.5 = (f32[136,128]{1,0:T(8,128)S(1)}, f32[136,128]{1,0:T(8,128)S(1)}, u32[]{:S(2)}, u32[]{:S(2)}) collective-permute-start(f32[136,128]{1,0:T(8,128)S(1)} %add.12), channel_id=1, source_target_pairs={{0,8},{4,12},{8,0},{12,4},{1,9},{5,13},{9,1},{13,5},{2,10},{6,14},... | collective-permute-start | bytes 208904 | tf_op jit(solution)/shard_map/ppermute | solution.py:365
  20.7 4.8 %collective-permute-start.6 = (f32[152,128]{1,0:T(8,128)S(1)}, f32[152,128]{1,0:T(8,128)S(1)}, u32[]{:S(2)}, u32[]{:S(2)}) collective-permute-start(f32[152,128]{1,0:T(8,128)S(1)} %pad_maximum_fusion), channel_id=1, source_target_pairs={{0,1},{1,0},{2,3},{3,2},{4,5},{5,4},{6,7},{7,6},{8,9},{9,8},{10,11... | collective-permute-start | bytes 233480 | tf_op jit(solution)/shard_map/ppermute | solution.py:377
  25.6 5.5 %collective-permute-start.7 = (f32[152,128]{1,0:T(8,128)S(1)}, f32[152,128]{1,0:T(8,128)S(1)}, u32[]{:S(2)}, u32[]{:S(2)}) collective-permute-start(f32[152,128]{1,0:T(8,128)S(1)} %add_select_fusion), channel_id=1, source_target_pairs={{0,2},{1,3},{2,0},{3,1},{4,6},{5,7},{6,4},{7,5},{8,10},{9,11},{10,... | collective-permute-start | bytes 233480 | tf_op jit(solution)/shard_map/ppermute | solution.py:377
  31.2 1.3 %collective-permute-start.8 = (f32[136,128]{1,0:T(8,128)S(1)}, f32[136,128]{1,0:T(8,128)S(1)}, u32[]{:S(2)}, u32[]{:S(2)}) collective-permute-start(f32[136,128]{1,0:T(8,128)S(1)} %add_select_fusion.1.mine_ref), channel_id=1, source_target_pairs={{0,4},{4,0},{8,12},{12,8},{1,5},{5,1},{9,13},{13,9},{2,6},{6,2},{1... | collective-permute-start | bytes 208904 | tf_op jit(solution)/shard_map/ppermute | solution.py:382

commit v11 on v10

--- a/solution.py
+++ b/solution.py
@@ -193,6 +193,10 @@
     feats_ref[0] = jnp.where(second_cells() & begins, feats_ref[0].astype(F32), 0.0).astype(BF16)
 
 
+def frame_sums(flat):
+    return lax.dot_general(flat, flat, (((0,), (0,)), ((), ())), preferred_element_type=F32)
+
+
 def edge_kernel(band_ref, x_ref, side_ref, diag_ref, inner_ref, edge_ref, mine_ref, other_ref, passed_ref):
     even = is_even("row")
     side = side_ref[...].astype(F32)
@@ -202,8 +206,7 @@
     ends = lax.axis_index("col") == lax.axis_size("col") - 1
     edge = jnp.where(second_cells() & ends, 0.0, edge).astype(BF16)
     edge_ref[...] = edge
-    flat = jnp.concatenate([inner_ref[...].reshape(16 * BLOCKS, FRAMES), edge], axis=0)
-    gram = lax.dot_general(flat, flat, (((0,), (0,)), ((), ())), preferred_element_type=F32)
+    gram = frame_sums(inner_ref[...].reshape(16 * BLOCKS, FRAMES)) + frame_sums(edge)
     top, cross, low = gram[:HALF, :HALF], gram[:HALF, HALF:], gram[HALF:, HALF:]
     i = lax.broadcasted_iota(jnp.int32, (HALF, HALF), 0)
     j = lax.broadcasted_iota(jnp.int32, (HALF, HALF), 1)

time: 37.5 us -> 37.5 us (level)
  no operation moved by 1% of the time
where the time goes in v11:
time: 37.5 us; the launch traced here: 37.3 us
  starting transfers between devices  13.6 us (36%)
  waiting for transfers between devices  12.3 us (33%)
  Pallas kernels  9.26 us (25%)
  local copies, waits for them, and re-layouts  1.05 us (3%)
  between operations  0.78 us (2%)
    ppermute x2, starting transfers between devices, on_device(): got = lax.ppermute(mine, 'col', [(i, i ^ step) for i in range(size_col)])  5.53 us
    pallas_call x1, Pallas kernels, on_device(): call(kernel, [((MODES, FRAMES), F32), ((ROWS // 4, COLS // 4, ORIENT * MO...  4.73 us
    ppermute x2, waiting for transfers between devices, on_device(): got = lax.ppermute(mine, 'col', [(i, i ^ step) for i in range(size_col)])  4.48 us
    ppermute x1, starting transfers between devices, on_device(): mine = mine + lax.ppermute(other, 'row', near)  3.7 us
    ppermute x1, waiting for transfers between devices, on_device(): lax.ppermute(mine, 'row', [(i, i ^ step) for i in range(size_row)])  3.28 us
    pallas_call x1, Pallas kernels, on_device(): call(inner_kernel, outs, 4, [pltpu.VMEM((16, 128), F32)])  3.08 us
    ppermute x1, waiting for transfers between devices, on_device(): side = lax.ppermute(side, 'col', to_left)  2.01 us
    ppermute x1, starting transfers between devices, on_device(): side = lax.ppermute(side, 'col', to_left)  1.29 us
  transfers between devices with their start and end apart: 9, of which 7 were waited for; matrix products, arithmetic and copies ran while one was open for 0% of the time, Pallas kernels for 9%

profile of v11, /device:TPU:0, one launch (start us, length us, event | category | flops | bytes accessed | tf_op | source)
XLA Modules:
  0.0 37.3 jit_solution(16770983166886615781)
XLA Ops:
  0.6 0.0 copy-start
  0.6 1.0 %copy-done = bf16[257,8,128]{2,1,0:T(8,128)(2,1)S(1)} copy-done((bf16[257,8,128]{2,1,0:T(8,128)(2,1)S(1)}, bf16[257,8,128]{2,1,0:T(8,128)(2,1)}, u32[]{:S(2)}) %copy-start) | copy-done | bytes 526360
  1.7 0.0 copy-start.2
  1.7 0.5 %shard_map.50 = (f32[2056,128]{1,0:T(8,128)S(1)}, bf16[400,256]{1,0:T(8,128)(2,1)S(1)}, bf16[400,256]{1,0:T(8,128)(2,1)S(1)}, f32[64,256]{1,0:T(8,128)S(1)}) custom-call(bf16[257,8,128]{2,1,0:T(8,128)(2,1)S(1)} %copy-done), custom_call_target="tpu_custom_call" | custom-call | tf_op jit(solution)/shard_map/pallas_call | solution.py:348
  2.1 0.5 %collective-permute-start = (bf16[400,256]{1,0:T(8,128)(2,1)S(1)}, bf16[400,256]{1,0:T(8,128)(2,1)S(1)}, u32[]{:S(2)}, u32[]{:S(2)}) collective-permute-start(bf16[400,256]{1,0:T(8,128)(2,1)S(1)} %get-tuple-element.19), channel_id=1, source_target_pairs={{0,4},{4,0},{8,12},{12,8},{1,5},{5,1},{9,13},{13,9},{2,6},{6,2},{1... | collective-permute-start | bytes 614408 | tf_op jit(solution)/shard_map/ppermute | solution.py:349
  2.7 0.7 %collective-permute-start.1 = (bf16[400,256]{1,0:T(8,128)(2,1)S(1)}, bf16[400,256]{1,0:T(8,128)(2,1)S(1)}, u32[]{:S(2)}, u32[]{:S(2)}) collective-permute-start(bf16[400,256]{1,0:T(8,128)(2,1)S(1)} %get-tuple-element.20), channel_id=1, source_target_pairs={{4,8},{8,4},{5,9},{9,5},{6,10},{10,6},{7,11},{11,7},{20,24},{24,20... | collective-permute-start | bytes 614408 | tf_op jit(solution)/shard_map/ppermute | solution.py:350
  3.3 0.4 %collective-permute-done.a_ref = bf16[400,256]{1,0:T(8,128)(2,1)S(1)} collective-permute-done((bf16[400,256]{1,0:T(8,128)(2,1)S(1)}, bf16[400,256]{1,0:T(8,128)(2,1)S(1)}, u32[]{:S(2)}, u32[]{:S(2)}) %collective-permute-start) | collective-permute-done | bytes 204832 | tf_op jit(solution)/shard_map/ppermute | solution.py:349
  3.7 0.2 shard_map.52
  3.9 1.3 %collective-permute-start.2 = (bf16[88,384]{1,0:T(8,128)(2,1)S(1)}, bf16[88,384]{1,0:T(8,128)(2,1)S(1)}, u32[]{:S(2)}, u32[]{:S(2)}) collective-permute-start(bf16[88,384]{1,0:T(8,128)(2,1)S(1)} %get-tuple-element.25), channel_id=1, source_target_pairs={{1,0},{2,1},{3,2},{5,4},{6,5},{7,6},{9,8},{10,9},{11,10},{13,12},{... | collective-permute-start | bytes 202760 | tf_op jit(solution)/shard_map/ppermute | solution.py:353
  5.2 0.7 %collective-permute-start.3 = (bf16[24,384]{1,0:T(8,128)(2,1)S(1)}, bf16[24,384]{1,0:T(8,128)(2,1)S(1)}, u32[]{:S(2)}, u32[]{:S(2)}) collective-permute-start(bf16[24,384]{1,0:T(8,128)(2,1)S(1)} %get-tuple-element.26), channel_id=1, source_target_pairs={{5,8},{6,9},{7,10},{9,4},{10,5},{11,6},{21,24},{22,25},{23,26},{25... | collective-permute-start | bytes 55304 | tf_op jit(solution)/shard_map/ppermute | solution.py:354
  5.9 0.0 collective-permute-done.1.b_ref
  5.9 0.0 copy-done.2
  5.9 3.1 %shard_map.51 = (bf16[16,16,256]{2,1,0:T(8,128)(2,1)S(1)}, bf16[17,112,384]{2,1,0:T(8,128)(2,1)S(1)}, bf16[128,256]{1,0:T(8,128)(2,1)S(1)}) custom-call(bf16[400,256]{1,0:T(8,128)(2,1)S(1)} %collective-permute-done.a_ref, bf16[400,256]{1,0:T(8,128)(2,1)S(1)} %collective-permute-done.1.b_ref, f32[2056,128]{1,0:T(8,128)S(1)} %get-tuple-element.21.rows_ref, ...), custom_call_target="tpu_custom_call" | custom-call | tf_op jit(solution)/shard_map/pallas_call | solution.py:357
  9.0 0.0 copy-start.1
  9.0 0.0 collective-permute-done.3.diag_ref
  9.0 2.0 %collective-permute-done.2.side_ref = bf16[88,384]{1,0:T(8,128)(2,1)S(1)} collective-permute-done((bf16[88,384]{1,0:T(8,128)(2,1)S(1)}, bf16[88,384]{1,0:T(8,128)(2,1)S(1)}, u32[]{:S(2)}, u32[]{:S(2)}) %collective-permute-start.2) | collective-permute-done | bytes 67616 | tf_op jit(solution)/shard_map/ppermute | solution.py:353
  11.0 0.6 %shard_map.53 = (bf16[16,256]{1,0:T(8,128)(2,1)S(1)}, f32[136,128]{1,0:T(8,128)S(1)}, f32[136,128]{1,0:T(8,128)S(1)}, f32[16,128]{1,0:T(8,128)S(1)}) custom-call(bf16[128,256]{1,0:T(8,128)(2,1)S(1)} %get-tuple-element.22.band_ref, bf16[17,112,384]{2,1,0:T(8,128)(2,1)S(1)} %get-tuple-element.23.x_ref, bf16[88,384]{1,0:T(8,128)(2,1)S(1)} %collective-permute-done.2.side_ref, ...), custom_call_target="tpu_custom_call" | custom-call | tf_op jit(solution)/shard_map/pallas_call | solution.py:361
  11.6 3.7 %collective-permute-start.4 = (f32[136,128]{1,0:T(8,128)S(1)}, f32[136,128]{1,0:T(8,128)S(1)}, u32[]{:S(2)}, u32[]{:S(2)}) collective-permute-start(f32[136,128]{1,0:T(8,128)S(1)} %get-tuple-element.29), channel_id=1, source_target_pairs={{0,4},{4,0},{8,12},{12,8},{1,5},{5,1},{9,13},{13,9},{2,6},{6,2},{1... | collective-permute-start | bytes 208904 | tf_op jit(solution)/shard_map/ppermute | solution.py:365
  15.3 0.9 %collective-permute-done.4 = f32[136,128]{1,0:T(8,128)S(1)} collective-permute-done((f32[136,128]{1,0:T(8,128)S(1)}, f32[136,128]{1,0:T(8,128)S(1)}, u32[]{:S(2)}, u32[]{:S(2)}) %collective-permute-start.4) | collective-permute-done | bytes 69664 | tf_op jit(solution)/shard_map/ppermute | solution.py:365
  16.2 1.2 %collective-permute-start.5 = (f32[136,128]{1,0:T(8,128)S(1)}, f32[136,128]{1,0:T(8,128)S(1)}, u32[]{:S(2)}, u32[]{:S(2)}) collective-permute-start(f32[136,128]{1,0:T(8,128)S(1)} %add.12), channel_id=1, source_target_pairs={{0,8},{4,12},{8,0},{12,4},{1,9},{5,13},{9,1},{13,5},{2,10},{6,14},... | collective-permute-start | bytes 208904 | tf_op jit(solution)/shard_map/ppermute | solution.py:368
  17.4 3.3 %collective-permute-done.5 = f32[136,128]{1,0:T(8,128)S(1)} collective-permute-done((f32[136,128]{1,0:T(8,128)S(1)}, f32[136,128]{1,0:T(8,128)S(1)}, u32[]{:S(2)}, u32[]{:S(2)}) %collective-permute-start.5) | collective-permute-done | bytes 69664 | tf_op jit(solution)/shard_map/ppermute | solution.py:368
  20.7 2.4 %collective-permute-start.6 = (f32[152,128]{1,0:T(8,128)S(1)}, f32[152,128]{1,0:T(8,128)S(1)}, u32[]{:S(2)}, u32[]{:S(2)}) collective-permute-start(f32[152,128]{1,0:T(8,128)S(1)} %pad_maximum_fusion), channel_id=1, source_target_pairs={{0,1},{1,0},{2,3},{3,2},{4,5},{5,4},{6,7},{7,6},{8,9},{9,8},{10,11... | collective-permute-start | bytes 233480 | tf_op jit(solution)/shard_map/ppermute | solution.py:380
  23.2 2.4 %collective-permute-done.6 = f32[152,128]{1,0:T(8,128)S(1)} collective-permute-done((f32[152,128]{1,0:T(8,128)S(1)}, f32[152,128]{1,0:T(8,128)S(1)}, u32[]{:S(2)}, u32[]{:S(2)}) %collective-permute-start.6) | collective-permute-done | bytes 77856 | tf_op jit(solution)/shard_map/ppermute | solution.py:380
  25.6 0.1 add_select_fusion
  25.6 3.1 %collective-permute-start.7 = (f32[152,128]{1,0:T(8,128)S(1)}, f32[152,128]{1,0:T(8,128)S(1)}, u32[]{:S(2)}, u32[]{:S(2)}) collective-permute-start(f32[152,128]{1,0:T(8,128)S(1)} %add_select_fusion), channel_id=1, source_target_pairs={{0,2},{1,3},{2,0},{3,1},{4,6},{5,7},{6,4},{7,5},{8,10},{9,11},{10,... | collective-permute-start | bytes 233480 | tf_op jit(solution)/shard_map/ppermute | solution.py:380
  28.7 0.0 copy-done.1
  28.8 0.3 shard_map.54.start_ref
  29.0 2.1 %collective-permute-done.7 = f32[152,128]{1,0:T(8,128)S(1)} collective-permute-done((f32[152,128]{1,0:T(8,128)S(1)}, f32[152,128]{1,0:T(8,128)S(1)}, u32[]{:S(2)}, u32[]{:S(2)}) %collective-permute-start.7) | collective-permute-done | bytes 77856 | tf_op jit(solution)/shard_map/ppermute | solution.py:380
  31.1 0.1 add_select_fusion.1.mine_ref
  31.2 0.1 collective-permute-start.8
  31.3 1.2 %collective-permute-done.8.other_ref = f32[136,128]{1,0:T(8,128)S(1)} collective-permute-done((f32[136,128]{1,0:T(8,128)S(1)}, f32[136,128]{1,0:T(8,128)S(1)}, u32[]{:S(2)}, u32[]{:S(2)}) %collective-permute-start.8) | collective-permute-done | bytes 69664 | tf_op jit(solution)/shard_map/ppermute | solution.py:385
  32.5 4.7 %shard_map.55 = (f32[64,256]{1,0:T(8,128)}, f32[2,32,256]{2,1,0:T(8,128)}) custom-call(f32[136,128]{1,0:T(8,128)S(1)} %add_select_fusion.1.mine_ref, f32[136,128]{1,0:T(8,128)S(1)} %collective-permute-done.8.other_ref, f32[64,256]{1,0:T(8,128)S(1)} %shard_map.54.start_ref, bf16[16,16,256]{2,1,0:T(8,128)(2,1)S(1)} %get-tuple-element.27.inner_ref, ...), custom_call_target="tpu_custom_call" | custom-call | tf_op jit(solution)/shard_map/pallas_call | solution.py:389
  (5 shorter events, 0.0 us)
Async XLA Ops:
  0.6 1.0 %copy-start = (bf16[257,8,128]{2,1,0:T(8,128)(2,1)S(1)}, bf16[257,8,128]{2,1,0:T(8,128)(2,1)}, u32[]{:S(2)}) copy-start(bf16[257,8,128]{2,1,0:T(8,128)(2,1)} %video_ref.1) | copy-start | bytes 1579012
  1.7 4.2 %copy-start.2 = (f32[4,2,7,7]{3,1,2,0:T(2,128)S(1)}, f32[4,2,7,7]{3,1,2,0:T(2,128)}, u32[]{:S(2)}) copy-start(f32[4,2,7,7]{3,1,2,0:T(2,128)} %param.4) | copy-start | bytes 4708
  2.1 1.6 %collective-permute-start = (bf16[400,256]{1,0:T(8,128)(2,1)S(1)}, bf16[400,256]{1,0:T(8,128)(2,1)S(1)}, u32[]{:S(2)}, u32[]{:S(2)}) collective-permute-start(bf16[400,256]{1,0:T(8,128)(2,1)S(1)} %get-tuple-element.19), channel_id=1, source_target_pairs={{0,4},{4,0},{8,12},{12,8},{1,5},{5,1},{9,13},{13,9},{2,6},{6,2},{1... | collective-permute-start | bytes 614408 | tf_op jit(solution)/shard_map/ppermute | solution.py:349
  2.7 3.2 %collective-permute-start.1 = (bf16[400,256]{1,0:T(8,128)(2,1)S(1)}, bf16[400,256]{1,0:T(8,128)(2,1)S(1)}, u32[]{:S(2)}, u32[]{:S(2)}) collective-permute-start(bf16[400,256]{1,0:T(8,128)(2,1)S(1)} %get-tuple-element.20), channel_id=1, source_target_pairs={{4,8},{8,4},{5,9},{9,5},{6,10},{10,6},{7,11},{11,7},{20,24},{24,20... | collective-permute-start | bytes 614408 | tf_op jit(solution)/shard_map/ppermute | solution.py:350
  3.9 7.1 %collective-permute-start.2 = (bf16[88,384]{1,0:T(8,128)(2,1)S(1)}, bf16[88,384]{1,0:T(8,128)(2,1)S(1)}, u32[]{:S(2)}, u32[]{:S(2)}) collective-permute-start(bf16[88,384]{1,0:T(8,128)(2,1)S(1)} %get-tuple-element.25), channel_id=1, source_target_pairs={{1,0},{2,1},{3,2},{5,4},{6,5},{7,6},{9,8},{10,9},{11,10},{13,12},{... | collective-permute-start | bytes 202760 | tf_op jit(solution)/shard_map/ppermute | solution.py:353
  5.2 3.8 %collective-permute-start.3 = (bf16[24,384]{1,0:T(8,128)(2,1)S(1)}, bf16[24,384]{1,0:T(8,128)(2,1)S(1)}, u32[]{:S(2)}, u32[]{:S(2)}) collective-permute-start(bf16[24,384]{1,0:T(8,128)(2,1)S(1)} %get-tuple-element.26), channel_id=1, source_target_pairs={{5,8},{6,9},{7,10},{9,4},{10,5},{11,6},{21,24},{22,25},{23,26},{25... | collective-permute-start | bytes 55304 | tf_op jit(solution)/shard_map/ppermute | solution.py:354
  9.0 19.8 %copy-start.1 = (f32[256,64]{0,1:T(8,128)S(1)}, f32[256,64]{0,1:T(8,128)}, u32[]{:S(2)}) copy-start(f32[256,64]{0,1:T(8,128)} %param.5) | copy-start | bytes 196612
  11.6 4.6 %collective-permute-start.4 = (f32[136,128]{1,0:T(8,128)S(1)}, f32[136,128]{1,0:T(8,128)S(1)}, u32[]{:S(2)}, u32[]{:S(2)}) collective-permute-start(f32[136,128]{1,0:T(8,128)S(1)} %get-tuple-element.29), channel_id=1, source_target_pairs={{0,4},{4,0},{8,12},{12,8},{1,5},{5,1},{9,13},{13,9},{2,6},{6,2},{1... | collective-permute-start | bytes 208904 | tf_op jit(solution)/shard_map/ppermute | solution.py:365
  16.2 4.5 %collective-permute-start.5 = (f32[136,128]{1,0:T(8,128)S(1)}, f32[136,128]{1,0:T(8,128)S(1)}, u32[]{:S(2)}, u32[]{:S(2)}) collective-permute-start(f32[136,128]{1,0:T(8,128)S(1)} %add.12), channel_id=1, source_target_pairs={{0,8},{4,12},{8,0},{12,4},{1,9},{5,13},{9,1},{13,5},{2,10},{6,14},... | collective-permute-start | bytes 208904 | tf_op jit(solution)/shard_map/ppermute | solution.py:368
  20.7 4.8 %collective-permute-start.6 = (f32[152,128]{1,0:T(8,128)S(1)}, f32[152,128]{1,0:T(8,128)S(1)}, u32[]{:S(2)}, u32[]{:S(2)}) collective-permute-start(f32[152,128]{1,0:T(8,128)S(1)} %pad_maximum_fusion), channel_id=1, source_target_pairs={{0,1},{1,0},{2,3},{3,2},{4,5},{5,4},{6,7},{7,6},{8,9},{9,8},{10,11... | collective-permute-start | bytes 233480 | tf_op jit(solution)/shard_map/ppermute | solution.py:380
  25.6 5.5 %collective-permute-start.7 = (f32[152,128]{1,0:T(8,128)S(1)}, f32[152,128]{1,0:T(8,128)S(1)}, u32[]{:S(2)}, u32[]{:S(2)}) collective-permute-start(f32[152,128]{1,0:T(8,128)S(1)} %add_select_fusion), channel_id=1, source_target_pairs={{0,2},{1,3},{2,0},{3,1},{4,6},{5,7},{6,4},{7,5},{8,10},{9,11},{10,... | collective-permute-start | bytes 233480 | tf_op jit(solution)/shard_map/ppermute | solution.py:380
  31.2 1.3 %collective-permute-start.8 = (f32[136,128]{1,0:T(8,128)S(1)}, f32[136,128]{1,0:T(8,128)S(1)}, u32[]{:S(2)}, u32[]{:S(2)}) collective-permute-start(f32[136,128]{1,0:T(8,128)S(1)} %add_select_fusion.1.mine_ref), channel_id=1, source_target_pairs={{0,4},{4,0},{8,12},{12,8},{1,5},{5,1},{9,13},{13,9},{2,6},{6,2},{1... | collective-permute-start | bytes 208904 | tf_op jit(solution)/shard_map/ppermute | solution.py:385
